TPU v7x, 32 devices: a whole 2x2x4 slice. The times are simulated.
32 devices in a mesh: group: 2 (over x), expert: 8 (over z, y), tensor: 2 (over core).
Axes of the slice: x: 2, y: 2, z: 4, core: 2. Of those that a mesh axis runs over, the one named last changes fastest.
Arguments:
- tokens: bfloat16 [2048, 3584], P(('group', 'expert', 'tensor')), parts along dimension 0, may hold values from -6 to 6
- route_ids: int32 [2048, 8], P(('group', 'expert', 'tensor')), parts along dimension 0, may hold values from 0 to 31, all different within a row; in each aligned block of 64 rows (0 to 63, 64 to 127, ...) at most 18 rows name the same one
- route_gates: float32 [2048, 8], P(('group', 'expert', 'tensor')), parts along dimension 0, may hold values from 0.1 to 0.6
- expert_gate: bfloat16 [32, 3584, 1024], P('expert', None, 'tensor'), may hold values from -0.09375 to 0.09375
- expert_up: bfloat16 [32, 3584, 1024], P('expert', None, 'tensor'), may hold values from -0.09375 to 0.09375
- expert_down: bfloat16 [32, 1024, 3584], P('expert', 'tensor'), may hold values from -0.1875 to 0.1875
- shared_gate: bfloat16 [3584, 1024], P('expert', 'tensor'), may hold values from -0.09375 to 0.09375
- shared_up: bfloat16 [3584, 1024], P('expert', 'tensor'), may hold values from -0.09375 to 0.09375
- shared_down: bfloat16 [1024, 3584], P('tensor', 'expert'), may hold values from -0.1875 to 0.1875
Outputs:
- mixed: bfloat16 [2048, 3584], P(('group', 'expert', 'tensor')), parts along dimension 0
There are 2 independent parts, one for each index of `group`. A program takes and returns all parts, laid end to end along the dimension named above; an argument that names none is the same for every part. Nothing has to cross between parts.
Inputs may be any that keep to these rules, and one draw needn't show every extreme that they name: `route_ids`: each row names 8 different experts; among the 64 rows of one device no expert is named by more than 18 rows, and in every draw some expert is named by exactly 18 rows of some device.
All inputs are finite; a program needn't handle non-finite values.
Results may differ from a plain program's by a relative error of at most 0.006.
Values may be sent and summed in bfloat16 or wider, within the bound.
No kernel may reach another device: no remote copies, remote signals or barrier semaphores. Data moves between devices by JAX's collectives and lax.ppermute only.
A program may use at most 192 MiB of HBM per device.

v0:
```python
import jax
import jax.numpy as jnp
from jax import lax
from jax.sharding import PartitionSpec as P

MOST = 18


def swiglu_rows(inputs, gate_piece, up_piece):
    gated = jnp.dot(inputs, gate_piece, preferred_element_type=jnp.float32)
    upward = jnp.dot(inputs, up_piece, preferred_element_type=jnp.float32)
    return jax.nn.silu(gated) * upward


def expert_partial(block_rows, block_ids, expert_gate, expert_up, expert_down):
    groups, halves, items, features = block_rows.shape
    flat_rows = block_rows.reshape(groups * halves * items, features)
    flat_slots = block_ids.reshape(groups * halves * items, 1)
    partial_value = jnp.zeros((flat_rows.shape[0], features), jnp.float32)
    for which in range(expert_gate.shape[0]):
        active = (flat_slots == which).astype(jnp.float32)
        hidden = (swiglu_rows(flat_rows, expert_gate[which], expert_up[which]) * active).astype(
            jnp.bfloat16
        )
        partial_value = partial_value + jnp.dot(
            hidden, expert_down[which], preferred_element_type=jnp.float32
        )
    rounded = lax.optimization_barrier(partial_value.astype(jnp.bfloat16)).astype(jnp.float32)
    return rounded.reshape(groups, halves, items, features)


def on_device(
    tokens,
    route_ids,
    route_gates,
    expert_gate,
    expert_up,
    expert_down,
    shared_gate,
    shared_up,
    shared_down,
):
    index_count = lax.axis_size("expert")
    half_count = lax.axis_size("tensor")
    row_count, feature_count = tokens.shape
    route_count = route_ids.shape[1]
    local_count = expert_gate.shape[0]
    capacity = local_count * MOST
    whole_rows = lax.all_gather(tokens, "tensor", axis=0, tiled=True)
    first = jnp.dot(
        whole_rows,
        lax.all_gather(shared_gate, "expert", axis=0, tiled=True),
        preferred_element_type=jnp.float32,
    )
    second = jnp.dot(
        whole_rows,
        lax.all_gather(shared_up, "expert", axis=0, tiled=True),
        preferred_element_type=jnp.float32,
    )
    shared_hidden = (jax.nn.silu(first) * second).astype(jnp.bfloat16)
    shared_terms = jnp.dot(
        shared_hidden,
        lax.all_gather(shared_down, "expert", axis=1, tiled=True),
        preferred_element_type=jnp.float32,
    )
    shared_out = lax.psum_scatter(shared_terms, "tensor", scatter_dimension=0, tiled=True)
    flat_ids = route_ids.reshape(-1)
    target = flat_ids // local_count
    local_id = flat_ids - target * local_count
    onehot = (target[:, None] == jnp.arange(index_count, dtype=jnp.int32)[None, :]).astype(
        jnp.int32
    )
    earlier = jnp.cumsum(onehot, axis=0) - onehot
    within = jnp.sum(earlier * onehot, axis=1)
    slot_pos = target * capacity + within
    source_row = jnp.arange(flat_ids.shape[0], dtype=jnp.int32) // route_count
    picked_rows = tokens[source_row]
    slot_values = local_id.astype(jnp.float32)
    send_rows = (
        jnp.zeros((index_count * capacity, feature_count), jnp.bfloat16)
        .at[slot_pos]
        .set(picked_rows)
    )
    send_slots = (
        jnp.full((index_count * capacity,), -1.0, jnp.float32).at[slot_pos].set(slot_values)
    )
    send_rows = send_rows.reshape(index_count, capacity, feature_count)
    send_slots = send_slots.astype(jnp.bfloat16).reshape(index_count, capacity)
    wide_rows = jnp.broadcast_to(
        send_rows[:, None], (index_count, half_count, capacity, feature_count)
    ).reshape(index_count * half_count, capacity, feature_count)
    wide_slots = jnp.broadcast_to(send_slots[:, None], (index_count, half_count, capacity)).reshape(
        index_count * half_count, capacity
    )
    arrived_rows = lax.all_to_all(
        wide_rows, ("expert", "tensor"), split_axis=0, concat_axis=0, tiled=True
    )
    arrived_slots = lax.all_to_all(
        wide_slots, ("expert", "tensor"), split_axis=0, concat_axis=0, tiled=True
    )
    items = arrived_rows.shape[1]
    block_rows = arrived_rows.reshape(index_count, half_count, items, feature_count)
    block_slots = arrived_slots.reshape(index_count, half_count, items)
    partial_value = expert_partial(block_rows, block_slots, expert_gate, expert_up, expert_down)
    summed = lax.psum_scatter(
        partial_value.astype(jnp.bfloat16), "tensor", scatter_dimension=1, tiled=True
    ).astype(jnp.float32)
    outcome = summed.reshape(index_count, items, feature_count).astype(jnp.bfloat16)
    returned = lax.all_to_all(outcome, "expert", split_axis=0, concat_axis=0, tiled=True)
    results = returned.reshape(index_count * capacity, feature_count)[slot_pos]
    weighted = results.astype(jnp.float32) * route_gates.reshape(-1, 1)
    routed = jnp.sum(weighted.reshape(row_count, route_count, feature_count), axis=1)
    return (routed + shared_out).astype(jnp.bfloat16)


def solution(mesh):
    in_specs = (
        P(("group", "expert", "tensor"), None),
        P(("group", "expert", "tensor"), None),
        P(("group", "expert", "tensor"), None),
        P("expert", None, "tensor"),
        P("expert", None, "tensor"),
        P("expert", "tensor", None),
        P("expert", "tensor"),
        P("expert", "tensor"),
        P("tensor", "expert"),
    )
    out_specs = P(("group", "expert", "tensor"), None)
    return jax.shard_map(
        on_device, mesh=mesh, in_specs=in_specs, out_specs=out_specs, check_vma=False
    )
```

profile of v0, /device:TPU:0, one launch (start us, length us, event | category | flops | bytes accessed | tf_op | source)
XLA Modules:
  0.0 641.3 jit_solution(13363493835121896789)
XLA Ops:
  7.4 0.8 copy.19
  8.1 0.1 reshape.253
  8.2 0.1 reshape.252
  8.3 0.1 reshape.251
  8.4 1.1 reduce-window.6
  9.6 0.2 slice_reduce_fusion
  9.9 0.1 fusion.119
  10.0 2.4 scatter_custom_fusion.1
  12.4 0.1 broadcast_in_dim.30
  12.5 0.6 copy.22
  13.2 7.4 %all-to-all-start.1 = ((bf16[16,1,72]{2,1,0:T(2,128)(2,1)}), bf16[16,1,72]{2,1,0:T(2,128)(2,1)S(1)}, u32[]{:S(2)}, u32[]{:S(2)}) async-start(bf16[16,1,72]{2,1,0:T(2,128)(2,1)} %copy.22), calls=%async_computation.1 | async-start | bytes 16384 | tf_op jit(solution)/shard_map/all_to_all | solution.py:98
  20.6 18.6 %scatter_custom_fusion = bf16[576,3584]{1,0:T(8,128)(2,1)} fusion(s32[512]{0:T(512)S(1)} %bitcast.111, bf16[64,3584]{1,0:T(8,128)(2,1)} %param.9, s32[1024]{0:T(1024)S(1)} %pad_clamp_fusion.1, bf16[]{:T(256)} %constant.46.clone.1), kind=kCustom, calls=%fused_computation.32 | custom fusion | bytes 4129280 | tf_op jit(solution)/shard_map/scatter | solution.py:82
  39.2 6.0 broadcast_in_dim.28
  45.2 6.0 all-to-all-start
  51.2 0.0 all-reduce.3.cloned.1.call-start
  51.3 0.1 fusion.124
  51.4 0.1 reshape.257
  51.5 0.1 reshape.258
  51.6 0.1 reshape.259
  51.6 0.1 reshape.260
  51.7 147.9 %all-to-all-done = bf16[16,72,3584]{2,1,0:T(8,128)(2,1)} async-done(((bf16[16,72,3584]{2,1,0:T(8,128)(2,1)}), bf16[16,72,3584]{2,1,0:T(8,128)(2,1)}, u32[]{:S(2)}, u32[]{:S(2)}) %all-to-all-start) | async-done | bytes 8257568 | tf_op jit(solution)/shard_map/all_to_all | solution.py:95
  199.7 10.4 %fusion.21 = f32[1152,512]{1,0:T(8,128)} fusion(bf16[1152,3584]{1,0:T(8,128)(2,1)} %bitcast.7, bf16[4,3584,512]{2,1,0:T(8,128)(2,1)} %param.12), kind=kOutput, calls=%fused_computation.30 | convolution fusion | flops 4227858432 | bytes 14286848 | tf_op jit(solution)/shard_map/dot_general | solution.py:10
  210.1 10.5 %fusion.15 = f32[1152,512]{1,0:T(8,128)} fusion(bf16[1152,3584]{1,0:T(8,128)(2,1)} %bitcast.7, bf16[4,3584,512]{2,1,0:T(8,128)(2,1)} %param.12), kind=kOutput, calls=%fused_computation.24 | convolution fusion | flops 4227858432 | bytes 14286848 | tf_op jit(solution)/shard_map/dot_general | solution.py:10
  220.5 7.0 %fusion.10 = f32[1152,512]{1,0:T(8,128)S(1)} fusion(bf16[1152,3584]{1,0:T(8,128)(2,1)} %bitcast.7, bf16[4,3584,512]{2,1,0:T(8,128)(2,1)S(1)} %bitcast.116), kind=kOutput, calls=%fused_computation.19 | convolution fusion | flops 4227858432 | bytes 14286848 | tf_op jit(solution)/shard_map/dot_general | solution.py:10
  227.5 8.2 %fusion.5 = f32[1152,512]{1,0:T(8,128)} fusion(bf16[1152,3584]{1,0:T(8,128)(2,1)} %bitcast.7, bf16[4,3584,512]{2,1,0:T(8,128)(2,1)S(1)} %bitcast.116), kind=kOutput, calls=%fused_computation.14 | convolution fusion | flops 4227858432 | bytes 14286848 | tf_op jit(solution)/shard_map/dot_general | solution.py:10
  235.7 17.0 %fusion.17 = f32[1152,3584]{1,0:T(8,128)} fusion(bf16[4,512,3584]{2,1,0:T(8,128)(2,1)} %param.14, bf16[1152,3584]{1,0:T(8,128)(2,1)} %bitcast.7, bf16[4,3584,512]{2,1,0:T(8,128)(2,1)} %param.13, f32[1152,512]{1,0:T(8,128)} %fusion.21, f32[1152]{0:T(1024)S(1)} %reshape.257), kind=kOutput, calls=%fused_computation.26 | convolution fusion | flops 8459845632 | bytes 34476544 | tf_op jit(solution)/shard_map/dot_general | solution.py:25
  252.7 19.7 %convolution_add_fusion.2 = f32[1152,3584]{1,0:T(8,128)} fusion(f32[1152,3584]{1,0:T(8,128)} %fusion.17, bf16[4,512,3584]{2,1,0:T(8,128)(2,1)} %param.14, bf16[1152,3584]{1,0:T(8,128)(2,1)} %bitcast.7, bf16[4,3584,512]{2,1,0:T(8,128)(2,1)} %param.13, f32[1152,512]{1,0:T(8,128)} %fusion.15, f32[1152]{0:T(1024)S(1)} %reshape.258), kind=kOutput, calls=%fused_computation.6 | convolution fusion | flops 8463974400 | bytes 50991616 | tf_op jit(solution)/shard_map/dot_general | solution.py:25
  272.4 19.1 %convolution_add_fusion.1 = f32[1152,3584]{1,0:T(8,128)} fusion(f32[1152,3584]{1,0:T(8,128)} %convolution_add_fusion.2, bf16[4,512,3584]{2,1,0:T(8,128)(2,1)} %param.14, bf16[1152,3584]{1,0:T(8,128)(2,1)} %bitcast.7, bf16[4,3584,512]{2,1,0:T(8,128)(2,1)} %param.13, f32[1152,512]{1,0:T(8,128)S(1)} %fusion.10, f32[1152]{0:T(1024)S(1)} %reshape.259), kind=kOutput, calls=%fused_computation.5 | convolution fusion | flops 8463974400 | bytes 50991616 | tf_op jit(solution)/shard_map/dot_general | solution.py:25
  291.5 18.7 %fusion = bf16[1152,3584]{1,0:T(8,128)(2,1)} fusion(f32[1152,3584]{1,0:T(8,128)} %convolution_add_fusion.1, bf16[4,512,3584]{2,1,0:T(8,128)(2,1)} %param.14, bf16[1152,3584]{1,0:T(8,128)(2,1)} %bitcast.7, bf16[4,3584,512]{2,1,0:T(8,128)(2,1)} %param.13, f32[1152,512]{1,0:T(8,128)} %fusion.5, f32[1152]{0:T(1024)S(1)} %reshape.260), kind=kOutput, calls=%fused_computation.7 | convolution fusion | flops 8468103168 | bytes 42734080 | tf_op jit(solution)/shard_map/dot_general | solution.py:25
  310.2 0.0 all-gather.4.cloned.1.call-start
  310.2 0.5 all-gather.4.cloned.1.call-update
  310.8 0.0 all-gather.6.cloned.1.call-start
  310.8 0.5 all-gather.6.cloned.1.call-update
  311.4 0.5 all-gather.8.cloned.1.call-update
  312.0 0.6 dynamic-slice
  312.5 67.8 %all-reduce.3.cloned.1.call-done = bf16[8,2,72,3584]{3,2,1,0:T(8,128)(2,1)} async-done(((bf16[8,2,72,3584]{3,2,1,0:T(8,128)(2,1)}), bf16[8,2,72,3584]{3,2,1,0:T(8,128)(2,1)}) %all-reduce.3.cloned.1.call-update) | async-done | bytes 8257552
  380.3 5.1 dynamic-slice_bitcast_fusion
  385.4 5.9 all-to-all-start.2
  391.3 2.5 all_gather.12
  393.8 46.7 %all-gather.4.cloned.1.call-done = bf16[3584,512]{1,0:T(8,128)(2,1)} async-done(((bf16[448,512]{1,0:T(8,128)(2,1)}), bf16[3584,512]{1,0:T(8,128)(2,1)}) %all-gather.4.cloned.1.call-update) | async-done | bytes 3670032 | tf_op jit(solution)/shard_map/all_gather | solution.py:52
  440.5 2.7 fusion.136
  443.2 98.1 %all-gather.6.cloned.1.call-done = bf16[3584,512]{1,0:T(8,128)(2,1)} async-done(((bf16[448,512]{1,0:T(8,128)(2,1)}), bf16[3584,512]{1,0:T(8,128)(2,1)}) %all-gather.6.cloned.1.call-update) | async-done | bytes 3670032 | tf_op jit(solution)/shard_map/all_gather | solution.py:57
  541.3 67.5 %all-gather.8.cloned.1.call-done = bf16[512,3584]{0,1:T(8,128)(2,1)} async-done(((bf16[512,448]{0,1:T(8,128)(2,1)}), bf16[512,3584]{0,1:T(8,128)(2,1)}) %all-gather.8.cloned.1.call-update) | async-done | bytes 3670032 | tf_op jit(solution)/shard_map/all_gather | solution.py:63
  608.8 6.3 fusion.111
  615.1 0.1 copy.23
  615.2 10.9 %gather_fusion = bf16[512,3584]{1,0:T(8,128)(2,1)} fusion(bf16[576,3584]{1,0:T(8,128)(2,1)} %bitcast.23, s32[1024]{0:T(1024)S(1)} %pad_clamp_fusion), kind=kCustom, calls=%fused_computation.1 | custom fusion | bytes 7342080 | tf_op jit(solution)/shard_map/gather | solution.py:110
  626.1 5.0 fusion.1
  631.2 2.0 add_convert_fusion
  (37 shorter events, 0.3 us)
Async XLA Ops:
  10.0 35.2 %copy-start.1 = (s32[512,1]{0,1:T(1,128)}, s32[512,1]{0,1:T(1,128)S(1)}, u32[]{:S(2)}) copy-start(s32[512,1]{0,1:T(1,128)S(1)} %compare_select_fusion.1) | copy-start | bytes 6148
  13.2 26.0 %all-to-all-start.1 = ((bf16[16,1,72]{2,1,0:T(2,128)(2,1)}), bf16[16,1,72]{2,1,0:T(2,128)(2,1)S(1)}, u32[]{:S(2)}, u32[]{:S(2)}) async-start(bf16[16,1,72]{2,1,0:T(2,128)(2,1)} %copy.22), calls=%async_computation.1 | async-start | bytes 16384 | tf_op jit(solution)/shard_map/all_to_all | solution.py:98
  45.2 154.5 %all-to-all-start = ((bf16[16,72,3584]{2,1,0:T(8,128)(2,1)}), bf16[16,72,3584]{2,1,0:T(8,128)(2,1)}, u32[]{:S(2)}, u32[]{:S(2)}) async-start(bf16[16,72,3584]{2,1,0:T(8,128)(2,1)} %bitcast.106), calls=%async_computation | async-start | bytes 16515072 | tf_op jit(solution)/shard_map/all_to_all | solution.py:95
  51.2 329.1 %all-reduce.3.cloned.1.call-start = ((), (), s32[]{:S(2)}) async-start(), calls=%async_computation.8 | async-start | bytes 16515072
  199.7 20.9 %slice-start = ((s8[14680064]{0:T(1024)(128)(4,1)}), s8[4194304]{0:T(1024)(128)(4,1)S(1)}, s32[]{:S(2)}) async-start(s8[14680064]{0:T(1024)(128)(4,1)} %bitcast.115), calls=%async_computation.9 | async-start | bytes 8388608
  199.7 20.9 %slice-start.1 = ((s8[14680064]{0:T(1024)(128)(4,1)}), s8[4194304]{0:T(1024)(128)(4,1)S(1)}, s32[]{:S(2)}) async-start(s8[14680064]{0:T(1024)(128)(4,1)} %bitcast.115), calls=%async_computation.10 | async-start | bytes 8388608
  210.0 10.5 %slice-start.2 = ((s8[14680064]{0:T(1024)(128)(4,1)}), s8[4194304]{0:T(1024)(128)(4,1)S(1)}, s32[]{:S(2)}) async-start(s8[14680064]{0:T(1024)(128)(4,1)} %bitcast.115), calls=%async_computation.11 | async-start | bytes 8388608
  210.1 10.5 %slice-start.3 = ((s8[14680064]{0:T(1024)(128)(4,1)}), s8[2097152]{0:T(1024)(128)(4,1)S(1)}, s32[]{:S(2)}) async-start(s8[14680064]{0:T(1024)(128)(4,1)} %bitcast.115), calls=%async_computation.12 | async-start | bytes 4194304
  310.2 1.8 copy-start.4
  310.2 130.3 %all-gather.4.cloned.1.call-start = ((), (), s32[]{:S(2)}) async-start(), calls=%async_computation.4 | async-start | bytes 4128768 | tf_op jit(solution)/shard_map/all_gather | solution.py:52
  310.8 230.6 %all-gather.6.cloned.1.call-start = ((), (), s32[]{:S(2)}) async-start(), calls=%async_computation.5 | async-start | bytes 4128768 | tf_op jit(solution)/shard_map/all_gather | solution.py:57
  311.4 297.4 %all-gather.8.cloned.1.call-start = ((), (), s32[]{:S(2)}) async-start(), calls=%async_computation.6 | async-start | bytes 4128768 | tf_op jit(solution)/shard_map/all_gather | solution.py:63
  385.4 5.9 copy-start
  385.4 229.8 %all-to-all-start.2 = ((bf16[8,72,3584]{2,1,0:T(8,128)(2,1)}), bf16[8,72,3584]{2,1,0:T(8,128)(2,1)}, u32[]{:S(2)}, u32[]{:S(2)}) async-start(bf16[8,72,3584]{2,1,0:T(8,128)(2,1)} %dynamic-slice_bitcast_fusion), calls=%async_computation.2 | async-start | bytes 8257536 | tf_op jit(solution)/shard_map/all_to_all | solution.py:109
  391.3 239.9 %reduce-scatter.3.cloned.1.call-start = ((), (), s32[]{:S(2)}) async-start(), calls=%async_computation.7 | async-start | bytes 2752512 | tf_op jit(solution)/shard_map/reduce_scatter | solution.py:66
  443.2 171.9 %copy-start.3 = (f32[64,8]{0,1:T(8,128)S(1)}, f32[64,8]{0,1:T(8,128)}, u32[]{:S(2)}) copy-start(f32[64,8]{0,1:T(8,128)} %param.11) | copy-start | bytes 6148
  443.2 172.0 %copy-start.2 = (s32[512,1]{0,1:T(1,128)S(1)}, s32[512,1]{0,1:T(1,128)}, u32[]{:S(2)}) copy-start(s32[512,1]{0,1:T(1,128)} %copy-done.1) | copy-start | bytes 6148
Sparse Core Ops, SparseCore 0:
  310.3 69.9 all-reduce.2
  615.2 7.9 reduce-scatter.2
Sparse Core Ops, SparseCore 1:
  312.9 127.6 all-gather.3
  442.6 98.7 all-gather.5
  543.4 65.3 all-gather.7
where the time goes:
time: 649 us; the launch traced here: 641 us
  waiting for transfers between devices  430 us (66%)
  matrix products  119 us (18%)
  local copies, waits for them, and re-layouts  46 us (7%)
  starting transfers between devices  19.5 us (3%)
  between operations  15.8 us (2%)
  other arithmetic  8.48 us (1%)
    all_to_all x1, waiting for transfers between devices, on_device(): lax.all_to_all(wide_rows, ('expert', 'tensor'), split_axis=0, concat_axis...  148 us
    all_gather x1, waiting for transfers between devices, on_device(): lax.all_gather(shared_up, 'expert', axis=0, tiled=True)  98.1 us
    dot_general x4, matrix products, expert_partial(): jnp.dot(hidden, expert_down[which], preferred_element_type=jnp.float32)  74.5 us
    unnamed x6, waiting for transfers between devices  69.4 us
    all_gather x1, waiting for transfers between devices, on_device(): lax.all_gather(shared_down, 'expert', axis=1, tiled=True)  67.5 us
    all_gather x1, waiting for transfers between devices, on_device(): lax.all_gather(shared_gate, 'expert', axis=0, tiled=True)  46.7 us
    dot_general x4, matrix products, swiglu_rows(): gated = jnp.dot(inputs, gate_piece, preferred_element_type=jnp.float32)  36 us
    scatter x1, local copies, waits for them, and re-layouts, on_device(): send_rows = jnp.zeros((index_count * capacity, feature_count), jnp.bfloat...  18.6 us
  transfers between devices with their start and end apart: 8, of which 5 were waited for; matrix products, arithmetic and copies ran while one was open for 8% of the time, Pallas kernels for 0%

commit v1 on v0

v1 whole, which is shorter than its diff:
```python
import functools

import jax
import jax.numpy as jnp
import numpy as np
from jax import lax
from jax.experimental import pallas as pl
from jax.experimental.pallas import tpu as pltpu
from jax.sharding import PartitionSpec as P

MOST = 18
LANES = 128
MIB = 1 << 20
BF16 = jnp.bfloat16
F32 = jnp.float32


def cost(flops, moved):
    return pl.CostEstimate(flops=int(flops), bytes_accessed=int(moved), transcendentals=0)


def params(mib):
    return pltpu.CompilerParams(vmem_limit_bytes=mib * MIB)


def column_tiles(total, width=512):
    return [(at, min(width, total - at)) for at in range(0, total, width)]


def silu(value):
    return value * (1.0 / (1.0 + jnp.exp(-value)))


def pick_kernel(count, *refs):
    picks, tokens, out = refs[0], refs[1 : 1 + count], refs[1 + count]
    experts, slots, features = out.shape
    which = picks[0]
    for at, width in column_tiles(features):
        piece = jnp.concatenate([t[:, at : at + width] for t in tokens], axis=0)
        rows = jnp.dot(which, piece, preferred_element_type=F32).astype(BF16)
        out[:, :, at : at + width] = rows.reshape(experts, slots, width)


def pick_rows(picks, chunk, tokens, experts):
    slots, width = picks.shape[1:]
    features = tokens[0].shape[1]
    return pl.pallas_call(
        functools.partial(pick_kernel, len(tokens)),
        out_shape=jax.ShapeDtypeStruct((experts, slots // experts, features), BF16),
        grid=(1,),
        in_specs=[pl.BlockSpec((1, slots, width), lambda i: (chunk, 0, 0))]
        + [pl.BlockSpec(t.shape, lambda i: (0, 0)) for t in tokens],
        out_specs=pl.BlockSpec((experts, slots // experts, features), lambda i: (0, 0, 0)),
        compiler_params=params(24),
        cost_estimate=cost(2 * slots * width * features, 2 * features * (slots + width)),
        name="pick_rows",
    )(picks, *tokens)


def expert_kernel(count, *refs):
    rows_in, (scale, gate, up, down) = refs[:count], refs[count : count + 4]
    rows_out, (rows, total) = refs[count + 4 : 2 * count + 4], refs[2 * count + 4 :]
    slots = rows_in[0].shape[1]
    features = rows.shape[1]
    step = pl.program_id(1)

    @pl.when(step == 0)
    def _():
        for i, r in enumerate(rows_in):
            rows[i * slots : (i + 1) * slots, :] = r[0]

    value = rows[...]
    gated = jnp.dot(value, gate[0], preferred_element_type=F32)
    upward = jnp.dot(value, up[0], preferred_element_type=F32)
    hidden = (silu(gated) * upward * scale[0]).astype(BF16)

    @pl.when(step == 0)
    def _():
        for at, width in column_tiles(features):
            total[:, at : at + width] = jnp.dot(
                hidden, down[0, :, at : at + width], preferred_element_type=F32
            )

    @pl.when(step == 1)
    def _():
        for at, width in column_tiles(features):
            done = total[:, at : at + width] + jnp.dot(
                hidden, down[0, :, at : at + width], preferred_element_type=F32
            )
            done = done.astype(BF16)
            for i, r in enumerate(rows_out):
                r[0, :, at : at + width] = done[i * slots : (i + 1) * slots]


def run_experts(rows, scale, gate, up, down):
    experts, slots, features = rows[0].shape
    hidden = gate.shape[2]
    tile = hidden // 2
    count = len(rows)
    height = count * slots
    spec = pl.BlockSpec((1, slots, features), lambda e, h: (e, 0, 0))
    return pl.pallas_call(
        functools.partial(expert_kernel, count),
        out_shape=[jax.ShapeDtypeStruct(r.shape, BF16) for r in rows],
        grid=(experts, 2),
        in_specs=[spec] * count
        + [
            pl.BlockSpec((1, height, 1), lambda e, h: (e, 0, 0)),
            pl.BlockSpec((1, features, tile), lambda e, h: (e, 0, h)),
            pl.BlockSpec((1, features, tile), lambda e, h: (e, 0, h)),
            pl.BlockSpec((1, tile, features), lambda e, h: (e, h, 0)),
        ],
        out_specs=[spec] * count,
        scratch_shapes=[pltpu.VMEM((height, features), BF16), pltpu.VMEM((height, features), F32)],
        compiler_params=params(48),
        cost_estimate=cost(
            6 * experts * height * features * hidden,
            2 * experts * features * (3 * hidden + 2 * height),
        ),
        name="run_experts",
    )(*rows, scale, gate, up, down)


def shared_kernel(count, sums, last, *refs):
    start, tokens, weight = refs[0], refs[1 : 1 + count], refs[1 + count]
    before, out = refs[2 + count : 2 + count + sums], refs[2 + count + sums]
    window = pl.ds(pl.multiple_of(start[0], LANES), weight.shape[0])
    piece = jnp.concatenate([t[:, window] for t in tokens], axis=0)
    value = jnp.dot(piece, weight[...], preferred_element_type=F32)
    for b in before:
        value = value + b[...].astype(F32)
    if last:
        half = value.shape[1] // 2
        value = silu(value[:, :half]) * value[:, half:]
    out[...] = value.astype(BF16)


def shared_term(start, tokens, weight, before, last=False):
    height = sum(t.shape[0] for t in tokens)
    width = weight.shape[1] // 2 if last else weight.shape[1]
    vmem = pl.BlockSpec(memory_space=pltpu.VMEM)
    return pl.pallas_call(
        functools.partial(shared_kernel, len(tokens), len(before), last),
        out_shape=jax.ShapeDtypeStruct((height, width), BF16),
        in_specs=[pl.BlockSpec(memory_space=pltpu.SMEM)]
        + [vmem] * (len(tokens) + 1 + len(before)),
        out_specs=vmem,
        compiler_params=params(16),
        cost_estimate=cost(
            2 * height * weight.size, 2 * (weight.size + height * (tokens[0].shape[1] + 3 * width))
        ),
        name="shared_term",
    )(start, *tokens, weight, *before)


def merge_kernel(start, picks, rows, hidden, down, own, other):
    height = own.shape[0]
    which = picks[0]
    for at, width in column_tiles(own.shape[1]):
        value = jnp.concatenate(
            [rows[e, :, at : at + width] for e in range(rows.shape[0])], axis=0
        )
        value = jnp.dot(which, value, preferred_element_type=F32)
        own[:, at : at + width] = value[:height].astype(own.dtype)
        other[:, at : at + width] = value[height:].astype(other.dtype)
    window = pl.ds(pl.multiple_of(start[0], LANES), down.shape[1])
    value = jnp.dot(hidden[...], down[...], preferred_element_type=F32)
    own[:, window] = (own[:, window].astype(F32) + value[:height]).astype(own.dtype)
    other[:, window] = (other[:, window].astype(F32) + value[height:]).astype(other.dtype)


def merge_block(start, picks, place, rows, hidden, down):
    height, slots = picks.shape[1:]
    features = rows.shape[2]
    whole = lambda a: pl.BlockSpec(a.shape, lambda i: (0,) * a.ndim)
    return pl.pallas_call(
        merge_kernel,
        out_shape=[jax.ShapeDtypeStruct((height // 2, features), BF16)] * 2,
        grid=(1,),
        in_specs=[
            pl.BlockSpec(memory_space=pltpu.SMEM),
            pl.BlockSpec((1, height, slots), lambda i: (place, 0, 0)),
            whole(rows),
            whole(hidden),
            whole(down),
        ],
        out_specs=[pl.BlockSpec((height // 2, features), lambda i: (0, 0))] * 2,
        compiler_params=params(24),
        cost_estimate=cost(2 * height * slots * features, 2 * features * (slots + 2 * height)),
        name="merge_block",
    )(start, picks, rows, hidden, down)


def window_of(count, size, total):
    need = max((i * size) % LANES + size for i in range(count))
    width = min(total, -(-need // LANES) * LANES)
    starts = np.array([min(i * size // LANES * LANES, total - width) for i in range(count)])
    return width, starts.astype(np.int32), (np.arange(count) * size - starts).astype(np.int32)


def on_device(
    tokens,
    route_ids,
    route_gates,
    expert_gate,
    expert_up,
    expert_down,
    shared_gate,
    shared_up,
    shared_down,
):
    n = lax.axis_size("expert")
    half = n // 2
    me, core = lax.axis_index("expert"), lax.axis_index("tensor")
    row_count, features = tokens.shape
    top = route_ids.shape[1]
    experts = expert_gate.shape[0]
    block = 2 * row_count

    path = np.array(list(range(0, n, 2)) + list(range(n - 1, 0, -2)), np.int32)
    onward = [(int(path[i]), int(path[(i + 1) % n])) for i in range(n)]
    backward = [(b, a) for a, b in onward]
    place = jnp.asarray(np.argsort(path).astype(np.int32))[me]
    send_on = lambda a: lax.ppermute(a, "expert", onward)
    send_back = lambda a: lax.ppermute(a, "expert", backward)
    swap = lambda a: lax.ppermute(a, "tensor", [(0, 1), (1, 0)])

    routing = jnp.concatenate([route_ids.astype(F32), route_gates], axis=1)
    routing = lax.all_gather(routing, ("expert", "tensor"), axis=0, tiled=True)
    routing = routing.reshape(n, 2, row_count, 2 * top)
    pairs = [0, half] + [p for k in range(1, half) for p in (k, n - k)]
    chunk_of = {p: i // 2 for i, p in enumerate(pairs)}
    order = jnp.asarray(path)[(place + jnp.asarray(np.array(pairs, np.int32))) % n]
    routing = routing[order]
    routing = jnp.where(core == 0, routing, routing[:, ::-1])
    routing = routing.reshape(half, 2 * block, 2 * top)
    ids, gates = routing[..., :top].astype(jnp.int32), routing[..., top:]
    local = me * experts + jnp.arange(experts, dtype=jnp.int32)
    hit = ids[:, None] == local[None, :, None, None]
    named = jnp.any(hit, axis=3)
    gate_of = jnp.sum(jnp.where(hit, gates[:, None], 0.0), axis=3)
    slots = -(-4 * MOST // 16) * 16
    upto = jnp.asarray(np.triu(np.ones((2 * block, 2 * block), np.float32)), BF16)
    rank = jnp.dot(named.astype(BF16), upto, preferred_element_type=F32).astype(jnp.int32) - 1
    first = (jnp.arange(experts, dtype=jnp.int32) * slots)[None, :, None]
    slot = jnp.where(named, rank + first, -1)
    number = jnp.arange(experts * slots, dtype=jnp.int32)
    match = slot[:, :, None, :] == number[None, None, :, None]
    picks = jnp.any(match, axis=1).astype(BF16)
    scale = jnp.sum(jnp.where(match, gate_of[:, :, None, :], 0.0), axis=(1, 3))
    scale = scale.reshape(half, experts, slots).transpose(1, 0, 2)
    scale = scale.reshape(experts, half * slots, 1)
    spread = jnp.swapaxes(slot, 1, 2)
    spread = jnp.any(spread[:, :, :, None] == number[None, None, None, :], axis=2).astype(BF16)
    spread = spread.reshape(n, block, experts * slots)

    width, starts, shifts = window_of(n, shared_gate.shape[0], features)
    start = jnp.asarray(starts)[me].reshape(1)
    shift = jnp.asarray(shifts)[me]
    zero = jnp.int32(0)
    both = jnp.concatenate([shared_gate, shared_up], axis=1)
    both = lax.dynamic_update_slice(jnp.zeros((width, both.shape[1]), BF16), both, (shift, zero))
    down = lax.dynamic_update_slice(
        jnp.zeros((shared_down.shape[0], width), BF16), shared_down, (zero, shift)
    )

    seen = {0: [tokens, swap(tokens)]}
    term = lambda r, *before, **k: shared_term(start, seen[r], both, before, **k)
    sum_on, sum_back = term(0), None
    ahead, behind = tokens, tokens
    rows = {}
    for k in range(1, half):
        ahead, behind = send_on(ahead), send_back(behind)
        seen[n - k] = [ahead, swap(ahead)]
        seen[k] = [behind, swap(behind)]
        sum_on = term(n - k, send_on(sum_on))
        sum_back = term(k) if k == 1 else term(k, send_back(sum_back))
        rows[k] = pick_rows(picks, k, seen[k] + seen[n - k], experts)
    split = row_count // 2
    ahead, behind = send_on(ahead[:split]), send_back(behind[split:])
    seen[half] = [ahead, behind, swap(ahead), swap(behind)]
    rows[0] = pick_rows(picks, 0, seen[0] + seen[half], experts)
    hidden = {half: term(half, send_on(sum_on), send_back(sum_back), last=True)}

    routed = {}
    for at in range(0, half, 4):
        group = list(range(at, min(at + 4, half)))
        part = scale[:, at * slots : (at + len(group)) * slots]
        outs = run_experts([rows[j] for j in group], part, expert_gate, expert_up, expert_down)
        routed.update(zip(group, outs))

    for k in range(1, half):
        hidden[half - k] = send_on(hidden[half - k + 1])
        hidden[half + k] = send_back(hidden[half + k - 1])
    hidden[0] = jnp.concatenate(
        [send_on(hidden[1][:row_count]), send_back(hidden[n - 1][row_count:])], axis=0
    )

    def contribution(r):
        own, other = merge_block(
            start, spread, pairs.index(r), routed[chunk_of[r]], hidden[r], down
        )
        return own.astype(F32), swap(other).astype(F32)

    own, other = contribution(half)
    ahead = send_on((own + other)[:split].astype(BF16))
    behind = send_back((own + other)[split:].astype(BF16))
    for k in range(half - 1, 0, -1):
        own, other = contribution(k)
        sent = ahead.astype(F32)
        if k == half - 1:
            sent = jnp.concatenate([sent, jnp.zeros((row_count - split, features), F32)], axis=0)
        ahead = send_on((own + other + sent).astype(BF16))
        own, other = contribution(n - k)
        sent = behind.astype(F32)
        if k == half - 1:
            sent = jnp.concatenate([jnp.zeros((split, features), F32), sent], axis=0)
        behind = send_back((own + other + sent).astype(BF16))
    own, other = contribution(0)
    return (own + other + ahead.astype(F32) + behind.astype(F32)).astype(BF16)


def solution(mesh):
    in_specs = (
        P(("group", "expert", "tensor"), None),
        P(("group", "expert", "tensor"), None),
        P(("group", "expert", "tensor"), None),
        P("expert", None, "tensor"),
        P("expert", None, "tensor"),
        P("expert", "tensor", None),
        P("expert", "tensor"),
        P("expert", "tensor"),
        P("tensor", "expert"),
    )
    out_specs = P(("group", "expert", "tensor"), None)
    return jax.shard_map(
        on_device, mesh=mesh, in_specs=in_specs, out_specs=out_specs, check_vma=False
    )
```

time: 649 us -> 230 us (0.35); the launches traced: 641 us -> 229 us
  waiting for transfers between devices: 430 us -> 71.9 us
  matrix products: 119 us -> 1.12 us
  Pallas kernels: 0 us -> 60.7 us
  blocking collectives: 2.46 us -> 22.4 us
  local copies, waits for them, and re-layouts: 46 us -> 26.1 us
  starting transfers between devices: 19.5 us -> 33.8 us
  between operations: 15.8 us -> 2.63 us
    all_gather x3 -> x0, waiting for transfers between devices: 212 us -> none  [the longest x1 98.1 us: on_device(): lax.all_gather(shared_up, 'expert', axis=0, tiled=True)]
    all_to_all x3 -> x0, waiting for transfers between devices: 148 us -> none  [the longest x1 148 us: on_device(): lax.all_to_all(wide_rows, ('expert', 'tensor'), split_axis=0, concat_axis...]
    dot_general x10 -> x1, matrix products: 119 us -> 1.12 us  [on_device(): jnp.dot(named.astype(BF16), upto, preferred_element_type=F32)]
    ppermute x0 -> x48, waiting for transfers between devices: none -> 71.9 us  [the longest x15 37.9 us: on_device(): send_back = lambda a: lax.ppermute(a, 'expert', backward)]
    unnamed x6 -> x0, waiting for transfers between devices: 69.4 us -> none
    pallas_call x0 -> x21, Pallas kernels: none -> 60.7 us  [the longest x1 26.3 us: run_experts(): pl.pallas_call(functools.partial(expert_kernel, count), out_shape=[jax.Sh...]
    ppermute x0 -> x48, starting transfers between devices: none -> 33.8 us  [the longest x15 21.2 us: on_device(): send_back = lambda a: lax.ppermute(a, 'expert', backward)]
    scatter x2 -> x0, local copies, waits for them, and re-layouts: 21.1 us -> none  [the longest x1 18.6 us: on_device(): send_rows = jnp.zeros((index_count * capacity, feature_count), jnp.bfloat...]
  transfers between devices with their start and end apart: 8 -> 48, of which waited for: 5 -> 12; matrix products, arithmetic and copies ran while one was open for 8% -> 12% of each run, Pallas kernels for 0% -> 25%
where the time goes in v1:
time: 230 us; the launch traced here: 229 us
  waiting for transfers between devices  71.9 us (31%)
  Pallas kernels  60.7 us (26%)
  starting transfers between devices  33.8 us (15%)
  local copies, waits for them, and re-layouts  26.1 us (11%)
  blocking collectives  22.4 us (10%)
  other arithmetic  10.6 us (5%)
  between operations  2.63 us (1%)
    ppermute x15, waiting for transfers between devices, on_device(): send_back = lambda a: lax.ppermute(a, 'expert', backward)  37.9 us
    ppermute x16, waiting for transfers between devices, on_device(): send_on = lambda a: lax.ppermute(a, 'expert', onward)  33.9 us
    pallas_call x1, Pallas kernels, run_experts(): pl.pallas_call(functools.partial(expert_kernel, count), out_shape=[jax.Sh...  26.3 us
    all_gather x1, blocking collectives, on_device(): routing = lax.all_gather(routing, ('expert', 'tensor'), axis=0, tiled=True)  22.4 us
    ppermute x15, starting transfers between devices, on_device(): send_back = lambda a: lax.ppermute(a, 'expert', backward)  21.2 us
    pallas_call x8, Pallas kernels, shared_term(): pl.pallas_call(functools.partial(shared_kernel, len(tokens), len(before),...  16.1 us
    pallas_call x8, Pallas kernels, merge_block(): pl.pallas_call(merge_kernel, out_shape=[jax.ShapeDtypeStruct((height // 2...  11.5 us
    unnamed x53, local copies, waits for them, and re-layouts  10.3 us
  transfers between devices with their start and end apart: 48, of which 12 were waited for; matrix products, arithmetic and copies ran while one was open for 12% of the time, Pallas kernels for 25%

profile of v1, /device:TPU:0, one launch (start us, length us, event | category | flops | bytes accessed | tf_op | source)
XLA Modules:
  0.0 229.2 jit_solution(18201289697315827769)
XLA Ops:
  0.5 2.6 %collective-permute-start.1 = (bf16[64,3584]{1,0:T(8,128)(2,1)}, bf16[64,3584]{1,0:T(8,128)(2,1)S(1)}, u32[]{:S(2)}, u32[]{:S(2)}) collective-permute-start(bf16[64,3584]{1,0:T(8,128)(2,1)} %refs_1_.3), channel_id=1, source_target_pairs={{0,4},{4,8},{8,12},{12,14},{14,10},{10,6},{6,2},{2,0},{1,5},{5,9},... | collective-permute-start | bytes 1376264 | tf_op jit(solution)/shard_map/ppermute | solution.py:224
  8.3 22.4 %all-gather = f32[16,64,16]{1,2,0:T(8,128)S(1)} all-gather(f32[1,64,16]{1,2,0:T(8,128)S(1)} %maximum_bitcast_fusion), channel_id=1, replica_groups=mesh['group'=2,'expert'=8,'tensor'=2] {'expert','tensor'}, dimensions={0}, use_global_device_ids=true | all-gather | bytes 69632 | tf_op jit(solution)/shard_map/all_gather | solution.py:229
  37.8 1.7 shared_term.8
  39.8 1.9 collective-permute-start.6
  41.8 7.2 %collective-permute-done.17.refs_4_ = bf16[128,1024]{1,0:T(8,128)(2,1)} collective-permute-done((bf16[128,1024]{1,0:T(8,128)(2,1)}, bf16[128,1024]{1,0:T(8,128)(2,1)}, u32[]{:S(2)}, u32[]{:S(2)}) %collective-permute-start.17) | collective-permute-done | bytes 262176 | tf_op jit(solution)/shard_map/ppermute | solution.py:224
  49.0 1.9 shared_term.9
  51.0 7.8 %collective-permute-done.2.refs_3_.refs_1_ = bf16[64,3584]{1,0:T(8,128)(2,1)} collective-permute-done((bf16[64,3584]{1,0:T(8,128)(2,1)S(1)}, bf16[64,3584]{1,0:T(8,128)(2,1)}, u32[]{:S(2)}, u32[]{:S(2)}) %collective-permute-start.2) | collective-permute-done | bytes 458784 | tf_op jit(solution)/shard_map/ppermute | solution.py:224
  58.8 2.0 collective-permute-start.7
  64.5 2.0 shared_term.10
  66.5 2.1 collective-permute-start.19
  68.6 3.9 %collective-permute-done.7.refs_1_ = bf16[64,3584]{1,0:T(8,128)(2,1)} collective-permute-done((bf16[64,3584]{1,0:T(8,128)(2,1)}, bf16[64,3584]{1,0:T(8,128)(2,1)}, u32[]{:S(2)}, u32[]{:S(2)}) %collective-permute-start.7) | collective-permute-done | bytes 458784 | tf_op jit(solution)/shard_map/ppermute | solution.py:225
  73.5 2.0 collective-permute-start.8
  76.3 1.7 collective-permute-done.21.refs_4_
  79.8 2.8 %shared_term.13 = bf16[128,1024]{1,0:T(8,128)(2,1)} custom-call(s32[1]{0:T(128)} %dynamic_slice.9.refs_0_.start, bf16[64,3584]{1,0:T(8,128)(2,1)} %collective-permute-done.6.refs_1_, bf16[64,3584]{1,0:T(8,128)(2,1)S(1)} %collective-permute-done.13.refs_2_, bf16[512,1024]{1,0:T(8,128)(2,1)S(1)} %maximum_dynamic-update-slice_fusion.refs_3_.refs_5_, ...), custom_call_target="tpu_custom_call" | custom-call | flops 134217728 | bytes 2752512 | tf_op jit(solution)/shard_map/shared_term/pallas_call | solution.py:142
  82.6 2.0 collective-permute-start.22
  87.8 2.0 copy.51
  90.8 1.4 copy.47
  92.3 6.1 %dynamic_update_slice.7.down = bf16[512,512]{1,0:T(8,128)(2,1)S(1)} dynamic-update-slice(bf16[512,512]{1,0:T(8,128)(2,1)S(1)} %broadcast_in_dim.51, bf16[512,448]{1,0:T(8,128)(2,1)} %copy.51, s32[]{:T(128)} %constant.21.clone.1, s32[]{:T(128)S(6)} %select_n.63) | dynamic-update-slice | bytes 917508 | tf_op jit(solution)/shard_map/dynamic_update_slice | solution.py:263
  103.3 1.4 copy-done
  104.6 2.0 pick_rows.6.refs_2_
  106.6 2.1 shared_term.11
  108.8 2.2 shared_term.14
  111.1 2.2 collective-permute-start.23
  113.3 2.1 pick_rows.7.refs_3_
  115.4 1.4 copy-done.2
  116.8 2.1 pick_rows.4.refs_0_
  118.9 1.4 copy-done.3
  120.3 26.3 %run_experts.1 = (bf16[4,80,3584]{2,1,0:T(8,128)(2,1)S(1)}, bf16[4,80,3584]{2,1,0:T(8,128)(2,1)S(1)}, bf16[4,80,3584]{2,1,0:T(8,128)(2,1)}, bf16[4,80,3584]{2,1,0:T(8,128)(2,1)}) custom-call(bf16[4,80,3584]{2,1,0:T(8,128)(2,1)} %copy-done.3, bf16[4,80,3584]{2,1,0:T(8,128)(2,1)} %copy-done, bf16[4,80,3584]{2,1,0:T(8,128)(2,1)} %copy-done.1, ...), custom_call_target="tpu_custom_call" | custom-call | flops 14092861440 | bytes 62390272 | tf_op jit(solution)/shard_map/run_experts/pallas_call | solution.py:102
  146.6 2.3 %shared_term.15.hidden = bf16[128,512]{1,0:T(8,128)(2,1)S(1)} custom-call(s32[1]{0:T(128)} %dynamic_slice.9.refs_0_.start, bf16[32,3584]{1,0:T(8,128)(2,1)} %collective-permute-done.4.refs_3_.refs_1_, bf16[32,3584]{1,0:T(8,128)(2,1)} %collective-permute-done.8.refs_4_.refs_2_, bf16[32,3584]{1,0:T(8,128)(2,1)} %collective-permute-done.9.refs_5_.refs_3_, ...), custom_call_target="tpu_custom_call" | custom-call | flops 134217728 | bytes 2359296 | tf_op jit(solution)/shard_map/shared_term/pallas_call | solution.py:142
  148.9 1.6 merge_block.12
  150.6 2.0 collective-permute-start.28
  152.6 3.8 %collective-permute-done.24.hidden = bf16[128,512]{1,0:T(8,128)(2,1)S(1)} collective-permute-done((bf16[128,512]{1,0:T(8,128)(2,1)S(1)}, bf16[128,512]{1,0:T(8,128)(2,1)S(1)}, u32[]{:S(2)}, u32[]{:S(2)}) %collective-permute-start.24) | collective-permute-done | bytes 131104 | tf_op jit(solution)/shard_map/ppermute | solution.py:224
  156.7 1.7 collective-permute-start.29
  158.5 1.4 merge_block.11
  160.0 1.5 merge_block.15
  162.2 1.7 collective-permute-start.30
  164.5 1.4 merge_block.10
  165.9 2.4 %collective-permute-done.26.hidden = bf16[128,512]{1,0:T(8,128)(2,1)S(1)} collective-permute-done((bf16[128,512]{1,0:T(8,128)(2,1)S(1)}, bf16[128,512]{1,0:T(8,128)(2,1)S(1)}, u32[]{:S(2)}, u32[]{:S(2)}) %collective-permute-start.26) | collective-permute-done | bytes 131104 | tf_op jit(solution)/shard_map/ppermute | solution.py:224
  168.6 1.8 collective-permute-start.31
  170.4 1.4 merge_block.14
  171.8 1.4 merge_block.9
  173.2 1.4 merge_block.13
  175.2 1.4 merge_block.8
  178.1 6.7 %collective-permute-done.44 = bf16[32,3584]{1,0:T(8,128)(2,1)S(1)} collective-permute-done((bf16[32,3584]{1,0:T(8,128)(2,1)S(1)}, bf16[32,3584]{1,0:T(8,128)(2,1)S(1)}, u32[]{:S(2)}, u32[]{:S(2)}) %collective-permute-start.44) | collective-permute-done | bytes 229408 | tf_op jit(solution)/shard_map/ppermute | solution.py:225
  185.3 11.5 %collective-permute-done.38 = bf16[64,3584]{1,0:T(8,128)(2,1)S(1)} collective-permute-done((bf16[64,3584]{1,0:T(8,128)(2,1)S(1)}, bf16[64,3584]{1,0:T(8,128)(2,1)S(1)}, u32[]{:S(2)}, u32[]{:S(2)}) %collective-permute-start.38) | collective-permute-done | bytes 458784 | tf_op jit(solution)/shard_map/ppermute | solution.py:224
  199.0 8.9 %collective-permute-done.45 = bf16[64,3584]{1,0:T(8,128)(2,1)S(1)} collective-permute-done((bf16[64,3584]{1,0:T(8,128)(2,1)S(1)}, bf16[64,3584]{1,0:T(8,128)(2,1)S(1)}, u32[]{:S(2)}, u32[]{:S(2)}) %collective-permute-start.45) | collective-permute-done | bytes 458784 | tf_op jit(solution)/shard_map/ppermute | solution.py:225
  210.4 8.2 %collective-permute-done.46 = bf16[64,3584]{1,0:T(8,128)(2,1)S(1)} collective-permute-done((bf16[64,3584]{1,0:T(8,128)(2,1)S(1)}, bf16[64,3584]{1,0:T(8,128)(2,1)S(1)}, u32[]{:S(2)}, u32[]{:S(2)}) %collective-permute-start.46) | collective-permute-done | bytes 458784 | tf_op jit(solution)/shard_map/ppermute | solution.py:225
  219.8 8.5 %collective-permute-done.47 = bf16[64,3584]{1,0:T(8,128)(2,1)S(1)} collective-permute-done((bf16[64,3584]{1,0:T(8,128)(2,1)S(1)}, bf16[64,3584]{1,0:T(8,128)(2,1)S(1)}, u32[]{:S(2)}, u32[]{:S(2)}) %collective-permute-start.47) | collective-permute-done | bytes 458784 | tf_op jit(solution)/shard_map/ppermute | solution.py:225
  (172 shorter events, 38.8 us)
Async XLA Ops:
  0.0 37.8 %collective-permute-start = (bf16[64,3584]{1,0:T(8,128)(2,1)}, bf16[64,3584]{1,0:T(8,128)(2,1)S(1)}, u32[]{:S(2)}, u32[]{:S(2)}) collective-permute-start(bf16[64,3584]{1,0:T(8,128)(2,1)} %refs_1_.3), channel_id=1, source_target_pairs={{0,1},{1,0},{2,3},{3,2},{4,5},{5,4},{6,7},{7,6},{8,9},{9,8},{10,11... | collective-permute-start | bytes 1376264 | tf_op jit(solution)/shard_map/ppermute | solution.py:226
  0.5 36.9 %collective-permute-start.1 = (bf16[64,3584]{1,0:T(8,128)(2,1)}, bf16[64,3584]{1,0:T(8,128)(2,1)S(1)}, u32[]{:S(2)}, u32[]{:S(2)}) collective-permute-start(bf16[64,3584]{1,0:T(8,128)(2,1)} %refs_1_.3), channel_id=1, source_target_pairs={{0,4},{4,8},{8,12},{12,14},{14,10},{10,6},{6,2},{2,0},{1,5},{5,9},... | collective-permute-start | bytes 1376264 | tf_op jit(solution)/shard_map/ppermute | solution.py:224
  3.1 36.5 %collective-permute-start.5 = (bf16[64,3584]{1,0:T(8,128)(2,1)}, bf16[64,3584]{1,0:T(8,128)(2,1)S(1)}, u32[]{:S(2)}, u32[]{:S(2)}) collective-permute-start(bf16[64,3584]{1,0:T(8,128)(2,1)} %refs_1_.3), channel_id=1, source_target_pairs={{4,0},{8,4},{12,8},{14,12},{10,14},{6,10},{2,6},{0,2},{5,1},{9,5},... | collective-permute-start | bytes 1376264 | tf_op jit(solution)/shard_map/ppermute | solution.py:225
  37.4 11.6 %collective-permute-start.12 = (bf16[64,3584]{1,0:T(8,128)(2,1)S(1)}, bf16[64,3584]{1,0:T(8,128)(2,1)S(1)}, u32[]{:S(2)}, u32[]{:S(2)}) collective-permute-start(bf16[64,3584]{1,0:T(8,128)(2,1)S(1)} %collective-permute-done.1.refs_3_.refs_1_), channel_id=1, source_target_pairs={{0,1},{1,0},{2,3},{3,2},{4,5},{5,4},{6,7},{7,6},{8,9},{9,8},{10,11... | collective-permute-start | bytes 1376264 | tf_op jit(solution)/shard_map/ppermute | solution.py:226
  39.5 9.5 %collective-permute-start.17 = (bf16[128,1024]{1,0:T(8,128)(2,1)}, bf16[128,1024]{1,0:T(8,128)(2,1)}, u32[]{:S(2)}, u32[]{:S(2)}) collective-permute-start(bf16[128,1024]{1,0:T(8,128)(2,1)} %shared_term.8), channel_id=1, source_target_pairs={{0,4},{4,8},{8,12},{12,14},{14,10},{10,6},{6,2},{2,0},{1,5},{5,9},... | collective-permute-start | bytes 786440 | tf_op jit(solution)/shard_map/ppermute | solution.py:224
  39.5 19.3 %collective-permute-start.2 = (bf16[64,3584]{1,0:T(8,128)(2,1)S(1)}, bf16[64,3584]{1,0:T(8,128)(2,1)}, u32[]{:S(2)}, u32[]{:S(2)}) collective-permute-start(bf16[64,3584]{1,0:T(8,128)(2,1)S(1)} %collective-permute-done.1.refs_3_.refs_1_), channel_id=1, source_target_pairs={{0,4},{4,8},{8,12},{12,14},{14,10},{10,6},{6,2},{2,0},{1,5},{5,9},... | collective-permute-start | bytes 1376264 | tf_op jit(solution)/shard_map/ppermute | solution.py:224
  39.5 21.3 %collective-permute-start.11 = (bf16[64,3584]{1,0:T(8,128)(2,1)S(1)}, bf16[64,3584]{1,0:T(8,128)(2,1)S(1)}, u32[]{:S(2)}, u32[]{:S(2)}) collective-permute-start(bf16[64,3584]{1,0:T(8,128)(2,1)S(1)} %collective-permute-done.5.refs_1_), channel_id=1, source_target_pairs={{0,1},{1,0},{2,3},{3,2},{4,5},{5,4},{6,7},{7,6},{8,9},{9,8},{10,11... | collective-permute-start | bytes 1376264 | tf_op jit(solution)/shard_map/ppermute | solution.py:226
  39.8 19.1 %collective-permute-start.6 = (bf16[64,3584]{1,0:T(8,128)(2,1)S(1)}, bf16[64,3584]{1,0:T(8,128)(2,1)}, u32[]{:S(2)}, u32[]{:S(2)}) collective-permute-start(bf16[64,3584]{1,0:T(8,128)(2,1)S(1)} %collective-permute-done.5.refs_1_), channel_id=1, source_target_pairs={{4,0},{8,4},{12,8},{14,12},{10,14},{6,10},{2,6},{0,2},{5,1},{9,5},... | collective-permute-start | bytes 1376264 | tf_op jit(solution)/shard_map/ppermute | solution.py:225
  51.0 13.4 %collective-permute-start.18 = (bf16[128,1024]{1,0:T(8,128)(2,1)S(1)}, bf16[128,1024]{1,0:T(8,128)(2,1)S(1)}, u32[]{:S(2)}, u32[]{:S(2)}) collective-permute-start(bf16[128,1024]{1,0:T(8,128)(2,1)S(1)} %shared_term.9), channel_id=1, source_target_pairs={{0,4},{4,8},{8,12},{12,14},{14,10},{10,6},{6,2},{2,0},{1,5},{5,9},... | collective-permute-start | bytes 786440 | tf_op jit(solution)/shard_map/ppermute | solution.py:224
  58.8 5.6 %collective-permute-start.14 = (bf16[64,3584]{1,0:T(8,128)(2,1)}, bf16[64,3584]{1,0:T(8,128)(2,1)S(1)}, u32[]{:S(2)}, u32[]{:S(2)}) collective-permute-start(bf16[64,3584]{1,0:T(8,128)(2,1)} %collective-permute-done.2.refs_3_.refs_1_), channel_id=1, source_target_pairs={{0,1},{1,0},{2,3},{3,2},{4,5},{5,4},{6,7},{7,6},{8,9},{9,8},{10,11... | collective-permute-start | bytes 1376264 | tf_op jit(solution)/shard_map/ppermute | solution.py:226
  58.8 16.7 %collective-permute-start.3 = (bf16[64,3584]{1,0:T(8,128)(2,1)}, bf16[64,3584]{1,0:T(8,128)(2,1)S(1)}, u32[]{:S(2)}, u32[]{:S(2)}) collective-permute-start(bf16[64,3584]{1,0:T(8,128)(2,1)} %collective-permute-done.2.refs_3_.refs_1_), channel_id=1, source_target_pairs={{0,4},{4,8},{8,12},{12,14},{14,10},{10,6},{6,2},{2,0},{1,5},{5,9},... | collective-permute-start | bytes 1376264 | tf_op jit(solution)/shard_map/ppermute | solution.py:224
  58.8 13.7 %collective-permute-start.7 = (bf16[64,3584]{1,0:T(8,128)(2,1)}, bf16[64,3584]{1,0:T(8,128)(2,1)}, u32[]{:S(2)}, u32[]{:S(2)}) collective-permute-start(bf16[64,3584]{1,0:T(8,128)(2,1)} %collective-permute-done.6.refs_1_), channel_id=1, source_target_pairs={{4,0},{8,4},{12,8},{14,12},{10,14},{6,10},{2,6},{0,2},{5,1},{9,5},... | collective-permute-start | bytes 1376264 | tf_op jit(solution)/shard_map/ppermute | solution.py:225
  60.9 17.2 %collective-permute-start.13 = (bf16[64,3584]{1,0:T(8,128)(2,1)}, bf16[64,3584]{1,0:T(8,128)(2,1)S(1)}, u32[]{:S(2)}, u32[]{:S(2)}) collective-permute-start(bf16[64,3584]{1,0:T(8,128)(2,1)} %collective-permute-done.6.refs_1_), channel_id=1, source_target_pairs={{0,1},{1,0},{2,3},{3,2},{4,5},{5,4},{6,7},{7,6},{8,9},{9,8},{10,11... | collective-permute-start | bytes 1376264 | tf_op jit(solution)/shard_map/ppermute | solution.py:226
  64.3 13.7 %collective-permute-start.21 = (bf16[128,1024]{1,0:T(8,128)(2,1)S(1)}, bf16[128,1024]{1,0:T(8,128)(2,1)S(1)}, u32[]{:S(2)}, u32[]{:S(2)}) collective-permute-start(bf16[128,1024]{1,0:T(8,128)(2,1)S(1)} %shared_term.12), channel_id=1, source_target_pairs={{4,0},{8,4},{12,8},{14,12},{10,14},{6,10},{2,6},{0,2},{5,1},{9,5},... | collective-permute-start | bytes 786440 | tf_op jit(solution)/shard_map/ppermute | solution.py:225
  66.5 18.1 %collective-permute-start.19 = (bf16[128,1024]{1,0:T(8,128)(2,1)S(1)}, bf16[128,1024]{1,0:T(8,128)(2,1)S(1)}, u32[]{:S(2)}, u32[]{:S(2)}) collective-permute-start(bf16[128,1024]{1,0:T(8,128)(2,1)S(1)} %shared_term.10), channel_id=1, source_target_pairs={{0,4},{4,8},{8,12},{12,14},{14,10},{10,6},{6,2},{2,0},{1,5},{5,9},... | collective-permute-start | bytes 786440 | tf_op jit(solution)/shard_map/ppermute | solution.py:224
  73.5 9.1 %collective-permute-start.8 = (bf16[32,3584]{1,0:T(8,128)(2,1)S(1)}, bf16[32,3584]{1,0:T(8,128)(2,1)}, u32[]{:S(2)}, u32[]{:S(2)}) collective-permute-start(bf16[32,3584]{1,0:T(8,128)(2,1)S(1)} %slice.40), channel_id=1, source_target_pairs={{4,0},{8,4},{12,8},{14,12},{10,14},{6,10},{2,6},{0,2},{5,1},{9,5},... | collective-permute-start | bytes 688136 | tf_op jit(solution)/shard_map/ppermute | solution.py:225
  75.6 9.1 %collective-permute-start.4 = (bf16[32,3584]{1,0:T(8,128)(2,1)S(1)}, bf16[32,3584]{1,0:T(8,128)(2,1)}, u32[]{:S(2)}, u32[]{:S(2)}) collective-permute-start(bf16[32,3584]{1,0:T(8,128)(2,1)S(1)} %slice.39), channel_id=1, source_target_pairs={{0,4},{4,8},{8,12},{12,14},{14,10},{10,6},{6,2},{2,0},{1,5},{5,9},... | collective-permute-start | bytes 688136 | tf_op jit(solution)/shard_map/ppermute | solution.py:224
  78.0 28.6 %collective-permute-start.16 = (bf16[64,3584]{1,0:T(8,128)(2,1)S(1)}, bf16[64,3584]{1,0:T(8,128)(2,1)}, u32[]{:S(2)}, u32[]{:S(2)}) collective-permute-start(bf16[64,3584]{1,0:T(8,128)(2,1)S(1)} %collective-permute-done.3.refs_3_.refs_1_), channel_id=1, source_target_pairs={{0,1},{1,0},{2,3},{3,2},{4,5},{5,4},{6,7},{7,6},{8,9},{9,8},{10,11... | collective-permute-start | bytes 1376264 | tf_op jit(solution)/shard_map/ppermute | solution.py:226
  78.1 30.8 %collective-permute-start.15 = (bf16[64,3584]{1,0:T(8,128)(2,1)}, bf16[64,3584]{1,0:T(8,128)(2,1)}, u32[]{:S(2)}, u32[]{:S(2)}) collective-permute-start(bf16[64,3584]{1,0:T(8,128)(2,1)} %collective-permute-done.7.refs_1_), channel_id=1, source_target_pairs={{0,1},{1,0},{2,3},{3,2},{4,5},{5,4},{6,7},{7,6},{8,9},{9,8},{10,11... | collective-permute-start | bytes 1376264 | tf_op jit(solution)/shard_map/ppermute | solution.py:226
  82.6 26.2 %collective-permute-start.22 = (bf16[128,1024]{1,0:T(8,128)(2,1)}, bf16[128,1024]{1,0:T(8,128)(2,1)}, u32[]{:S(2)}, u32[]{:S(2)}) collective-permute-start(bf16[128,1024]{1,0:T(8,128)(2,1)} %shared_term.13), channel_id=1, source_target_pairs={{4,0},{8,4},{12,8},{14,12},{10,14},{6,10},{2,6},{0,2},{5,1},{9,5},... | collective-permute-start | bytes 786440 | tf_op jit(solution)/shard_map/ppermute | solution.py:225
  84.6 32.1 %collective-permute-start.10 = (bf16[32,3584]{1,0:T(8,128)(2,1)}, bf16[32,3584]{1,0:T(8,128)(2,1)}, u32[]{:S(2)}, u32[]{:S(2)}) collective-permute-start(bf16[32,3584]{1,0:T(8,128)(2,1)} %collective-permute-done.8.refs_4_.refs_2_), channel_id=1, source_target_pairs={{0,1},{1,0},{2,3},{3,2},{4,5},{5,4},{6,7},{7,6},{8,9},{9,8},{10,11... | collective-permute-start | bytes 688136 | tf_op jit(solution)/shard_map/ppermute | solution.py:226
  84.7 32.1 %collective-permute-start.9 = (bf16[32,3584]{1,0:T(8,128)(2,1)}, bf16[32,3584]{1,0:T(8,128)(2,1)}, u32[]{:S(2)}, u32[]{:S(2)}) collective-permute-start(bf16[32,3584]{1,0:T(8,128)(2,1)} %collective-permute-done.4.refs_3_.refs_1_), channel_id=1, source_target_pairs={{0,1},{1,0},{2,3},{3,2},{4,5},{5,4},{6,7},{7,6},{8,9},{9,8},{10,11... | collective-permute-start | bytes 688136 | tf_op jit(solution)/shard_map/ppermute | solution.py:226
  108.7 37.8 %collective-permute-start.20 = (bf16[128,1024]{1,0:T(8,128)(2,1)S(1)}, bf16[128,1024]{1,0:T(8,128)(2,1)S(1)}, u32[]{:S(2)}, u32[]{:S(2)}) collective-permute-start(bf16[128,1024]{1,0:T(8,128)(2,1)S(1)} %shared_term.11), channel_id=1, source_target_pairs={{0,4},{4,8},{8,12},{12,14},{14,10},{10,6},{6,2},{2,0},{1,5},{5,9},... | collective-permute-start | bytes 786440 | tf_op jit(solution)/shard_map/ppermute | solution.py:224
  111.1 35.5 %collective-permute-start.23 = (bf16[128,1024]{1,0:T(8,128)(2,1)S(1)}, bf16[128,1024]{1,0:T(8,128)(2,1)S(1)}, u32[]{:S(2)}, u32[]{:S(2)}) collective-permute-start(bf16[128,1024]{1,0:T(8,128)(2,1)S(1)} %shared_term.14), channel_id=1, source_target_pairs={{4,0},{8,4},{12,8},{14,12},{10,14},{6,10},{2,6},{0,2},{5,1},{9,5},... | collective-permute-start | bytes 786440 | tf_op jit(solution)/shard_map/ppermute | solution.py:225
  150.5 13.5 %collective-permute-start.36 = (bf16[64,3584]{1,0:T(8,128)(2,1)S(1)}, bf16[64,3584]{1,0:T(8,128)(2,1)S(1)}, u32[]{:S(2)}, u32[]{:S(2)}) collective-permute-start(bf16[64,3584]{1,0:T(8,128)(2,1)S(1)} %get-tuple-element.38), channel_id=1, source_target_pairs={{0,1},{1,0},{2,3},{3,2},{4,5},{5,4},{6,7},{7,6},{8,9},{9,8},{10,11... | collective-permute-start | bytes 1376264 | tf_op jit(solution)/shard_map/ppermute | solution.py:226
  150.6 5.9 %collective-permute-start.24 = (bf16[128,512]{1,0:T(8,128)(2,1)S(1)}, bf16[128,512]{1,0:T(8,128)(2,1)S(1)}, u32[]{:S(2)}, u32[]{:S(2)}) collective-permute-start(bf16[128,512]{1,0:T(8,128)(2,1)S(1)} %shared_term.15.hidden), channel_id=1, source_target_pairs={{0,4},{4,8},{8,12},{12,14},{14,10},{10,6},{6,2},{2,0},{1,5},{5,9},... | collective-permute-start | bytes 393224 | tf_op jit(solution)/shard_map/ppermute | solution.py:224
  150.6 6.1 %collective-permute-start.28 = (bf16[128,512]{1,0:T(8,128)(2,1)S(1)}, bf16[128,512]{1,0:T(8,128)(2,1)S(1)}, u32[]{:S(2)}, u32[]{:S(2)}) collective-permute-start(bf16[128,512]{1,0:T(8,128)(2,1)S(1)} %shared_term.15.hidden), channel_id=1, source_target_pairs={{4,0},{8,4},{12,8},{14,12},{10,14},{6,10},{2,6},{0,2},{5,1},{9,5},... | collective-permute-start | bytes 393224 | tf_op jit(solution)/shard_map/ppermute | solution.py:225
  156.5 5.5 %collective-permute-start.25 = (bf16[128,512]{1,0:T(8,128)(2,1)S(1)}, bf16[128,512]{1,0:T(8,128)(2,1)S(1)}, u32[]{:S(2)}, u32[]{:S(2)}) collective-permute-start(bf16[128,512]{1,0:T(8,128)(2,1)S(1)} %collective-permute-done.24.hidden), channel_id=1, source_target_pairs={{0,4},{4,8},{8,12},{12,14},{14,10},{10,6},{6,2},{2,0},{1,5},{5,9},... | collective-permute-start | bytes 393224 | tf_op jit(solution)/shard_map/ppermute | solution.py:224
  156.7 5.5 %collective-permute-start.29 = (bf16[128,512]{1,0:T(8,128)(2,1)S(1)}, bf16[128,512]{1,0:T(8,128)(2,1)S(1)}, u32[]{:S(2)}, u32[]{:S(2)}) collective-permute-start(bf16[128,512]{1,0:T(8,128)(2,1)S(1)} %collective-permute-done.28.hidden), channel_id=1, source_target_pairs={{4,0},{8,4},{12,8},{14,12},{10,14},{6,10},{2,6},{0,2},{5,1},{9,5},... | collective-permute-start | bytes 393224 | tf_op jit(solution)/shard_map/ppermute | solution.py:225
  159.9 16.7 %collective-permute-start.35 = (bf16[64,3584]{1,0:T(8,128)(2,1)S(1)}, bf16[64,3584]{1,0:T(8,128)(2,1)S(1)}, u32[]{:S(2)}, u32[]{:S(2)}) collective-permute-start(bf16[64,3584]{1,0:T(8,128)(2,1)S(1)} %get-tuple-element.36), channel_id=1, source_target_pairs={{0,1},{1,0},{2,3},{3,2},{4,5},{5,4},{6,7},{7,6},{8,9},{9,8},{10,11... | collective-permute-start | bytes 1376264 | tf_op jit(solution)/shard_map/ppermute | solution.py:226
  161.5 16.3 %collective-permute-start.43 = (bf16[64,3584]{1,0:T(8,128)(2,1)S(1)}, bf16[64,3584]{1,0:T(8,128)(2,1)S(1)}, u32[]{:S(2)}, u32[]{:S(2)}) collective-permute-start(bf16[64,3584]{1,0:T(8,128)(2,1)S(1)} %get-tuple-element.44), channel_id=1, source_target_pairs={{0,1},{1,0},{2,3},{3,2},{4,5},{5,4},{6,7},{7,6},{8,9},{9,8},{10,11... | collective-permute-start | bytes 1376264 | tf_op jit(solution)/shard_map/ppermute | solution.py:226
  161.9 6.3 %collective-permute-start.26 = (bf16[128,512]{1,0:T(8,128)(2,1)S(1)}, bf16[128,512]{1,0:T(8,128)(2,1)S(1)}, u32[]{:S(2)}, u32[]{:S(2)}) collective-permute-start(bf16[128,512]{1,0:T(8,128)(2,1)S(1)} %collective-permute-done.25.hidden), channel_id=1, source_target_pairs={{0,4},{4,8},{8,12},{12,14},{14,10},{10,6},{6,2},{2,0},{1,5},{5,9},... | collective-permute-start | bytes 393224 | tf_op jit(solution)/shard_map/ppermute | solution.py:224
  162.2 6.3 %collective-permute-start.30 = (bf16[128,512]{1,0:T(8,128)(2,1)S(1)}, bf16[128,512]{1,0:T(8,128)(2,1)S(1)}, u32[]{:S(2)}, u32[]{:S(2)}) collective-permute-start(bf16[128,512]{1,0:T(8,128)(2,1)S(1)} %collective-permute-done.29.hidden), channel_id=1, source_target_pairs={{4,0},{8,4},{12,8},{14,12},{10,14},{6,10},{2,6},{0,2},{5,1},{9,5},... | collective-permute-start | bytes 393224 | tf_op jit(solution)/shard_map/ppermute | solution.py:225
  164.1 12.6 %collective-permute-start.37 = (bf16[32,3584]{1,0:T(8,128)(2,1)S(1)}, bf16[32,3584]{1,0:T(8,128)(2,1)S(1)}, u32[]{:S(2)}, u32[]{:S(2)}) collective-permute-start(bf16[32,3584]{1,0:T(8,128)(2,1)S(1)} %get-tuple-element.45), channel_id=1, source_target_pairs={{0,4},{4,8},{8,12},{12,14},{14,10},{10,6},{6,2},{2,0},{1,5},{5,9},... | collective-permute-start | bytes 688136 | tf_op jit(solution)/shard_map/ppermute | solution.py:224
  168.3 6.3 %collective-permute-start.27 = (bf16[64,512]{1,0:T(8,128)(2,1)S(1)}, bf16[64,512]{1,0:T(8,128)(2,1)S(1)}, u32[]{:S(2)}, u32[]{:S(2)}) collective-permute-start(bf16[64,512]{1,0:T(8,128)(2,1)S(1)} %slice.42), channel_id=1, source_target_pairs={{0,4},{4,8},{8,12},{12,14},{14,10},{10,6},{6,2},{2,0},{1,5},{5,9},... | collective-permute-start | bytes 196616 | tf_op jit(solution)/shard_map/ppermute | solution.py:224
  168.6 6.1 %collective-permute-start.31 = (bf16[64,512]{1,0:T(8,128)(2,1)S(1)}, bf16[64,512]{1,0:T(8,128)(2,1)S(1)}, u32[]{:S(2)}, u32[]{:S(2)}) collective-permute-start(bf16[64,512]{1,0:T(8,128)(2,1)S(1)} %slice.43), channel_id=1, source_target_pairs={{4,0},{8,4},{12,8},{14,12},{10,14},{6,10},{2,6},{0,2},{5,1},{9,5},... | collective-permute-start | bytes 196616 | tf_op jit(solution)/shard_map/ppermute | solution.py:225
  174.6 10.6 %collective-permute-start.34 = (bf16[64,3584]{1,0:T(8,128)(2,1)S(1)}, bf16[64,3584]{1,0:T(8,128)(2,1)S(1)}, u32[]{:S(2)}, u32[]{:S(2)}) collective-permute-start(bf16[64,3584]{1,0:T(8,128)(2,1)S(1)} %get-tuple-element.33), channel_id=1, source_target_pairs={{0,1},{1,0},{2,3},{3,2},{4,5},{5,4},{6,7},{7,6},{8,9},{9,8},{10,11... | collective-permute-start | bytes 1376264 | tf_op jit(solution)/shard_map/ppermute | solution.py:226
  174.7 23.2 %collective-permute-start.42 = (bf16[64,3584]{1,0:T(8,128)(2,1)S(1)}, bf16[64,3584]{1,0:T(8,128)(2,1)S(1)}, u32[]{:S(2)}, u32[]{:S(2)}) collective-permute-start(bf16[64,3584]{1,0:T(8,128)(2,1)S(1)} %get-tuple-element.42), channel_id=1, source_target_pairs={{0,1},{1,0},{2,3},{3,2},{4,5},{5,4},{6,7},{7,6},{8,9},{9,8},{10,11... | collective-permute-start | bytes 1376264 | tf_op jit(solution)/shard_map/ppermute | solution.py:226
  176.6 32.5 %collective-permute-start.33 = (bf16[64,3584]{1,0:T(8,128)(2,1)S(1)}, bf16[64,3584]{1,0:T(8,128)(2,1)S(1)}, u32[]{:S(2)}, u32[]{:S(2)}) collective-permute-start(bf16[64,3584]{1,0:T(8,128)(2,1)S(1)} %get-tuple-element.30), channel_id=1, source_target_pairs={{0,1},{1,0},{2,3},{3,2},{4,5},{5,4},{6,7},{7,6},{8,9},{9,8},{10,11... | collective-permute-start | bytes 1376264 | tf_op jit(solution)/shard_map/ppermute | solution.py:226
  176.8 7.9 %collective-permute-start.44 = (bf16[32,3584]{1,0:T(8,128)(2,1)S(1)}, bf16[32,3584]{1,0:T(8,128)(2,1)S(1)}, u32[]{:S(2)}, u32[]{:S(2)}) collective-permute-start(bf16[32,3584]{1,0:T(8,128)(2,1)S(1)} %get-tuple-element.46), channel_id=1, source_target_pairs={{4,0},{8,4},{12,8},{14,12},{10,14},{6,10},{2,6},{0,2},{5,1},{9,5},... | collective-permute-start | bytes 688136 | tf_op jit(solution)/shard_map/ppermute | solution.py:225
  177.8 32.6 %collective-permute-start.41 = (bf16[64,3584]{1,0:T(8,128)(2,1)S(1)}, bf16[64,3584]{1,0:T(8,128)(2,1)S(1)}, u32[]{:S(2)}, u32[]{:S(2)}) collective-permute-start(bf16[64,3584]{1,0:T(8,128)(2,1)S(1)} %get-tuple-element.40), channel_id=1, source_target_pairs={{0,1},{1,0},{2,3},{3,2},{4,5},{5,4},{6,7},{7,6},{8,9},{9,8},{10,11... | collective-permute-start | bytes 1376264 | tf_op jit(solution)/shard_map/ppermute | solution.py:226
  184.7 12.1 %collective-permute-start.38 = (bf16[64,3584]{1,0:T(8,128)(2,1)S(1)}, bf16[64,3584]{1,0:T(8,128)(2,1)S(1)}, u32[]{:S(2)}, u32[]{:S(2)}) collective-permute-start(bf16[64,3584]{1,0:T(8,128)(2,1)S(1)} %add_convert_fusion.6), channel_id=1, source_target_pairs={{0,4},{4,8},{8,12},{12,14},{14,10},{10,6},{6,2},{2,0},{1,5},{5,9},... | collective-permute-start | bytes 1376264 | tf_op jit(solution)/shard_map/ppermute | solution.py:224
  185.2 34.6 %collective-permute-start.32 = (bf16[64,3584]{1,0:T(8,128)(2,1)S(1)}, bf16[64,3584]{1,0:T(8,128)(2,1)S(1)}, u32[]{:S(2)}, u32[]{:S(2)}) collective-permute-start(bf16[64,3584]{1,0:T(8,128)(2,1)S(1)} %get-tuple-element.27), channel_id=1, source_target_pairs={{0,1},{1,0},{2,3},{3,2},{4,5},{5,4},{6,7},{7,6},{8,9},{9,8},{10,11... | collective-permute-start | bytes 1376264 | tf_op jit(solution)/shard_map/ppermute | solution.py:226
  196.8 11.2 %collective-permute-start.45 = (bf16[64,3584]{1,0:T(8,128)(2,1)S(1)}, bf16[64,3584]{1,0:T(8,128)(2,1)S(1)}, u32[]{:S(2)}, u32[]{:S(2)}) collective-permute-start(bf16[64,3584]{1,0:T(8,128)(2,1)S(1)} %add_convert_fusion.3), channel_id=1, source_target_pairs={{4,0},{8,4},{12,8},{14,12},{10,14},{6,10},{2,6},{0,2},{5,1},{9,5},... | collective-permute-start | bytes 1376264 | tf_op jit(solution)/shard_map/ppermute | solution.py:225
  197.9 11.2 %collective-permute-start.39 = (bf16[64,3584]{1,0:T(8,128)(2,1)S(1)}, bf16[64,3584]{1,0:T(8,128)(2,1)S(1)}, u32[]{:S(2)}, u32[]{:S(2)}) collective-permute-start(bf16[64,3584]{1,0:T(8,128)(2,1)S(1)} %add_convert_fusion.5), channel_id=1, source_target_pairs={{0,4},{4,8},{8,12},{12,14},{14,10},{10,6},{6,2},{2,0},{1,5},{5,9},... | collective-permute-start | bytes 1376264 | tf_op jit(solution)/shard_map/ppermute | solution.py:224
  208.1 10.5 %collective-permute-start.46 = (bf16[64,3584]{1,0:T(8,128)(2,1)S(1)}, bf16[64,3584]{1,0:T(8,128)(2,1)S(1)}, u32[]{:S(2)}, u32[]{:S(2)}) collective-permute-start(bf16[64,3584]{1,0:T(8,128)(2,1)S(1)} %add_convert_fusion.2), channel_id=1, source_target_pairs={{4,0},{8,4},{12,8},{14,12},{10,14},{6,10},{2,6},{0,2},{5,1},{9,5},... | collective-permute-start | bytes 1376264 | tf_op jit(solution)/shard_map/ppermute | solution.py:225
  209.3 10.5 %collective-permute-start.40 = (bf16[64,3584]{1,0:T(8,128)(2,1)S(1)}, bf16[64,3584]{1,0:T(8,128)(2,1)S(1)}, u32[]{:S(2)}, u32[]{:S(2)}) collective-permute-start(bf16[64,3584]{1,0:T(8,128)(2,1)S(1)} %add_convert_fusion.4), channel_id=1, source_target_pairs={{0,4},{4,8},{8,12},{12,14},{14,10},{10,6},{6,2},{2,0},{1,5},{5,9},... | collective-permute-start | bytes 1376264 | tf_op jit(solution)/shard_map/ppermute | solution.py:224
  218.8 9.4 %collective-permute-start.47 = (bf16[64,3584]{1,0:T(8,128)(2,1)S(1)}, bf16[64,3584]{1,0:T(8,128)(2,1)S(1)}, u32[]{:S(2)}, u32[]{:S(2)}) collective-permute-start(bf16[64,3584]{1,0:T(8,128)(2,1)S(1)} %add_convert_fusion.1), channel_id=1, source_target_pairs={{4,0},{8,4},{12,8},{14,12},{10,14},{6,10},{2,6},{0,2},{5,1},{9,5},... | collective-permute-start | bytes 1376264 | tf_op jit(solution)/shard_map/ppermute | solution.py:225
  (26 other events, 188.6 us)

commit v2 on v0

v2 whole, which is shorter than its diff:
```python
import functools

import jax
import jax.numpy as jnp
from jax import lax
from jax.experimental import pallas as pl
from jax.experimental.pallas import tpu as pltpu
from jax.sharding import PartitionSpec as P

MOST = 18
LANES = 128
MIB = 1 << 20
BF16 = jnp.bfloat16
F32 = jnp.float32


def cost(moved=3 * 10**6):
    return pl.CostEstimate(flops=1000, bytes_accessed=moved, transcendentals=0)


def params(mib):
    return pltpu.CompilerParams(vmem_limit_bytes=mib * MIB)


def column_tiles(total, width=512):
    return [(at, min(width, total - at)) for at in range(0, total, width)]


def silu(value):
    return value * (1.0 / (1.0 + jnp.exp(-value)))


def whole(array):
    return pl.BlockSpec(array.shape, lambda i: (0,) * array.ndim)


def pick_kernel(count, experts, top, cut, first, *refs):
    tokens, out, spread = refs[:count], refs[count], refs[count + 1]
    if cut:
        tokens = [
            r if i % 2 and count == 4 else r.at[:cut] if cut > 0 else r.at[-cut:]
            for i, r in enumerate(tokens)
        ]
    features = out.shape[2]
    height, slots = spread.shape
    notes = jnp.concatenate([t[:, features - LANES :] for t in tokens], axis=0).astype(F32)
    lane = lax.broadcasted_iota(jnp.int32, notes.shape, 1)
    named = jnp.zeros(notes.shape, F32)
    for e in range(experts):
        same = (notes == (first[0] + e).astype(F32)) & (lane < top)
        hit = jnp.max(jnp.where(same, 1.0, 0.0), axis=1, keepdims=True)
        named = jnp.where(lane == e, hit, named)
    down = lax.broadcasted_iota(jnp.int32, (height, height), 0)
    across = lax.broadcasted_iota(jnp.int32, (height, height), 1)
    upto = jnp.where(across <= down, 1.0, 0.0).astype(BF16)
    rank = jnp.dot(upto, named.astype(BF16), preferred_element_type=F32).astype(jnp.int32) - 1
    slot = jnp.where(named > 0.0, rank + lane * (slots // experts), -1)
    turned = jnp.transpose(slot.astype(F32)).astype(jnp.int32)
    number = lax.broadcasted_iota(jnp.int32, (slots, height), 0)
    column = lax.broadcasted_iota(jnp.int32, (height, slots), 1)
    picks = number == turned[0:1, :]
    back = column == slot[:, 0:1]
    for e in range(1, experts):
        picks = picks | (number == turned[e : e + 1, :])
        back = back | (column == slot[:, e : e + 1])
    picks = jnp.where(picks, 1.0, 0.0).astype(BF16)
    spread[...] = jnp.where(back, 1.0, 0.0).astype(BF16)
    for at, width in column_tiles(features):
        piece = jnp.concatenate([t[:, at : at + width] for t in tokens], axis=0)
        rows = jnp.dot(picks, piece, preferred_element_type=F32).astype(BF16)
        out[:, :, at : at + width] = rows.reshape(experts, slots // experts, width)


def pick_rows(first, tokens, experts, slots, top, cut):
    height = sum(t.shape[0] for t in tokens)
    if cut > 0:
        height += sum(cut - t.shape[0] for t in tokens[::2])
    if cut < 0:
        height += cut * len(tokens)
    features = tokens[0].shape[1]
    vmem = pl.BlockSpec(memory_space=pltpu.VMEM)
    return pl.pallas_call(
        functools.partial(pick_kernel, len(tokens), experts, top, cut),
        out_shape=[
            jax.ShapeDtypeStruct((experts, slots, features), BF16),
            jax.ShapeDtypeStruct((height, experts * slots), BF16),
        ],
        in_specs=[pl.BlockSpec(memory_space=pltpu.SMEM)] + [vmem] * len(tokens),
        out_specs=[vmem, vmem],
        compiler_params=params(16),
        cost_estimate=cost(),
        name="pick_rows",
    )(first, *tokens)


def expert_kernel(count, top, first, *refs):
    rows_in, (gate, up, down) = refs[:count], refs[count : count + 3]
    rows_out, rows = refs[count + 3 : 2 * count + 3], refs[2 * count + 3]
    slots, wide = rows_in[0].shape[1:]
    features = down.shape[2]
    for i, r in enumerate(rows_in):
        rows[i * slots : (i + 1) * slots, :] = r[0]
    notes = rows[:, features:].astype(F32)
    lane = lax.broadcasted_iota(jnp.int32, notes.shape, 1)
    expert = (first[0] + pl.program_id(0)).astype(F32)
    chosen = jnp.where((notes == expert) & (lane < top), 1.0, 0.0)
    scale = jnp.zeros((notes.shape[0], 1), F32)
    for part in (1, 2, 3):
        moved = jnp.concatenate([notes[:, part * top :], notes[:, : part * top]], axis=1)
        scale = scale + jnp.sum(chosen * moved, axis=1, keepdims=True)
    value = rows[:, :features]
    gated = jnp.dot(value, gate[0], preferred_element_type=F32)
    upward = jnp.dot(value, up[0], preferred_element_type=F32)
    hidden = (silu(gated) * upward * scale).astype(BF16)
    for at, width in column_tiles(features):
        done = jnp.dot(hidden, down[0, :, at : at + width], preferred_element_type=F32)
        done = done.astype(BF16)
        for i, r in enumerate(rows_out):
            r[0, :, at : at + width] = done[i * slots : (i + 1) * slots]


def run_experts(first, rows, gate, up, down, top):
    experts, slots, wide = rows[0].shape
    features, hidden = gate.shape[1:]
    count = len(rows)
    height = count * slots
    return pl.pallas_call(
        functools.partial(expert_kernel, count, top),
        out_shape=[jax.ShapeDtypeStruct((experts, slots, features), BF16)] * count,
        grid=(experts,),
        in_specs=[pl.BlockSpec(memory_space=pltpu.SMEM)]
        + [pl.BlockSpec((1, slots, wide), lambda e: (e, 0, 0))] * count
        + [
            pl.BlockSpec((1, features, hidden), lambda e: (e, 0, 0)),
            pl.BlockSpec((1, features, hidden), lambda e: (e, 0, 0)),
            pl.BlockSpec((1, hidden, features), lambda e: (e, 0, 0)),
        ],
        out_specs=[pl.BlockSpec((1, slots, features), lambda e: (e, 0, 0))] * count,
        scratch_shapes=[pltpu.VMEM((height, wide), BF16)],
        compiler_params=params(38),
        cost_estimate=cost(7 * 10**7),
        name="run_experts",
    )(first, *rows, gate, up, down)


def first_kernel(shifts, start, shift, tokens, ids, gates, *refs):
    parts, (weight, down), sends = refs[:6], refs[6:8], refs[8:]
    height, width = parts[0].shape
    depth = parts[4].shape[1]
    gap = weight.shape[0] - height
    for s in shifts:

        @pl.when(shift[0] == s)
        def _():
            for i in range(4):
                here = slice(i * width, (i + 1) * width)
                if s:
                    weight[:s, here] = jnp.zeros((s, width), BF16)
                weight[s : s + height, here] = parts[i][...]
                if s < gap:
                    weight[s + height :, here] = jnp.zeros((gap - s, width), BF16)
            for i in range(2):
                here = slice(i * depth, (i + 1) * depth)
                if s:
                    down[:s, here] = jnp.zeros((s, depth), BF16)
                down[s : s + height, here] = parts[4 + i][...]
                if s < gap:
                    down[s + height :, here] = jnp.zeros((gap - s, depth), BF16)

    rows, features = tokens.shape
    gate = gates[...]
    high = gate.astype(BF16).astype(F32)
    middle = (gate - high).astype(BF16).astype(F32)
    low = gate - high - middle
    notes = [ids[...].astype(F32), high, middle, low]
    notes.append(jnp.zeros((LANES - 4 * ids.shape[0], rows), F32))
    notes = jnp.transpose(jnp.concatenate(notes, axis=0)).astype(BF16)
    window = pl.ds(pl.multiple_of(start[0], LANES), weight.shape[0])
    value = jnp.dot(tokens[:, window], weight[...], preferred_element_type=F32).astype(BF16)
    split = rows // 2
    wide = features + LANES
    for i, out in enumerate(sends):
        here = slice(i % 2 * split, (i % 2 + 1) * split) if i < 4 else slice(0, rows)
        out[:, :features] = tokens[here, :]
        out[:, features:wide] = notes[here]
        if i < 2:
            out[:, wide:] = value[here]


def first_step(start, shift, shifts, tokens, ids, gates, weights, width):
    rows, features = tokens.shape
    split, wide = rows // 2, features + LANES
    inner = weights[0].shape[1]
    outs = [(width, 4 * inner), (width, 2 * inner)]
    outs += [(split, wide + 4 * inner)] * 2 + [(split, wide)] * 2 + [(rows, wide)]
    outs = [jax.ShapeDtypeStruct(shape, BF16) for shape in outs]
    smem = pl.BlockSpec(memory_space=pltpu.SMEM)
    arrays = [tokens, ids, gates, *weights]
    return pl.pallas_call(
        functools.partial(first_kernel, shifts),
        out_shape=outs,
        grid=(1,),
        in_specs=[smem, smem] + [whole(a) for a in arrays],
        out_specs=[whole(o) for o in outs],
        compiler_params=params(60),
        cost_estimate=cost(),
        name="first_step",
    )(start, shift, *arrays)


def step_kernel(wide, sends, start, weight, on, back, *refs):
    others, outs = (refs[:-3], refs[-3:]) if len(refs) > 2 else ((), refs)
    height = on.shape[0]
    window = pl.ds(pl.multiple_of(start[0], LANES), weight.shape[0])
    piece = jnp.concatenate([on[:, window], back[:, window]], axis=0)
    value = jnp.dot(piece, weight[...], preferred_element_type=F32)
    for i, arrived in enumerate((on, back)):
        part = value[i * height : (i + 1) * height]
        if arrived.shape[1] > wide:
            part = part + arrived[:, wide:].astype(F32)
        if sends[i]:
            outs[i][:, :wide] = arrived[:, :wide]
            outs[i][:, wide:] = part.astype(BF16)
        else:
            outs[i][...] = part.astype(BF16)
    if others:
        at = 0
        for r in (*others, on, back):
            outs[2][at : at + r.shape[0], :] = r[:, :wide]
            at += r.shape[0]


def step_on(start, weight, on, back, wide, sends, others=()):
    height, width = on.shape[0], weight.shape[1]
    vmem = pl.BlockSpec(memory_space=pltpu.VMEM)
    shapes = [(height, wide + width) if full else (height, width) for full in sends]
    if others:
        shapes.append((sum(o.shape[0] for o in others) + 2 * height, wide))
    return pl.pallas_call(
        functools.partial(step_kernel, wide, sends),
        out_shape=[jax.ShapeDtypeStruct(shape, BF16) for shape in shapes],
        in_specs=[pl.BlockSpec(memory_space=pltpu.SMEM)] + [vmem] * (3 + len(others)),
        out_specs=[vmem] * len(shapes),
        compiler_params=params(16),
        cost_estimate=cost(),
        name="step_on",
    )(start, weight, on, back, *others)


def last_kernel(wide, start, weight, main, side, *refs):
    others, (units, *tokens) = (refs[:1], refs[1:]) if len(refs) == 3 else ((), refs)
    height = main.shape[0]
    window = pl.ds(pl.multiple_of(start[0], LANES), weight.shape[0])
    value = jnp.dot(main[:, window], weight[...], preferred_element_type=F32)
    value = value + main[:, wide:].astype(F32) + side[...].astype(F32)
    half = value.shape[1] // 2
    units[...] = (silu(value[:, :half]) * value[:, half:]).astype(BF16)
    if others:
        for i, r in enumerate((*others, main)):
            tokens[0][i * height : (i + 1) * height, :] = r[:, :wide]


def last_step(start, weight, main, side, wide, others=()):
    height = main.shape[0]
    vmem = pl.BlockSpec(memory_space=pltpu.VMEM)
    return pl.pallas_call(
        functools.partial(last_kernel, wide),
        out_shape=[jax.ShapeDtypeStruct((height, weight.shape[1] // 2), BF16)]
        + [jax.ShapeDtypeStruct((2 * height, wide), BF16)] * len(others),
        in_specs=[pl.BlockSpec(memory_space=pltpu.SMEM)] + [vmem] * (3 + len(others)),
        out_specs=[vmem] * (1 + len(others)),
        compiler_params=params(16),
        cost_estimate=cost(),
        name="last_step",
    )(start, weight, main, side, *others)


def merge_kernel(count, *refs):
    spreads, rows, owns = refs[:count], refs[count : 2 * count], refs[2 * count : 3 * count]
    other = refs[3 * count]
    for i in range(count):
        height, features = owns[i].shape
        which = spreads[i][...]
        for at, width in column_tiles(features):
            value = jnp.concatenate(
                [rows[i][e, :, at : at + width] for e in range(rows[i].shape[0])], axis=0
            )
            value = jnp.dot(which, value, preferred_element_type=F32)
            owns[i][:, at : at + width] = value[:height]
            other[i * height : (i + 1) * height, at : at + width] = value[height:].astype(BF16)


def merge_rows(spreads, rows):
    height, features = spreads[0].shape[0] // 2, rows[0].shape[2]
    count = len(rows)
    outs = [jax.ShapeDtypeStruct((height, features), F32)] * count
    outs.append(jax.ShapeDtypeStruct((count * height, features), BF16))
    arrays = [*spreads, *rows]
    return pl.pallas_call(
        functools.partial(merge_kernel, count),
        out_shape=outs,
        grid=(1,),
        in_specs=[whole(a) for a in arrays],
        out_specs=[whole(o) for o in outs],
        compiler_params=params(36),
        cost_estimate=cost(),
        name="merge_rows",
    )(*arrays)


def add_kernel(places, base, counts, joined, start, own, other, down, *refs):
    arrived, outs, total = refs[: sum(counts)], refs[sum(counts) : -1], refs[-1]
    features = own.shape[1]
    height = total.shape[0] // len(places)
    window = pl.ds(pl.multiple_of(start[0], LANES), down.shape[0])
    units = []
    for i, at in enumerate(places):
        mine = arrived[sum(counts[:i]) : sum(counts[: i + 1])]
        here = slice(i * height, (i + 1) * height)
        value = other[base + at : base + at + height, :].astype(F32)
        value = value + own[at : at + height, :]
        for a in mine:
            if a.shape[1] > features:
                value = value + a[:, :features].astype(F32)
        total[here, :] = value
        wide = mine[0].shape[1]
        units.append(mine[0][:, features:] if wide > features else mine[0][...])
    value = lax.dot_general(
        jnp.concatenate(units, axis=0),
        down[...],
        (((1,), (1,)), ((), ())),
        preferred_element_type=F32,
    )
    total[:, window] = total[:, window] + value
    if joined:
        outs[0][...] = total[...].astype(BF16)
    else:
        for i, out in enumerate(outs):
            out[:, :features] = total[i * height : (i + 1) * height, :].astype(BF16)
            out[:, features:] = units[i]


def add_step(start, term, down, places, arrived, joined=False):
    own, other, base = term
    features = own.shape[1]
    counts = [len(a) for a in arrived]
    height = arrived[0][0].shape[0]
    count = len(places)
    vmem = pl.BlockSpec(memory_space=pltpu.VMEM)
    if joined:
        outs = [jax.ShapeDtypeStruct((count * height, features), BF16)]
    else:
        shape = (height, features + down.shape[1])
        outs = [jax.ShapeDtypeStruct(shape, BF16)] * count
    return pl.pallas_call(
        functools.partial(add_kernel, places, base, counts, joined),
        out_shape=outs,
        in_specs=[pl.BlockSpec(memory_space=pltpu.SMEM)] + [vmem] * (3 + sum(counts)),
        out_specs=[vmem] * len(outs),
        scratch_shapes=[pltpu.VMEM((count * height, features), F32)],
        compiler_params=params(16),
        cost_estimate=cost(),
        name="add_step",
    )(start, own, other, down, *[a for b in arrived for a in b])


def window_width(count, size, total):
    need = max((i * size) % LANES + size for i in range(count))
    return min(total, -(-need // LANES) * LANES)


def on_device(
    tokens,
    route_ids,
    route_gates,
    expert_gate,
    expert_up,
    expert_down,
    shared_gate,
    shared_up,
    shared_down,
):
    n = lax.axis_size("expert")
    half = n // 2
    me = lax.axis_index("expert")
    row_count, features = tokens.shape
    top = route_ids.shape[1]
    experts = expert_gate.shape[0]
    slots = -(-4 * MOST // 16) * 16

    path = list(range(0, n, 2)) + list(range(n - 1, 0, -2))
    onward = [(path[i], path[(i + 1) % n]) for i in range(n)]
    backward = [(b, a) for a, b in onward]
    send_on = lambda a: lax.ppermute(a, "expert", onward)
    send_back = lambda a: lax.ppermute(a, "expert", backward)
    swap = lambda a: lax.ppermute(a, "tensor", [(0, 1), (1, 0)])

    first = (me * experts).reshape(1)

    size = shared_gate.shape[0]
    width = window_width(n, size, features)
    start = jnp.minimum(me * size // LANES * LANES, features - width)
    shift = (me * size - start).reshape(1)
    start = start.reshape(1)
    shifts = {i * size - min(i * size // LANES * LANES, features - width) for i in range(n)}
    weights = [f for w in (shared_gate, shared_up, shared_down.T) for f in (w, swap(w))]
    both, down, *sends = first_step(
        start, shift, sorted(shifts), tokens, route_ids.T, route_gates.T, weights, width
    )

    after = lambda x, y: lax.optimization_barrier((x, y))[0]
    split = row_count // 2
    tokens = sends[4]
    wide = tokens.shape[1]
    ahead, behind = [send_on(p) for p in sends[:2]], [send_back(p) for p in sends[2:4]]
    pick = lambda arrays, cut=0: pick_rows(first, arrays, experts, slots, top, cut)
    pairs, picked = {}, {}
    done = tokens
    for k in range(1, half):
        others = []
        for stream in (0, 1):
            full = (k < half - 1 or stream == 0, k < half - 1 or stream == 1)
            on, back = ahead[stream], behind[stream]
            if stream and k == 1:
                others = [tokens] + others
            sends = step_on(start, after(both, done), on, back, wide, full, others)
            done = sends[0]
            ahead[stream], behind[stream] = send_on(sends[0]), send_back(sends[1])
            others = [on, back]
            if stream == 0 and k > 1:
                picked[k - 1] = pick([after(pairs[k - 1][0], done), pairs[k - 1][1]], -row_count if k == 2 else 0)
                done = picked[k - 1][1]
        pairs[k] = [sends[2], swap(sends[2])]
    main = [ahead[0], behind[1]]
    [upper] = last_step(start, after(both, done), main[0], behind[0], wide)
    k = half - 1
    picked[k] = pick([after(pairs[k][0], upper), pairs[k][1]])
    done = picked[k][1]
    lower, end = last_step(start, after(both, done), main[1], ahead[1], wide, main[:1])
    units = upper, lower
    picked[0] = pick([pairs[1][0], end, pairs[1][1], swap(end)], row_count)

    lag = send_on(units[1]), send_back(units[0])
    routed = {}
    for at in range(0, half, 4):
        group = list(range(at, min(at + 4, half)))
        rows = [picked[j][0] for j in group]
        weights = expert_gate, expert_up, expert_down
        routed.update(zip(group, run_experts(first, rows, *weights, top)))

    def terms_of(chunks, done):
        spreads = [picked[c][1] for c in chunks]
        spreads[0] = after(spreads[0], done)
        *owns, other = merge_rows(spreads, [routed[c] for c in chunks])
        other = swap(other)
        return {c: (own, other, i * block) for i, (c, own) in enumerate(zip(chunks, owns))}

    block = 2 * row_count
    terms = terms_of([0, half - 1], lag)
    lead = add_step(
        start, terms[0], down, (row_count, row_count + split), [[units[0]], [units[1]]]
    )
    done = lead[0]
    lead = send_on(lead[0]), send_back(lead[1])
    for k in range(half - 1, 0, -1):
        lag = add_step(start, terms[k], after(down, done), (3 * split, 0), [[lag[0]], [lag[1]]])
        done = lag[0]
        lag = send_on(lag[0]), send_back(lag[1])
        if k > 1 and k - 1 not in terms:
            terms.update(terms_of([k - 1, k - 2] if k > 2 else [k - 1], done))
            done = terms[k - 1][1]
        lead = add_step(
            start, terms[k], after(down, done), (split, 2 * split), [[lead[0]], [lead[1]]]
        )
        done = lead[0]
        lead = send_on(lead[0]), send_back(lead[1])
    arrived = [[lead[0], lag[1]], [lag[0], lead[1]]]
    return add_step(start, terms[0], after(down, done), (0, split), arrived, joined=True)[0]


def solution(mesh):
    in_specs = (
        P(("group", "expert", "tensor"), None),
        P(("group", "expert", "tensor"), None),
        P(("group", "expert", "tensor"), None),
        P("expert", None, "tensor"),
        P("expert", None, "tensor"),
        P("expert", "tensor", None),
        P("expert", "tensor"),
        P("expert", "tensor"),
        P("tensor", "expert"),
    )
    out_specs = P(("group", "expert", "tensor"), None)
    return jax.shard_map(
        on_device, mesh=mesh, in_specs=in_specs, out_specs=out_specs, check_vma=False
    )
```

time: 649 us -> 177 us (0.27); the launches traced: 641 us -> 177 us
  waiting for transfers between devices: 430 us -> 87.1 us
  matrix products: 119 us -> 0 us
  Pallas kernels: 0 us -> 50.1 us
  local copies, waits for them, and re-layouts: 46 us -> 3.8 us
  starting transfers between devices: 19.5 us -> 35.2 us
  between operations: 15.8 us -> 0.27 us
  other arithmetic: 8.48 us -> 0 us
    all_gather x3 -> x0, waiting for transfers between devices: 212 us -> none  [the longest x1 98.1 us: on_device(): lax.all_gather(shared_up, 'expert', axis=0, tiled=True)]
    all_to_all x3 -> x0, waiting for transfers between devices: 148 us -> none  [the longest x1 148 us: on_device(): lax.all_to_all(wide_rows, ('expert', 'tensor'), split_axis=0, concat_axis...]
    dot_general x10 -> x0, matrix products: 119 us -> none  [the longest x4 74.5 us: expert_partial(): jnp.dot(hidden, expert_down[which], preferred_element_type=jnp.float32)]
    ppermute x0 -> x41, waiting for transfers between devices: none -> 87.1 us  [the longest x16 41.6 us: on_device(): send_on = lambda a: lax.ppermute(a, 'expert', onward)]
    unnamed x6 -> x0, waiting for transfers between devices: 69.4 us -> none
    pallas_call x0 -> x24, Pallas kernels: none -> 50.1 us  [the longest x1 20.4 us: run_experts(): pl.pallas_call(functools.partial(expert_kernel, count, top), out_shape=[j...]
    ppermute x0 -> x41, starting transfers between devices: none -> 35.2 us  [the longest x16 27 us: on_device(): send_on = lambda a: lax.ppermute(a, 'expert', onward)]
    scatter x2 -> x0, local copies, waits for them, and re-layouts: 21.1 us -> none  [the longest x1 18.6 us: on_device(): send_rows = jnp.zeros((index_count * capacity, feature_count), jnp.bfloat...]
  transfers between devices with their start and end apart: 8 -> 41, of which waited for: 5 -> 29; matrix products, arithmetic and copies ran while one was open for 8% -> 0% of each run, Pallas kernels for 0% -> 8%
where the time goes in v2:
time: 177 us
  waiting for transfers between devices  87.1 us (49%)
  Pallas kernels  50.1 us (28%)
  starting transfers between devices  35.2 us (20%)
  local copies, waits for them, and re-layouts  3.8 us (2%)
    ppermute x16, waiting for transfers between devices, on_device(): send_on = lambda a: lax.ppermute(a, 'expert', onward)  41.6 us
    ppermute x16, waiting for transfers between devices, on_device(): send_back = lambda a: lax.ppermute(a, 'expert', backward)  39.2 us
    ppermute x16, starting transfers between devices, on_device(): send_on = lambda a: lax.ppermute(a, 'expert', onward)  27 us
    pallas_call x1, Pallas kernels, run_experts(): pl.pallas_call(functools.partial(expert_kernel, count, top), out_shape=[j...  20.4 us
    pallas_call x4, Pallas kernels, pick_rows(): pl.pallas_call(functools.partial(pick_kernel, len(tokens), experts, top,...  8.06 us
    pallas_call x6, Pallas kernels, step_on(): pl.pallas_call(functools.partial(step_kernel, wide, sends), out_shape=[ja...  7.18 us
    ppermute x16, starting transfers between devices, on_device(): send_back = lambda a: lax.ppermute(a, 'expert', backward)  6.82 us
    ppermute x9, waiting for transfers between devices, on_device(): swap = lambda a: lax.ppermute(a, 'tensor', [(0, 1), (1, 0)])  6.23 us
  transfers between devices with their start and end apart: 41, of which 29 were waited for; matrix products, arithmetic and copies ran while one was open for 0% of the time, Pallas kernels for 8%

profile of v2, /device:TPU:0, one launch (start us, length us, event | category | flops | bytes accessed | tf_op | source)
XLA Modules:
  0.0 176.5 jit_solution(801626329048796664)
XLA Ops:
  4.2 4.3 %first_step.1 = (bf16[512,2048]{1,0:T(8,128)(2,1)}, bf16[512,1024]{1,0:T(8,128)(2,1)}, bf16[32,5760]{1,0:T(8,128)(2,1)}, bf16[32,5760]{1,0:T(8,128)(2,1)}, bf16[...) custom-call(s32[1]{0:T(128)} %bitcast.start, s32[1]{0:T(128)} %bitcast.2.shift, ...), custom_call_target="tpu_custom_call" | custom-call | flops 1000 | bytes 3000000 | tf_op jit(solution)/shard_map/first_step/pallas_call | solution.py:199
  8.5 2.9 %collective-permute-start.3 = (bf16[32,5760]{1,0:T(8,128)(2,1)}, bf16[32,5760]{1,0:T(8,128)(2,1)S(1)}, u32[]{:S(2)}, u32[]{:S(2)}) collective-permute-start(bf16[32,5760]{1,0:T(8,128)(2,1)} %get-tuple-element.84), channel_id=1, source_target_pairs={{0,4},{4,8},{8,12},{12,14},{14,10},{10,6},{6,2},{2,0},{1,5},{5,9},... | collective-permute-start | bytes 1105928 | tf_op jit(solution)/shard_map/ppermute | solution.py:394
  11.4 1.6 collective-permute-start.5
  13.5 8.4 %collective-permute-done.4.back.refs_2_ = bf16[32,3712]{1,0:T(8,128)(2,1)S(1)} collective-permute-done((bf16[32,3712]{1,0:T(8,128)(2,1)}, bf16[32,3712]{1,0:T(8,128)(2,1)S(1)}, u32[]{:S(2)}, u32[]{:S(2)}) %collective-permute-start.4) | collective-permute-done | bytes 237600 | tf_op jit(solution)/shard_map/ppermute | solution.py:395
  21.9 1.6 copy-done
  25.6 2.8 %collective-permute-done.5.on = bf16[32,5760]{1,0:T(8,128)(2,1)S(1)} collective-permute-done((bf16[32,5760]{1,0:T(8,128)(2,1)}, bf16[32,5760]{1,0:T(8,128)(2,1)S(1)}, u32[]{:S(2)}, u32[]{:S(2)}) %collective-permute-start.5) | collective-permute-done | bytes 368672 | tf_op jit(solution)/shard_map/ppermute | solution.py:394
  29.7 1.8 %collective-permute-start.7 = (bf16[32,5760]{1,0:T(8,128)(2,1)}, bf16[32,5760]{1,0:T(8,128)(2,1)}, u32[]{:S(2)}, u32[]{:S(2)}) collective-permute-start(bf16[32,5760]{1,0:T(8,128)(2,1)} %get-tuple-element.86), channel_id=1, source_target_pairs={{0,4},{4,8},{8,12},{12,14},{14,10},{10,6},{6,2},{2,0},{1,5},{5,9},... | collective-permute-start | bytes 1105928 | tf_op jit(solution)/shard_map/ppermute | solution.py:394
  31.8 1.8 %collective-permute-start.10 = (bf16[32,5760]{1,0:T(8,128)(2,1)}, bf16[32,5760]{1,0:T(8,128)(2,1)}, u32[]{:S(2)}, u32[]{:S(2)}) collective-permute-start(bf16[32,5760]{1,0:T(8,128)(2,1)} %get-tuple-element.91), channel_id=1, source_target_pairs={{0,4},{4,8},{8,12},{12,14},{14,10},{10,6},{6,2},{2,0},{1,5},{5,9},... | collective-permute-start | bytes 1105928 | tf_op jit(solution)/shard_map/ppermute | solution.py:394
  33.8 7.6 %collective-permute-done.7.on.refs_0_ = bf16[32,5760]{1,0:T(8,128)(2,1)} collective-permute-done((bf16[32,5760]{1,0:T(8,128)(2,1)}, bf16[32,5760]{1,0:T(8,128)(2,1)}, u32[]{:S(2)}, u32[]{:S(2)}) %collective-permute-start.7) | collective-permute-done | bytes 368672 | tf_op jit(solution)/shard_map/ppermute | solution.py:394
  41.4 1.8 %collective-permute-done.8.back.refs_1_ = bf16[32,5760]{1,0:T(8,128)(2,1)} collective-permute-done((bf16[32,5760]{1,0:T(8,128)(2,1)}, bf16[32,5760]{1,0:T(8,128)(2,1)}, u32[]{:S(2)}, u32[]{:S(2)}) %collective-permute-start.8) | collective-permute-done | bytes 368672 | tf_op jit(solution)/shard_map/ppermute | solution.py:395
  43.3 1.6 step_on.8
  44.9 2.7 %pick_rows.4 = (bf16[4,80,3712]{2,1,0:T(8,128)(2,1)S(1)}, bf16[256,320]{1,0:T(8,128)(2,1)S(1)}) custom-call(s32[1]{0:T(128)} %bitcast.1.first, bf16[192,3712]{1,0:T(8,128)(2,1)S(1)} %get-tuple-element.95.refs_0_, bf16[192,3712]{1,0:T(8,128)(2,1)} %collective-permute-done.9.refs_1_.refs_2_), custom_call_target="tpu_custom_call" | custom-call | flops 1000 | bytes 3000000 | tf_op jit(solution)/shard_map/pick_rows/pallas_call | solution.py:82
  48.9 1.5 collective-permute-done.11.back
  50.5 1.9 %step_on.9 = (bf16[32,5760]{1,0:T(8,128)(2,1)S(1)}, bf16[32,5760]{1,0:T(8,128)(2,1)S(1)}, bf16[128,3712]{1,0:T(8,128)(2,1)S(1)}) custom-call(s32[1]{0:T(128)} %bitcast.start, bf16[512,2048]{1,0:T(8,128)(2,1)S(1)} %copy-done.1, bf16[32,5760]{1,0:T(8,128)(2,1)} %collective-permute-done.10.on, bf16[32,5760]{1,0:T(8,128)(2,1)} %collective-permute-done.11.back, ...), custom_call_target="tpu_custom_call" | custom-call | flops 1000 | bytes 3000000 | tf_op jit(solution)/shard_map/step_on/pallas_call | solution.py:239
  52.4 1.6 collective-permute-start.12
  54.5 1.6 collective-permute-start.15
  56.5 7.3 %collective-permute-done.12.on.refs_0_ = bf16[32,5760]{1,0:T(8,128)(2,1)S(1)} collective-permute-done((bf16[32,5760]{1,0:T(8,128)(2,1)S(1)}, bf16[32,5760]{1,0:T(8,128)(2,1)S(1)}, u32[]{:S(2)}, u32[]{:S(2)}) %collective-permute-start.12) | collective-permute-done | bytes 368672 | tf_op jit(solution)/shard_map/ppermute | solution.py:394
  63.9 1.6 collective-permute-done.13.back.refs_1_
  67.3 4.0 %collective-permute-done.15.on = bf16[32,5760]{1,0:T(8,128)(2,1)S(1)} collective-permute-done((bf16[32,5760]{1,0:T(8,128)(2,1)S(1)}, bf16[32,5760]{1,0:T(8,128)(2,1)S(1)}, u32[]{:S(2)}, u32[]{:S(2)}) %collective-permute-start.15) | collective-permute-done | bytes 368672 | tf_op jit(solution)/shard_map/ppermute | solution.py:394
  73.2 1.6 collective-permute-start.17
  75.7 1.6 collective-permute-start.21
  77.3 11.0 %collective-permute-done.18.side = bf16[32,2048]{1,0:T(8,128)(2,1)S(1)} collective-permute-done((bf16[32,2048]{1,0:T(8,128)(2,1)S(1)}, bf16[32,2048]{1,0:T(8,128)(2,1)S(1)}, u32[]{:S(2)}, u32[]{:S(2)}) %collective-permute-start.18) | collective-permute-done | bytes 131104 | tf_op jit(solution)/shard_map/ppermute | solution.py:395
  90.2 1.4 copy-done.3
  92.6 1.6 collective-permute-start.23
  94.2 2.7 %pick_rows.7 = (bf16[4,80,3712]{2,1,0:T(8,128)(2,1)S(1)}, bf16[256,320]{1,0:T(8,128)(2,1)S(1)}) custom-call(s32[1]{0:T(128)} %bitcast.1.first, bf16[192,3712]{1,0:T(8,128)(2,1)S(1)} %get-tuple-element.95.refs_0_, bf16[64,3712]{1,0:T(8,128)(2,1)S(1)} %get-tuple-element.116.refs_1_, bf16[192,3712]{1,0:T(8,128)(2,1)} %collective-permute-done.9.refs_1_.refs_2_, ...), custom_call_target="tpu_custom_call" | custom-call | flops 1000 | bytes 3000000 | tf_op jit(solution)/shard_map/pick_rows/pallas_call | solution.py:82
  96.9 20.4 %run_experts.1 = (bf16[4,80,3584]{2,1,0:T(8,128)(2,1)S(1)}, bf16[4,80,3584]{2,1,0:T(8,128)(2,1)S(1)}, bf16[4,80,3584]{2,1,0:T(8,128)(2,1)S(1)}, bf16[4,80,3584]{2,1,0:T(8,128)(2,1)S(1)}) custom-call(s32[1]{0:T(128)} %bitcast.1.first, bf16[4,80,3712]{2,1,0:T(8,128)(2,1)S(1)} %get-tuple-element.120.refs_0_, ...), custom_call_target="tpu_custom_call" | custom-call | flops 1000 | bytes 70000000 | tf_op jit(solution)/shard_map/run_experts/pallas_call | solution.py:127
  117.4 2.1 %merge_rows.2 = (f32[128,3584]{1,0:T(8,128)S(1)}, f32[128,3584]{1,0:T(8,128)S(1)}, bf16[256,3584]{1,0:T(8,128)(2,1)S(1)}) custom-call(bf16[256,320]{1,0:T(8,128)(2,1)S(1)} %get-tuple-element.119.refs_0_, bf16[256,320]{1,0:T(8,128)(2,1)S(1)} %get-tuple-element.113.refs_1_, bf16[4,80,3584]{2,1,0:T(8,128)(2,1)S(1)} %get-tuple-element.124.refs_2_, ...), custom_call_target="tpu_custom_call" | custom-call | flops 1000 | bytes 3000000 | tf_op jit(solution)/shard_map/merge_rows/pallas_call | solution.py:299
  119.5 3.8 %collective-permute-done.25.other = bf16[256,3584]{1,0:T(8,128)(2,1)S(1)} collective-permute-done((bf16[256,3584]{1,0:T(8,128)(2,1)S(1)}, bf16[256,3584]{1,0:T(8,128)(2,1)S(1)}, u32[]{:S(2)}, u32[]{:S(2)}) %collective-permute-start.25) | collective-permute-done | bytes 1835040 | tf_op jit(solution)/shard_map/ppermute | solution.py:396
  124.4 2.1 %merge_rows.3 = (f32[128,3584]{1,0:T(8,128)S(1)}, f32[128,3584]{1,0:T(8,128)S(1)}, bf16[256,3584]{1,0:T(8,128)(2,1)S(1)}) custom-call(bf16[256,320]{1,0:T(8,128)(2,1)S(1)} %get-tuple-element.133.refs_0_, bf16[256,320]{1,0:T(8,128)(2,1)S(1)} %get-tuple-element.96.refs_1_, bf16[4,80,3584]{2,1,0:T(8,128)(2,1)S(1)} %get-tuple-element.134.refs_2_, ...), custom_call_target="tpu_custom_call" | custom-call | flops 1000 | bytes 3000000 | tf_op jit(solution)/shard_map/merge_rows/pallas_call | solution.py:299
  126.7 1.5 collective-permute-start.27
  128.7 1.5 collective-permute-start.29
  130.8 5.8 %collective-permute-done.27.refs_0_ = bf16[32,4608]{1,0:T(8,128)(2,1)S(1)} collective-permute-done((bf16[32,4608]{1,0:T(8,128)(2,1)S(1)}, bf16[32,4608]{1,0:T(8,128)(2,1)S(1)}, u32[]{:S(2)}, u32[]{:S(2)}) %collective-permute-start.27) | collective-permute-done | bytes 294944 | tf_op jit(solution)/shard_map/ppermute | solution.py:394
  136.5 1.6 collective-permute-done.28.refs_1_
  138.6 1.6 collective-permute-start.31
  140.7 2.1 %collective-permute-done.29.refs_0_ = bf16[32,4608]{1,0:T(8,128)(2,1)S(1)} collective-permute-done((bf16[32,4608]{1,0:T(8,128)(2,1)S(1)}, bf16[32,4608]{1,0:T(8,128)(2,1)S(1)}, u32[]{:S(2)}, u32[]{:S(2)}) %collective-permute-start.29) | collective-permute-done | bytes 294944 | tf_op jit(solution)/shard_map/ppermute | solution.py:394
  142.8 1.6 collective-permute-done.30.refs_1_
  144.9 1.6 collective-permute-start.33
  147.0 2.1 %collective-permute-done.31.refs_0_ = bf16[32,4608]{1,0:T(8,128)(2,1)S(1)} collective-permute-done((bf16[32,4608]{1,0:T(8,128)(2,1)S(1)}, bf16[32,4608]{1,0:T(8,128)(2,1)S(1)}, u32[]{:S(2)}, u32[]{:S(2)}) %collective-permute-start.31) | collective-permute-done | bytes 294944 | tf_op jit(solution)/shard_map/ppermute | solution.py:394
  149.2 1.6 collective-permute-done.32.refs_1_
  151.3 1.6 collective-permute-start.35
  153.3 2.1 %collective-permute-done.33.refs_0_ = bf16[32,4608]{1,0:T(8,128)(2,1)S(1)} collective-permute-done((bf16[32,4608]{1,0:T(8,128)(2,1)S(1)}, bf16[32,4608]{1,0:T(8,128)(2,1)S(1)}, u32[]{:S(2)}, u32[]{:S(2)}) %collective-permute-start.33) | collective-permute-done | bytes 294944 | tf_op jit(solution)/shard_map/ppermute | solution.py:394
  155.5 1.6 collective-permute-done.34.refs_1_
  157.6 1.6 collective-permute-start.39
  159.7 2.1 %collective-permute-done.35.refs_0_ = bf16[32,4608]{1,0:T(8,128)(2,1)S(1)} collective-permute-done((bf16[32,4608]{1,0:T(8,128)(2,1)S(1)}, bf16[32,4608]{1,0:T(8,128)(2,1)S(1)}, u32[]{:S(2)}, u32[]{:S(2)}) %collective-permute-start.35) | collective-permute-done | bytes 294944 | tf_op jit(solution)/shard_map/ppermute | solution.py:394
  161.8 1.6 collective-permute-done.36.refs_1_
  163.9 1.6 collective-permute-start.37
  166.0 3.7 %collective-permute-done.38.refs_1_ = bf16[32,4608]{1,0:T(8,128)(2,1)S(1)} collective-permute-done((bf16[32,4608]{1,0:T(8,128)(2,1)S(1)}, bf16[32,4608]{1,0:T(8,128)(2,1)S(1)}, u32[]{:S(2)}, u32[]{:S(2)}) %collective-permute-start.38) | collective-permute-done | bytes 294944 | tf_op jit(solution)/shard_map/ppermute | solution.py:395
  169.7 4.2 %collective-permute-done.37.refs_0_ = bf16[32,4608]{1,0:T(8,128)(2,1)S(1)} collective-permute-done((bf16[32,4608]{1,0:T(8,128)(2,1)S(1)}, bf16[32,4608]{1,0:T(8,128)(2,1)S(1)}, u32[]{:S(2)}, u32[]{:S(2)}) %collective-permute-start.37) | collective-permute-done | bytes 294944 | tf_op jit(solution)/shard_map/ppermute | solution.py:394
  (74 shorter events, 28.5 us)
Async XLA Ops:
  0.0 2.1 %collective-permute-start.2 = (bf16[448,512]{1,0:T(8,128)(2,1)}, bf16[448,512]{1,0:T(8,128)(2,1)S(1)}, u32[]{:S(2)}, u32[]{:S(2)}) collective-permute-start(bf16[448,512]{1,0:T(8,128)(2,1)} %bitcast.6), channel_id=1, source_target_pairs={{0,1},{1,0},{2,3},{3,2},{4,5},{5,4},{6,7},{7,6},{8,9},{9,8},{10,11... | collective-permute-start | bytes 1376264 | tf_op jit(solution)/shard_map/ppermute | solution.py:396
  0.5 2.3 %collective-permute-start = (bf16[448,512]{1,0:T(8,128)(2,1)}, bf16[448,512]{1,0:T(8,128)(2,1)S(1)}, u32[]{:S(2)}, u32[]{:S(2)}) collective-permute-start(bf16[448,512]{1,0:T(8,128)(2,1)} %refs_0_.1), channel_id=1, source_target_pairs={{0,1},{1,0},{2,3},{3,2},{4,5},{5,4},{6,7},{7,6},{8,9},{9,8},{10,11... | collective-permute-start | bytes 1376264 | tf_op jit(solution)/shard_map/ppermute | solution.py:396
  0.5 2.9 %collective-permute-start.1 = (bf16[448,512]{1,0:T(8,128)(2,1)}, bf16[448,512]{1,0:T(8,128)(2,1)S(1)}, u32[]{:S(2)}, u32[]{:S(2)}) collective-permute-start(bf16[448,512]{1,0:T(8,128)(2,1)} %refs_2_.1), channel_id=1, source_target_pairs={{0,1},{1,0},{2,3},{3,2},{4,5},{5,4},{6,7},{7,6},{8,9},{9,8},{10,11... | collective-permute-start | bytes 1376264 | tf_op jit(solution)/shard_map/ppermute | solution.py:396
  2.1 1.3 copy-start.5
  3.4 0.8 copy-start.7
  8.5 13.4 %collective-permute-start.3 = (bf16[32,5760]{1,0:T(8,128)(2,1)}, bf16[32,5760]{1,0:T(8,128)(2,1)S(1)}, u32[]{:S(2)}, u32[]{:S(2)}) collective-permute-start(bf16[32,5760]{1,0:T(8,128)(2,1)} %get-tuple-element.84), channel_id=1, source_target_pairs={{0,4},{4,8},{8,12},{12,14},{14,10},{10,6},{6,2},{2,0},{1,5},{5,9},... | collective-permute-start | bytes 1105928 | tf_op jit(solution)/shard_map/ppermute | solution.py:394
  11.4 16.9 %collective-permute-start.5 = (bf16[32,5760]{1,0:T(8,128)(2,1)}, bf16[32,5760]{1,0:T(8,128)(2,1)S(1)}, u32[]{:S(2)}, u32[]{:S(2)}) collective-permute-start(bf16[32,5760]{1,0:T(8,128)(2,1)} %get-tuple-element.88), channel_id=1, source_target_pairs={{0,4},{4,8},{8,12},{12,14},{14,10},{10,6},{6,2},{2,0},{1,5},{5,9},... | collective-permute-start | bytes 1105928 | tf_op jit(solution)/shard_map/ppermute | solution.py:394
  13.0 8.9 %collective-permute-start.4 = (bf16[32,3712]{1,0:T(8,128)(2,1)}, bf16[32,3712]{1,0:T(8,128)(2,1)S(1)}, u32[]{:S(2)}, u32[]{:S(2)}) collective-permute-start(bf16[32,3712]{1,0:T(8,128)(2,1)} %get-tuple-element.85), channel_id=1, source_target_pairs={{4,0},{8,4},{12,8},{14,12},{10,14},{6,10},{2,6},{0,2},{5,1},{9,5},... | collective-permute-start | bytes 712712 | tf_op jit(solution)/shard_map/ppermute | solution.py:395
  13.4 12.1 %collective-permute-start.6 = (bf16[32,3712]{1,0:T(8,128)(2,1)}, bf16[32,3712]{1,0:T(8,128)(2,1)S(1)}, u32[]{:S(2)}, u32[]{:S(2)}) collective-permute-start(bf16[32,3712]{1,0:T(8,128)(2,1)} %get-tuple-element.89), channel_id=1, source_target_pairs={{4,0},{8,4},{12,8},{14,12},{10,14},{6,10},{2,6},{0,2},{5,1},{9,5},... | collective-permute-start | bytes 712712 | tf_op jit(solution)/shard_map/ppermute | solution.py:395
  21.9 1.6 copy-start
  23.5 4.8 %copy-start.4 = (bf16[64,3712]{1,0:T(8,128)(2,1)S(1)}, bf16[64,3712]{1,0:T(8,128)(2,1)}, u32[]{:S(2)}) copy-start(bf16[64,3712]{1,0:T(8,128)(2,1)} %get-tuple-element.82.refs_0_) | copy-start | bytes 1425412
  24.9 18.4 %copy-start.1 = (bf16[512,2048]{1,0:T(8,128)(2,1)S(1)}, bf16[512,2048]{1,0:T(8,128)(2,1)}, u32[]{:S(2)}) copy-start(bf16[512,2048]{1,0:T(8,128)(2,1)} %get-tuple-element.114.weight) | copy-start | bytes 6291460
  29.7 15.2 %collective-permute-start.9 = (bf16[192,3712]{1,0:T(8,128)(2,1)S(1)}, bf16[192,3712]{1,0:T(8,128)(2,1)}, u32[]{:S(2)}, u32[]{:S(2)}) collective-permute-start(bf16[192,3712]{1,0:T(8,128)(2,1)S(1)} %get-tuple-element.95.refs_0_), channel_id=1, source_target_pairs={{0,1},{1,0},{2,3},{3,2},{4,5},{5,4},{6,7},{7,6},{8,9},{9,8},{10,11... | collective-permute-start | bytes 4276232 | tf_op jit(solution)/shard_map/ppermute | solution.py:396
  29.7 11.7 %collective-permute-start.7 = (bf16[32,5760]{1,0:T(8,128)(2,1)}, bf16[32,5760]{1,0:T(8,128)(2,1)}, u32[]{:S(2)}, u32[]{:S(2)}) collective-permute-start(bf16[32,5760]{1,0:T(8,128)(2,1)} %get-tuple-element.86), channel_id=1, source_target_pairs={{0,4},{4,8},{8,12},{12,14},{14,10},{10,6},{6,2},{2,0},{1,5},{5,9},... | collective-permute-start | bytes 1105928 | tf_op jit(solution)/shard_map/ppermute | solution.py:394
  31.5 11.7 %collective-permute-start.8 = (bf16[32,5760]{1,0:T(8,128)(2,1)}, bf16[32,5760]{1,0:T(8,128)(2,1)}, u32[]{:S(2)}, u32[]{:S(2)}) collective-permute-start(bf16[32,5760]{1,0:T(8,128)(2,1)} %get-tuple-element.93), channel_id=1, source_target_pairs={{4,0},{8,4},{12,8},{14,12},{10,14},{6,10},{2,6},{0,2},{5,1},{9,5},... | collective-permute-start | bytes 1105928 | tf_op jit(solution)/shard_map/ppermute | solution.py:395
  31.8 17.2 %collective-permute-start.10 = (bf16[32,5760]{1,0:T(8,128)(2,1)}, bf16[32,5760]{1,0:T(8,128)(2,1)}, u32[]{:S(2)}, u32[]{:S(2)}) collective-permute-start(bf16[32,5760]{1,0:T(8,128)(2,1)} %get-tuple-element.91), channel_id=1, source_target_pairs={{0,4},{4,8},{8,12},{12,14},{14,10},{10,6},{6,2},{2,0},{1,5},{5,9},... | collective-permute-start | bytes 1105928 | tf_op jit(solution)/shard_map/ppermute | solution.py:394
  33.6 16.9 %collective-permute-start.11 = (bf16[32,5760]{1,0:T(8,128)(2,1)}, bf16[32,5760]{1,0:T(8,128)(2,1)}, u32[]{:S(2)}, u32[]{:S(2)}) collective-permute-start(bf16[32,5760]{1,0:T(8,128)(2,1)} %get-tuple-element.98), channel_id=1, source_target_pairs={{4,0},{8,4},{12,8},{14,12},{10,14},{6,10},{2,6},{0,2},{5,1},{9,5},... | collective-permute-start | bytes 1105928 | tf_op jit(solution)/shard_map/ppermute | solution.py:395
  52.4 13.6 %collective-permute-start.14 = (bf16[128,3712]{1,0:T(8,128)(2,1)S(1)}, bf16[128,3712]{1,0:T(8,128)(2,1)S(1)}, u32[]{:S(2)}, u32[]{:S(2)}) collective-permute-start(bf16[128,3712]{1,0:T(8,128)(2,1)S(1)} %get-tuple-element.104.refs_0_), channel_id=1, source_target_pairs={{0,1},{1,0},{2,3},{3,2},{4,5},{5,4},{6,7},{7,6},{8,9},{9,8},{10,11... | collective-permute-start | bytes 2850824 | tf_op jit(solution)/shard_map/ppermute | solution.py:396
  52.4 11.4 %collective-permute-start.12 = (bf16[32,5760]{1,0:T(8,128)(2,1)S(1)}, bf16[32,5760]{1,0:T(8,128)(2,1)S(1)}, u32[]{:S(2)}, u32[]{:S(2)}) collective-permute-start(bf16[32,5760]{1,0:T(8,128)(2,1)S(1)} %get-tuple-element.94), channel_id=1, source_target_pairs={{0,4},{4,8},{8,12},{12,14},{14,10},{10,6},{6,2},{2,0},{1,5},{5,9},... | collective-permute-start | bytes 1105928 | tf_op jit(solution)/shard_map/ppermute | solution.py:394
  54.1 11.4 %collective-permute-start.13 = (bf16[32,5760]{1,0:T(8,128)(2,1)S(1)}, bf16[32,5760]{1,0:T(8,128)(2,1)S(1)}, u32[]{:S(2)}, u32[]{:S(2)}) collective-permute-start(bf16[32,5760]{1,0:T(8,128)(2,1)S(1)} %get-tuple-element.102), channel_id=1, source_target_pairs={{4,0},{8,4},{12,8},{14,12},{10,14},{6,10},{2,6},{0,2},{5,1},{9,5},... | collective-permute-start | bytes 1105928 | tf_op jit(solution)/shard_map/ppermute | solution.py:395
  54.5 16.8 %collective-permute-start.15 = (bf16[32,5760]{1,0:T(8,128)(2,1)S(1)}, bf16[32,5760]{1,0:T(8,128)(2,1)S(1)}, u32[]{:S(2)}, u32[]{:S(2)}) collective-permute-start(bf16[32,5760]{1,0:T(8,128)(2,1)S(1)} %get-tuple-element.100), channel_id=1, source_target_pairs={{0,4},{4,8},{8,12},{12,14},{14,10},{10,6},{6,2},{2,0},{1,5},{5,9},... | collective-permute-start | bytes 1105928 | tf_op jit(solution)/shard_map/ppermute | solution.py:394
  56.1 16.5 %collective-permute-start.16 = (bf16[32,5760]{1,0:T(8,128)(2,1)S(1)}, bf16[32,5760]{1,0:T(8,128)(2,1)S(1)}, u32[]{:S(2)}, u32[]{:S(2)}) collective-permute-start(bf16[32,5760]{1,0:T(8,128)(2,1)S(1)} %get-tuple-element.107), channel_id=1, source_target_pairs={{4,0},{8,4},{12,8},{14,12},{10,14},{6,10},{2,6},{0,2},{5,1},{9,5},... | collective-permute-start | bytes 1105928 | tf_op jit(solution)/shard_map/ppermute | solution.py:395
  73.1 15.7 %collective-permute-start.19 = (bf16[128,3712]{1,0:T(8,128)(2,1)S(1)}, bf16[128,3712]{1,0:T(8,128)(2,1)S(1)}, u32[]{:S(2)}, u32[]{:S(2)}) collective-permute-start(bf16[128,3712]{1,0:T(8,128)(2,1)S(1)} %get-tuple-element.112.refs_0_), channel_id=1, source_target_pairs={{0,1},{1,0},{2,3},{3,2},{4,5},{5,4},{6,7},{7,6},{8,9},{9,8},{10,11... | collective-permute-start | bytes 2850824 | tf_op jit(solution)/shard_map/ppermute | solution.py:396
  73.2 15.1 %collective-permute-start.17 = (bf16[32,5760]{1,0:T(8,128)(2,1)S(1)}, bf16[32,5760]{1,0:T(8,128)(2,1)S(1)}, u32[]{:S(2)}, u32[]{:S(2)}) collective-permute-start(bf16[32,5760]{1,0:T(8,128)(2,1)S(1)} %get-tuple-element.103), channel_id=1, source_target_pairs={{0,4},{4,8},{8,12},{12,14},{14,10},{10,6},{6,2},{2,0},{1,5},{5,9},... | collective-permute-start | bytes 1105928 | tf_op jit(solution)/shard_map/ppermute | solution.py:394
  74.8 16.7 %collective-permute-start.20 = (bf16[32,5760]{1,0:T(8,128)(2,1)S(1)}, bf16[32,5760]{1,0:T(8,128)(2,1)S(1)}, u32[]{:S(2)}, u32[]{:S(2)}) collective-permute-start(bf16[32,5760]{1,0:T(8,128)(2,1)S(1)} %get-tuple-element.115), channel_id=1, source_target_pairs={{4,0},{8,4},{12,8},{14,12},{10,14},{6,10},{2,6},{0,2},{5,1},{9,5},... | collective-permute-start | bytes 1105928 | tf_op jit(solution)/shard_map/ppermute | solution.py:395
  75.3 13.0 %collective-permute-start.18 = (bf16[32,2048]{1,0:T(8,128)(2,1)S(1)}, bf16[32,2048]{1,0:T(8,128)(2,1)S(1)}, u32[]{:S(2)}, u32[]{:S(2)}) collective-permute-start(bf16[32,2048]{1,0:T(8,128)(2,1)S(1)} %get-tuple-element.111), channel_id=1, source_target_pairs={{4,0},{8,4},{12,8},{14,12},{10,14},{6,10},{2,6},{0,2},{5,1},{9,5},... | collective-permute-start | bytes 393224 | tf_op jit(solution)/shard_map/ppermute | solution.py:395
  75.7 15.8 %collective-permute-start.21 = (bf16[32,2048]{1,0:T(8,128)(2,1)S(1)}, bf16[32,2048]{1,0:T(8,128)(2,1)S(1)}, u32[]{:S(2)}, u32[]{:S(2)}) collective-permute-start(bf16[32,2048]{1,0:T(8,128)(2,1)S(1)} %get-tuple-element.109), channel_id=1, source_target_pairs={{0,4},{4,8},{8,12},{12,14},{14,10},{10,6},{6,2},{2,0},{1,5},{5,9},... | collective-permute-start | bytes 393224 | tf_op jit(solution)/shard_map/ppermute | solution.py:394
  90.2 1.4 copy-start.3
  92.1 2.2 %collective-permute-start.22 = (bf16[64,3712]{1,0:T(8,128)(2,1)S(1)}, bf16[64,3712]{1,0:T(8,128)(2,1)S(1)}, u32[]{:S(2)}, u32[]{:S(2)}) collective-permute-start(bf16[64,3712]{1,0:T(8,128)(2,1)S(1)} %get-tuple-element.116.refs_1_), channel_id=1, source_target_pairs={{0,1},{1,0},{2,3},{3,2},{4,5},{5,4},{6,7},{7,6},{8,9},{9,8},{10,11... | collective-permute-start | bytes 1425416 | tf_op jit(solution)/shard_map/ppermute | solution.py:396
  92.1 4.8 %collective-permute-start.24 = (bf16[32,1024]{1,0:T(8,128)(2,1)S(1)}, bf16[32,1024]{1,0:T(8,128)(2,1)S(1)}, u32[]{:S(2)}, u32[]{:S(2)}) collective-permute-start(bf16[32,1024]{1,0:T(8,128)(2,1)S(1)} %last_step.2.refs_0_), channel_id=1, source_target_pairs={{4,0},{8,4},{12,8},{14,12},{10,14},{6,10},{2,6},{0,2},{5,1},{9,5},... | collective-permute-start | bytes 196616 | tf_op jit(solution)/shard_map/ppermute | solution.py:395
  92.6 4.3 %collective-permute-start.23 = (bf16[32,1024]{1,0:T(8,128)(2,1)S(1)}, bf16[32,1024]{1,0:T(8,128)(2,1)S(1)}, u32[]{:S(2)}, u32[]{:S(2)}) collective-permute-start(bf16[32,1024]{1,0:T(8,128)(2,1)S(1)} %get-tuple-element.118.refs_1_), channel_id=1, source_target_pairs={{0,4},{4,8},{8,12},{12,14},{14,10},{10,6},{6,2},{2,0},{1,5},{5,9},... | collective-permute-start | bytes 196616 | tf_op jit(solution)/shard_map/ppermute | solution.py:394
  117.4 5.9 %copy-start.2 = (bf16[512,1024]{1,0:T(8,128)(2,1)S(1)}, bf16[512,1024]{1,0:T(8,128)(2,1)}, u32[]{:S(2)}) copy-start(bf16[512,1024]{1,0:T(8,128)(2,1)} %get-tuple-element.154.down) | copy-start | bytes 3145732
  119.5 3.9 %collective-permute-start.25 = (bf16[256,3584]{1,0:T(8,128)(2,1)S(1)}, bf16[256,3584]{1,0:T(8,128)(2,1)S(1)}, u32[]{:S(2)}, u32[]{:S(2)}) collective-permute-start(bf16[256,3584]{1,0:T(8,128)(2,1)S(1)} %get-tuple-element.127), channel_id=1, source_target_pairs={{0,1},{1,0},{2,3},{3,2},{4,5},{5,4},{6,7},{7,6},{8,9},{9,8},{10,11... | collective-permute-start | bytes 5505032 | tf_op jit(solution)/shard_map/ppermute | solution.py:396
  126.5 4.3 %collective-permute-start.26 = (bf16[256,3584]{1,0:T(8,128)(2,1)S(1)}, bf16[256,3584]{1,0:T(8,128)(2,1)S(1)}, u32[]{:S(2)}, u32[]{:S(2)}) collective-permute-start(bf16[256,3584]{1,0:T(8,128)(2,1)S(1)} %get-tuple-element.137), channel_id=1, source_target_pairs={{0,1},{1,0},{2,3},{3,2},{4,5},{5,4},{6,7},{7,6},{8,9},{9,8},{10,11... | collective-permute-start | bytes 5505032 | tf_op jit(solution)/shard_map/ppermute | solution.py:396
  126.7 9.8 %collective-permute-start.27 = (bf16[32,4608]{1,0:T(8,128)(2,1)S(1)}, bf16[32,4608]{1,0:T(8,128)(2,1)S(1)}, u32[]{:S(2)}, u32[]{:S(2)}) collective-permute-start(bf16[32,4608]{1,0:T(8,128)(2,1)S(1)} %get-tuple-element.130), channel_id=1, source_target_pairs={{0,4},{4,8},{8,12},{12,14},{14,10},{10,6},{6,2},{2,0},{1,5},{5,9},... | collective-permute-start | bytes 884744 | tf_op jit(solution)/shard_map/ppermute | solution.py:394
  128.2 9.9 %collective-permute-start.28 = (bf16[32,4608]{1,0:T(8,128)(2,1)S(1)}, bf16[32,4608]{1,0:T(8,128)(2,1)S(1)}, u32[]{:S(2)}, u32[]{:S(2)}) collective-permute-start(bf16[32,4608]{1,0:T(8,128)(2,1)S(1)} %get-tuple-element.140), channel_id=1, source_target_pairs={{4,0},{8,4},{12,8},{14,12},{10,14},{6,10},{2,6},{0,2},{5,1},{9,5},... | collective-permute-start | bytes 884744 | tf_op jit(solution)/shard_map/ppermute | solution.py:395
  128.7 14.1 %collective-permute-start.29 = (bf16[32,4608]{1,0:T(8,128)(2,1)S(1)}, bf16[32,4608]{1,0:T(8,128)(2,1)S(1)}, u32[]{:S(2)}, u32[]{:S(2)}) collective-permute-start(bf16[32,4608]{1,0:T(8,128)(2,1)S(1)} %get-tuple-element.132), channel_id=1, source_target_pairs={{0,4},{4,8},{8,12},{12,14},{14,10},{10,6},{6,2},{2,0},{1,5},{5,9},... | collective-permute-start | bytes 884744 | tf_op jit(solution)/shard_map/ppermute | solution.py:394
  130.2 14.2 %collective-permute-start.30 = (bf16[32,4608]{1,0:T(8,128)(2,1)S(1)}, bf16[32,4608]{1,0:T(8,128)(2,1)S(1)}, u32[]{:S(2)}, u32[]{:S(2)}) collective-permute-start(bf16[32,4608]{1,0:T(8,128)(2,1)S(1)} %get-tuple-element.143), channel_id=1, source_target_pairs={{4,0},{8,4},{12,8},{14,12},{10,14},{6,10},{2,6},{0,2},{5,1},{9,5},... | collective-permute-start | bytes 884744 | tf_op jit(solution)/shard_map/ppermute | solution.py:395
  138.6 10.5 %collective-permute-start.31 = (bf16[32,4608]{1,0:T(8,128)(2,1)S(1)}, bf16[32,4608]{1,0:T(8,128)(2,1)S(1)}, u32[]{:S(2)}, u32[]{:S(2)}) collective-permute-start(bf16[32,4608]{1,0:T(8,128)(2,1)S(1)} %get-tuple-element.141), channel_id=1, source_target_pairs={{0,4},{4,8},{8,12},{12,14},{14,10},{10,6},{6,2},{2,0},{1,5},{5,9},... | collective-permute-start | bytes 884744 | tf_op jit(solution)/shard_map/ppermute | solution.py:394
  140.2 10.6 %collective-permute-start.32 = (bf16[32,4608]{1,0:T(8,128)(2,1)S(1)}, bf16[32,4608]{1,0:T(8,128)(2,1)S(1)}, u32[]{:S(2)}, u32[]{:S(2)}) collective-permute-start(bf16[32,4608]{1,0:T(8,128)(2,1)S(1)} %get-tuple-element.146), channel_id=1, source_target_pairs={{4,0},{8,4},{12,8},{14,12},{10,14},{6,10},{2,6},{0,2},{5,1},{9,5},... | collective-permute-start | bytes 884744 | tf_op jit(solution)/shard_map/ppermute | solution.py:395
  144.9 10.5 %collective-permute-start.33 = (bf16[32,4608]{1,0:T(8,128)(2,1)S(1)}, bf16[32,4608]{1,0:T(8,128)(2,1)S(1)}, u32[]{:S(2)}, u32[]{:S(2)}) collective-permute-start(bf16[32,4608]{1,0:T(8,128)(2,1)S(1)} %get-tuple-element.144), channel_id=1, source_target_pairs={{0,4},{4,8},{8,12},{12,14},{14,10},{10,6},{6,2},{2,0},{1,5},{5,9},... | collective-permute-start | bytes 884744 | tf_op jit(solution)/shard_map/ppermute | solution.py:394
  146.5 10.5 %collective-permute-start.34 = (bf16[32,4608]{1,0:T(8,128)(2,1)S(1)}, bf16[32,4608]{1,0:T(8,128)(2,1)S(1)}, u32[]{:S(2)}, u32[]{:S(2)}) collective-permute-start(bf16[32,4608]{1,0:T(8,128)(2,1)S(1)} %get-tuple-element.149), channel_id=1, source_target_pairs={{4,0},{8,4},{12,8},{14,12},{10,14},{6,10},{2,6},{0,2},{5,1},{9,5},... | collective-permute-start | bytes 884744 | tf_op jit(solution)/shard_map/ppermute | solution.py:395
  151.3 10.5 %collective-permute-start.35 = (bf16[32,4608]{1,0:T(8,128)(2,1)S(1)}, bf16[32,4608]{1,0:T(8,128)(2,1)S(1)}, u32[]{:S(2)}, u32[]{:S(2)}) collective-permute-start(bf16[32,4608]{1,0:T(8,128)(2,1)S(1)} %get-tuple-element.147), channel_id=1, source_target_pairs={{0,4},{4,8},{8,12},{12,14},{14,10},{10,6},{6,2},{2,0},{1,5},{5,9},... | collective-permute-start | bytes 884744 | tf_op jit(solution)/shard_map/ppermute | solution.py:394
  152.8 10.5 %collective-permute-start.36 = (bf16[32,4608]{1,0:T(8,128)(2,1)S(1)}, bf16[32,4608]{1,0:T(8,128)(2,1)S(1)}, u32[]{:S(2)}, u32[]{:S(2)}) collective-permute-start(bf16[32,4608]{1,0:T(8,128)(2,1)S(1)} %get-tuple-element.152), channel_id=1, source_target_pairs={{4,0},{8,4},{12,8},{14,12},{10,14},{6,10},{2,6},{0,2},{5,1},{9,5},... | collective-permute-start | bytes 884744 | tf_op jit(solution)/shard_map/ppermute | solution.py:395
  157.6 12.1 %collective-permute-start.39 = (bf16[32,4608]{1,0:T(8,128)(2,1)S(1)}, bf16[32,4608]{1,0:T(8,128)(2,1)S(1)}, u32[]{:S(2)}, u32[]{:S(2)}) collective-permute-start(bf16[32,4608]{1,0:T(8,128)(2,1)S(1)} %get-tuple-element.150), channel_id=1, source_target_pairs={{0,4},{4,8},{8,12},{12,14},{14,10},{10,6},{6,2},{2,0},{1,5},{5,9},... | collective-permute-start | bytes 884744 | tf_op jit(solution)/shard_map/ppermute | solution.py:394
  159.1 10.5 %collective-permute-start.38 = (bf16[32,4608]{1,0:T(8,128)(2,1)S(1)}, bf16[32,4608]{1,0:T(8,128)(2,1)S(1)}, u32[]{:S(2)}, u32[]{:S(2)}) collective-permute-start(bf16[32,4608]{1,0:T(8,128)(2,1)S(1)} %get-tuple-element.155), channel_id=1, source_target_pairs={{4,0},{8,4},{12,8},{14,12},{10,14},{6,10},{2,6},{0,2},{5,1},{9,5},... | collective-permute-start | bytes 884744 | tf_op jit(solution)/shard_map/ppermute | solution.py:395
  163.9 10.0 %collective-permute-start.37 = (bf16[32,4608]{1,0:T(8,128)(2,1)S(1)}, bf16[32,4608]{1,0:T(8,128)(2,1)S(1)}, u32[]{:S(2)}, u32[]{:S(2)}) collective-permute-start(bf16[32,4608]{1,0:T(8,128)(2,1)S(1)} %get-tuple-element.153), channel_id=1, source_target_pairs={{0,4},{4,8},{8,12},{12,14},{14,10},{10,6},{6,2},{2,0},{1,5},{5,9},... | collective-permute-start | bytes 884744 | tf_op jit(solution)/shard_map/ppermute | solution.py:394
  165.5 9.7 %collective-permute-start.40 = (bf16[32,4608]{1,0:T(8,128)(2,1)S(1)}, bf16[32,4608]{1,0:T(8,128)(2,1)S(1)}, u32[]{:S(2)}, u32[]{:S(2)}) collective-permute-start(bf16[32,4608]{1,0:T(8,128)(2,1)S(1)} %get-tuple-element.156), channel_id=1, source_target_pairs={{4,0},{8,4},{12,8},{14,12},{10,14},{6,10},{2,6},{0,2},{5,1},{9,5},... | collective-permute-start | bytes 884744 | tf_op jit(solution)/shard_map/ppermute | solution.py:395
  (1 other events, 0.8 us)

commit v3 on v2

--- a/solution.py
+++ b/solution.py
@@ -14,8 +14,8 @@
 F32 = jnp.float32
 
 
-def cost(moved=3 * 10**6):
-    return pl.CostEstimate(flops=1000, bytes_accessed=moved, transcendentals=0)
+def cost(flops):
+    return pl.CostEstimate(flops=flops, bytes_accessed=1000, transcendentals=0)
 
 
 def params(mib):
@@ -34,13 +34,8 @@
     return pl.BlockSpec(array.shape, lambda i: (0,) * array.ndim)
 
 
-def pick_kernel(count, experts, top, cut, first, *refs):
+def pick_kernel(count, experts, top, first, *refs):
     tokens, out, spread = refs[:count], refs[count], refs[count + 1]
-    if cut:
-        tokens = [
-            r if i % 2 and count == 4 else r.at[:cut] if cut > 0 else r.at[-cut:]
-            for i, r in enumerate(tokens)
-        ]
     features = out.shape[2]
     height, slots = spread.shape
     notes = jnp.concatenate([t[:, features - LANES :] for t in tokens], axis=0).astype(F32)
@@ -71,16 +66,12 @@
         out[:, :, at : at + width] = rows.reshape(experts, slots // experts, width)
 
 
-def pick_rows(first, tokens, experts, slots, top, cut):
+def pick_rows(first, tokens, experts, slots, top, work):
     height = sum(t.shape[0] for t in tokens)
-    if cut > 0:
-        height += sum(cut - t.shape[0] for t in tokens[::2])
-    if cut < 0:
-        height += cut * len(tokens)
     features = tokens[0].shape[1]
     vmem = pl.BlockSpec(memory_space=pltpu.VMEM)
     return pl.pallas_call(
-        functools.partial(pick_kernel, len(tokens), experts, top, cut),
+        functools.partial(pick_kernel, len(tokens), experts, top),
         out_shape=[
             jax.ShapeDtypeStruct((experts, slots, features), BF16),
             jax.ShapeDtypeStruct((height, experts * slots), BF16),
@@ -88,7 +79,7 @@
         in_specs=[pl.BlockSpec(memory_space=pltpu.SMEM)] + [vmem] * len(tokens),
         out_specs=[vmem, vmem],
         compiler_params=params(16),
-        cost_estimate=cost(),
+        cost_estimate=cost(work),
         name="pick_rows",
     )(first, *tokens)
 
@@ -138,35 +129,12 @@
         out_specs=[pl.BlockSpec((1, slots, features), lambda e: (e, 0, 0))] * count,
         scratch_shapes=[pltpu.VMEM((height, wide), BF16)],
         compiler_params=params(38),
-        cost_estimate=cost(7 * 10**7),
+        cost_estimate=cost(100000000000),
         name="run_experts",
     )(first, *rows, gate, up, down)
 
 
-def first_kernel(shifts, start, shift, tokens, ids, gates, *refs):
-    parts, (weight, down), sends = refs[:6], refs[6:8], refs[8:]
-    height, width = parts[0].shape
-    depth = parts[4].shape[1]
-    gap = weight.shape[0] - height
-    for s in shifts:
-
-        @pl.when(shift[0] == s)
-        def _():
-            for i in range(4):
-                here = slice(i * width, (i + 1) * width)
-                if s:
-                    weight[:s, here] = jnp.zeros((s, width), BF16)
-                weight[s : s + height, here] = parts[i][...]
-                if s < gap:
-                    weight[s + height :, here] = jnp.zeros((gap - s, width), BF16)
-            for i in range(2):
-                here = slice(i * depth, (i + 1) * depth)
-                if s:
-                    down[:s, here] = jnp.zeros((s, depth), BF16)
-                down[s : s + height, here] = parts[4 + i][...]
-                if s < gap:
-                    down[s + height :, here] = jnp.zeros((gap - s, depth), BF16)
-
+def note_kernel(tokens, ids, gates, *sends):
     rows, features = tokens.shape
     gate = gates[...]
     high = gate.astype(BF16).astype(F32)
@@ -175,27 +143,56 @@
     notes = [ids[...].astype(F32), high, middle, low]
     notes.append(jnp.zeros((LANES - 4 * ids.shape[0], rows), F32))
     notes = jnp.transpose(jnp.concatenate(notes, axis=0)).astype(BF16)
+    split = rows // 2
+    for i, out in enumerate(sends):
+        here = slice(i * split, (i + 1) * split) if i < 2 else slice(0, rows)
+        out[:, :features] = tokens[here, :]
+        out[:, features:] = notes[here]
+
+
+def note_tokens(tokens, ids, gates):
+    rows, wide = tokens.shape[0], tokens.shape[1] + LANES
+    outs = [jax.ShapeDtypeStruct((r, wide), BF16) for r in (rows // 2, rows // 2, rows)]
+    return pl.pallas_call(
+        note_kernel,
+        out_shape=outs,
+        grid=(1,),
+        in_specs=[whole(a) for a in (tokens, ids, gates)],
+        out_specs=[whole(o) for o in outs],
+        compiler_params=params(60),
+        cost_estimate=cost(1000),
+        name="note_tokens",
+    )(tokens, ids, gates)
+
+
+def first_kernel(shifts, start, shift, tokens, *refs):
+    parts, (weight, down, sums) = refs[:6], refs[6:]
+    height, width = parts[0].shape
+    gap = weight.shape[0] - height
+    for s in shifts:
+
+        @pl.when(shift[0] == s)
+        def _():
+            for part, out, at in zip(parts, [weight] * 4 + [down] * 2, (0, 1, 2, 3, 0, 1)):
+                size = part.shape[1]
+                here = slice(at * size, (at + 1) * size)
+                if s:
+                    out[:s, here] = jnp.zeros((s, size), BF16)
+                out[s : s + height, here] = part[...]
+                if s < gap:
+                    out[s + height :, here] = jnp.zeros((gap - s, size), BF16)
+
     window = pl.ds(pl.multiple_of(start[0], LANES), weight.shape[0])
-    value = jnp.dot(tokens[:, window], weight[...], preferred_element_type=F32).astype(BF16)
-    split = rows // 2
-    wide = features + LANES
-    for i, out in enumerate(sends):
-        here = slice(i % 2 * split, (i % 2 + 1) * split) if i < 4 else slice(0, rows)
-        out[:, :features] = tokens[here, :]
-        out[:, features:wide] = notes[here]
-        if i < 2:
-            out[:, wide:] = value[here]
-
-
-def first_step(start, shift, shifts, tokens, ids, gates, weights, width):
-    rows, features = tokens.shape
-    split, wide = rows // 2, features + LANES
+    value = jnp.dot(tokens[:, window], weight[...], preferred_element_type=F32)
+    sums[...] = value.astype(BF16)
+
+
+def first_step(start, shift, shifts, tokens, weights, width):
     inner = weights[0].shape[1]
-    outs = [(width, 4 * inner), (width, 2 * inner)]
-    outs += [(split, wide + 4 * inner)] * 2 + [(split, wide)] * 2 + [(rows, wide)]
+    outs = [(width, 4 * inner), (width, 2 * inner), (tokens.shape[0], 4 * inner)]
     outs = [jax.ShapeDtypeStruct(shape, BF16) for shape in outs]
     smem = pl.BlockSpec(memory_space=pltpu.SMEM)
-    arrays = [tokens, ids, gates, *weights]
+    arrays = [tokens, *weights]
     return pl.pallas_call(
         functools.partial(first_kernel, shifts),
         out_shape=outs,
@@ -203,7 +200,7 @@
         in_specs=[smem, smem] + [whole(a) for a in arrays],
         out_specs=[whole(o) for o in outs],
         compiler_params=params(60),
-        cost_estimate=cost(),
+        cost_estimate=cost(100000000000),
         name="first_step",
     )(start, shift, *arrays)
 
@@ -215,9 +212,7 @@
     piece = jnp.concatenate([on[:, window], back[:, window]], axis=0)
     value = jnp.dot(piece, weight[...], preferred_element_type=F32)
     for i, arrived in enumerate((on, back)):
-        part = value[i * height : (i + 1) * height]
-        if arrived.shape[1] > wide:
-            part = part + arrived[:, wide:].astype(F32)
+        part = value[i * height : (i + 1) * height] + arrived[:, wide:].astype(F32)
         if sends[i]:
             outs[i][:, :wide] = arrived[:, :wide]
             outs[i][:, wide:] = part.astype(BF16)
@@ -230,7 +225,7 @@
             at += r.shape[0]
 
 
-def step_on(start, weight, on, back, wide, sends, others=()):
+def step_on(start, weight, on, back, wide, sends, others):
     height, width = on.shape[0], weight.shape[1]
     vmem = pl.BlockSpec(memory_space=pltpu.VMEM)
     shapes = [(height, wide + width) if full else (height, width) for full in sends]
@@ -242,9 +237,66 @@
         in_specs=[pl.BlockSpec(memory_space=pltpu.SMEM)] + [vmem] * (3 + len(others)),
         out_specs=[vmem] * len(shapes),
         compiler_params=params(16),
-        cost_estimate=cost(),
+        cost_estimate=cost(10000000000),
         name="step_on",
     )(start, weight, on, back, *others)
+
+
+def open_kernel(start, weight, *refs):
+    on, back, terms, outs = refs[:2], refs[2:4], refs[4], refs[5:]
+    pair = outs[2]
+    height, wide = on[0].shape
+    window = pl.ds(pl.multiple_of(start[0], LANES), weight.shape[0])
+    piece = jnp.concatenate([r[:, window] for r in (*on, *back)], axis=0)
+    value = jnp.dot(piece, weight[...], preferred_element_type=F32)
+    terms[...] = value[: 2 * height]
+    for i, r in enumerate(back):
+        outs[i][:, :wide] = r[...]
+        outs[i][:, wide:] = value[(2 + i) * height : (3 + i) * height].astype(BF16)
+    for i, r in enumerate((on[0], back[0], on[1], back[1])):
+        pair[i * height : (i + 1) * height, :] = r[...]
+
+
+def open_step(start, weight, on, back):
+    height, wide = on[0].shape
+    width = weight.shape[1]
+    outs = [jax.ShapeDtypeStruct((2 * height, width), F32)]
+    outs += [jax.ShapeDtypeStruct((height, wide + width), BF16)] * 2
+    outs += [jax.ShapeDtypeStruct((4 * height, wide), BF16)]
+    vmem = pl.BlockSpec(memory_space=pltpu.VMEM)
+    return pl.pallas_call(
+        open_kernel,
+        out_shape=outs,
+        in_specs=[pl.BlockSpec(memory_space=pltpu.SMEM)] + [vmem] * 5,
+        out_specs=[vmem] * 4,
+        compiler_params=params(16),
+        cost_estimate=cost(100000000000),
+        name="open_step",
+    )(start, weight, *on, *back)
+
+
+def onward_kernel(terms, sums, *refs):
+    on, outs = refs[:2], refs[2:]
+    height, wide = on[0].shape
+    for i, r in enumerate(on):
+        here = slice(i * height, (i + 1) * height)
+        outs[i][:, :wide] = r[...]
+        outs[i][:, wide:] = (terms[here, :] + sums[here, :].astype(F32)).astype(BF16)
+
+
+def onward_step(terms, sums, on):
+    height, wide = on[0].shape
+    vmem = pl.BlockSpec(memory_space=pltpu.VMEM)
+    out = jax.ShapeDtypeStruct((height, wide + sums.shape[1]), BF16)
+    return pl.pallas_call(
+        onward_kernel,
+        out_shape=[out] * 2,
+        in_specs=[vmem] * 4,
+        out_specs=[vmem] * 2,
+        compiler_params=params(16),
+        cost_estimate=cost(10000000000),
+        name="onward_step",
+    )(terms, sums, *on)
 
 
 def last_kernel(wide, start, weight, main, side, *refs):
@@ -270,7 +322,7 @@
         in_specs=[pl.BlockSpec(memory_space=pltpu.SMEM)] + [vmem] * (3 + len(others)),
         out_specs=[vmem] * (1 + len(others)),
         compiler_params=params(16),
-        cost_estimate=cost(),
+        cost_estimate=cost(7000000000),
         name="last_step",
     )(start, weight, main, side, *others)
 
@@ -303,12 +355,12 @@
         in_specs=[whole(a) for a in arrays],
         out_specs=[whole(o) for o in outs],
         compiler_params=params(36),
-        cost_estimate=cost(),
+        cost_estimate=cost(100000000000),
         name="merge_rows",
     )(*arrays)
 
 
-def add_kernel(places, base, counts, joined, start, own, other, down, *refs):
+def add_kernel(places, base, counts, joined, narrow, start, own, other, down, *refs):
     arrived, outs, total = refs[: sum(counts)], refs[sum(counts) : -1], refs[-1]
     features = own.shape[1]
     height = total.shape[0] // len(places)
@@ -333,14 +385,15 @@
     )
     total[:, window] = total[:, window] + value
     if joined:
-        outs[0][...] = total[...].astype(BF16)
+        outs[0][...] = total[...]
     else:
         for i, out in enumerate(outs):
             out[:, :features] = total[i * height : (i + 1) * height, :].astype(BF16)
-            out[:, features:] = units[i]
-
-
-def add_step(start, term, down, places, arrived, joined=False):
+            if not narrow:
+                out[:, features:] = units[i]
+
+
+def add_step(start, term, down, places, arrived, joined=False, narrow=False):
     own, other, base = term
     features = own.shape[1]
     counts = [len(a) for a in arrived]
@@ -348,20 +401,40 @@
     count = len(places)
     vmem = pl.BlockSpec(memory_space=pltpu.VMEM)
     if joined:
-        outs = [jax.ShapeDtypeStruct((count * height, features), BF16)]
+        outs = [jax.ShapeDtypeStruct((count * height, features), F32)]
     else:
-        shape = (height, features + down.shape[1])
+        shape = (height, features + (0 if narrow else down.shape[1]))
         outs = [jax.ShapeDtypeStruct(shape, BF16)] * count
     return pl.pallas_call(
-        functools.partial(add_kernel, places, base, counts, joined),
+        functools.partial(add_kernel, places, base, counts, joined, narrow),
         out_shape=outs,
         in_specs=[pl.BlockSpec(memory_space=pltpu.SMEM)] + [vmem] * (3 + sum(counts)),
         out_specs=[vmem] * len(outs),
         scratch_shapes=[pltpu.VMEM((count * height, features), F32)],
         compiler_params=params(16),
-        cost_estimate=cost(),
+        cost_estimate=cost(100000000000),
         name="add_step",
     )(start, own, other, down, *[a for b in arrived for a in b])
+
+
+def join_kernel(sums, first, second, out):
+    height, features = first.shape[0], out.shape[1]
+    for i, r in enumerate((first, second)):
+        here = slice(i * height, (i + 1) * height)
+        out[here, :] = (sums[here, :] + r[:, :features].astype(F32)).astype(BF16)
+
+
+def join(sums, arrived):
+    vmem = pl.BlockSpec(memory_space=pltpu.VMEM)
+    return pl.pallas_call(
+        join_kernel,
+        out_shape=jax.ShapeDtypeStruct(sums.shape, BF16),
+        in_specs=[vmem] * 3,
+        out_specs=vmem,
+        compiler_params=params(16),
+        cost_estimate=cost(100000000000),
+        name="join",
+    )(sums, *arrived)
 
 
 def window_width(count, size, total):
@@ -404,41 +477,44 @@
     start = start.reshape(1)
     shifts = {i * size - min(i * size // LANES * LANES, features - width) for i in range(n)}
     weights = [f for w in (shared_gate, shared_up, shared_down.T) for f in (w, swap(w))]
-    both, down, *sends = first_step(
-        start, shift, sorted(shifts), tokens, route_ids.T, route_gates.T, weights, width
-    )
-
     after = lambda x, y: lax.optimization_barrier((x, y))[0]
     split = row_count // 2
-    tokens = sends[4]
+    *parts, tokens = note_tokens(tokens, route_ids.T, route_gates.T)
     wide = tokens.shape[1]
-    ahead, behind = [send_on(p) for p in sends[:2]], [send_back(p) for p in sends[2:4]]
-    pick = lambda arrays, cut=0: pick_rows(first, arrays, experts, slots, top, cut)
+    ahead, behind = [send_on(p) for p in parts], [send_back(p) for p in parts]
+    own = swap(tokens)
+    first_start = after(start, own)
+    both, down, sums = first_step(first_start, shift, sorted(shifts), tokens, weights, width)
+    sums = send_on(sums)
+    pick = lambda arrays, work=10000000000: pick_rows(first, arrays, experts, slots, top, work)
     pairs, picked = {}, {}
-    done = tokens
-    for k in range(1, half):
+    terms, *sends, pair = open_step(after(start, down), both, ahead, behind)
+    pairs[1] = [pair, swap(pair)]
+    behind = [send_back(m) for m in sends]
+    sends = onward_step(terms, sums, ahead)
+    ahead = [send_on(m) for m in sends]
+    done = sends[0]
+    for k in range(2, half):
         others = []
         for stream in (0, 1):
             full = (k < half - 1 or stream == 0, k < half - 1 or stream == 1)
             on, back = ahead[stream], behind[stream]
-            if stream and k == 1:
-                others = [tokens] + others
-            sends = step_on(start, after(both, done), on, back, wide, full, others)
+            sends = step_on(after(start, done), both, on, back, wide, full, others)
             done = sends[0]
             ahead[stream], behind[stream] = send_on(sends[0]), send_back(sends[1])
             others = [on, back]
-            if stream == 0 and k > 1:
-                picked[k - 1] = pick([after(pairs[k - 1][0], done), pairs[k - 1][1]], -row_count if k == 2 else 0)
+            if stream == 0:
+                picked[k - 1] = pick([after(pairs[k - 1][0], done), pairs[k - 1][1]])
                 done = picked[k - 1][1]
         pairs[k] = [sends[2], swap(sends[2])]
     main = [ahead[0], behind[1]]
-    [upper] = last_step(start, after(both, done), main[0], behind[0], wide)
+    [upper] = last_step(after(start, done), both, main[0], behind[0], wide)
     k = half - 1
-    picked[k] = pick([after(pairs[k][0], upper), pairs[k][1]])
+    picked[k] = pick([after(pairs[k][0], upper), pairs[k][1]], work=1000)
     done = picked[k][1]
-    lower, end = last_step(start, after(both, done), main[1], ahead[1], wide, main[:1])
+    lower, end = last_step(after(start, done), both, main[1], ahead[1], wide, main[:1])
     units = upper, lower
-    picked[0] = pick([pairs[1][0], end, pairs[1][1], swap(end)], row_count)
+    picked[0] = pick([tokens, end, own, swap(end)])
 
     lag = send_on(units[1]), send_back(units[0])
     routed = {}
@@ -456,26 +532,26 @@
         return {c: (own, other, i * block) for i, (c, own) in enumerate(zip(chunks, owns))}
 
     block = 2 * row_count
-    terms = terms_of([0, half - 1], lag)
-    lead = add_step(
-        start, terms[0], down, (row_count, row_count + split), [[units[0]], [units[1]]]
-    )
+    terms = terms_of([0], lag)
+    terms.update(terms_of([half - 1], terms[0][0]))
+    places, done = (row_count, row_count + split), terms[half - 1][0]
+    lead = add_step(after(start, done), terms[0], down, places, [[units[0]], [units[1]]])
     done = lead[0]
     lead = send_on(lead[0]), send_back(lead[1])
     for k in range(half - 1, 0, -1):
-        lag = add_step(start, terms[k], after(down, done), (3 * split, 0), [[lag[0]], [lag[1]]])
+        lag = add_step(after(start, done), terms[k], down, (3 * split, 0), [[lag[0]], [lag[1]]])
         done = lag[0]
         lag = send_on(lag[0]), send_back(lag[1])
         if k > 1 and k - 1 not in terms:
             terms.update(terms_of([k - 1, k - 2] if k > 2 else [k - 1], done))
-            done = terms[k - 1][1]
-        lead = add_step(
-            start, terms[k], after(down, done), (split, 2 * split), [[lead[0]], [lead[1]]]
-        )
+            done = terms[k - 1][0]
+        places, arrived = (split, 2 * split), [[lead[0]], [lead[1]]]
+        lead = add_step(after(start, done), terms[k], down, places, arrived, narrow=k == 1)
         done = lead[0]
         lead = send_on(lead[0]), send_back(lead[1])
-    arrived = [[lead[0], lag[1]], [lag[0], lead[1]]]
-    return add_step(start, terms[0], after(down, done), (0, split), arrived, joined=True)[0]
+    arrived = [[lag[1]], [lag[0]]]
+    [sums] = add_step(after(start, done), terms[0], down, (0, split), arrived, joined=True)
+    return join(sums, lead)
 
 
 def solution(mesh):

time: 177 us -> 156 us (0.88)
  waiting for transfers between devices: 87.1 us -> 58.7 us
  starting transfers between devices: 35.2 us -> 40.3 us
  local copies, waits for them, and re-layouts: 3.8 us -> 6.65 us
    ppermute x16 -> x17, waiting for transfers between devices: 41.6 us -> 23.6 us  [on_device(): send_on = lambda a: lax.ppermute(a, 'expert', onward)]
    ppermute x16, starting transfers between devices: 6.82 us -> 13.5 us  [on_device(): send_back = lambda a: lax.ppermute(a, 'expert', backward)]
    ppermute x9 -> x11, waiting for transfers between devices: 6.23 us -> 0.77 us  [on_device(): swap = lambda a: lax.ppermute(a, 'tensor', [(0, 1), (1, 0)])]
    pallas_call x6 -> x4, Pallas kernels: 7.18 us -> 1.95 us  [step_on(): pl.pallas_call(functools.partial(step_kernel, wide, sends), out_shape=[ja...]
    ppermute x16, waiting for transfers between devices: 39.2 us -> 34.4 us  [on_device(): send_back = lambda a: lax.ppermute(a, 'expert', backward)]
    unnamed x16 -> x42, local copies, waits for them, and re-layouts: 3.8 us -> 6.65 us
    pallas_call x8, Pallas kernels: 5.08 us -> 7.84 us  [add_step(): pl.pallas_call(functools.partial(add_kernel, places, base, counts, joined...]
    pallas_call x4 -> x8, Pallas kernels: 8.06 us -> 10.3 us  [the longest x4 5.35 us: pick_rows(): pl.pallas_call(functools.partial(pick_kernel, len(tokens), experts, top),...]
  transfers between devices with their start and end apart: 41 -> 44, of which waited for: 29 -> 23; matrix products, arithmetic and copies ran while one was open for 0% -> 0% of each run, Pallas kernels for 8% -> 16%
where the time goes in v3:
time: 156 us
  waiting for transfers between devices  58.7 us (38%)
  Pallas kernels  49.5 us (32%)
  starting transfers between devices  40.3 us (26%)
  local copies, waits for them, and re-layouts  6.65 us (4%)
    ppermute x16, waiting for transfers between devices, on_device(): send_back = lambda a: lax.ppermute(a, 'expert', backward)  34.4 us
    ppermute x17, starting transfers between devices, on_device(): send_on = lambda a: lax.ppermute(a, 'expert', onward)  24.9 us
    ppermute x17, waiting for transfers between devices, on_device(): send_on = lambda a: lax.ppermute(a, 'expert', onward)  23.6 us
    pallas_call x1, Pallas kernels, run_experts(): pl.pallas_call(functools.partial(expert_kernel, count, top), out_shape=[j...  20.4 us
    ppermute x16, starting transfers between devices, on_device(): send_back = lambda a: lax.ppermute(a, 'expert', backward)  13.5 us
    pallas_call x8, Pallas kernels, add_step(): pl.pallas_call(functools.partial(add_kernel, places, base, counts, joined...  7.84 us
    unnamed x42, local copies, waits for them, and re-layouts  6.65 us
    pallas_call x4, Pallas kernels, pick_rows(): pl.pallas_call(functools.partial(pick_kernel, len(tokens), experts, top),...  5.35 us
  transfers between devices with their start and end apart: 44, of which 23 were waited for; matrix products, arithmetic and copies ran while one was open for 0% of the time, Pallas kernels for 16%

profile of v3, /device:TPU:0, one launch (start us, length us, event | category | flops | bytes accessed | tf_op | source)
XLA Modules:
  0.0 155.6 jit_solution(16727219957188099823)
XLA Ops:
  0.0 2.1 %note_tokens.1 = (bf16[32,3712]{1,0:T(8,128)(2,1)}, bf16[32,3712]{1,0:T(8,128)(2,1)}, bf16[64,3712]{1,0:T(8,128)(2,1)}) custom-call(bf16[64,3584]{1,0:T(8,128)(2,1)} %tokens.1, s32[8,64]{1,0:T(8,128)} %bitcast.6, f32[8,64]{1,0:T(8,128)} %bitcast.7), custom_call_target="tpu_custom_call" | custom-call | flops 1000 | bytes 1000 | tf_op jit(solution)/shard_map/note_tokens/pallas_call | solution.py:156
  3.1 3.0 %collective-permute-start.4 = (bf16[32,3712]{1,0:T(8,128)(2,1)}, bf16[32,3712]{1,0:T(8,128)(2,1)S(1)}, u32[]{:S(2)}, u32[]{:S(2)}) collective-permute-start(bf16[32,3712]{1,0:T(8,128)(2,1)} %get-tuple-element.89), channel_id=1, source_target_pairs={{0,4},{4,8},{8,12},{12,14},{14,10},{10,6},{6,2},{2,0},{1,5},{5,9},... | collective-permute-start | bytes 712712 | tf_op jit(solution)/shard_map/ppermute | solution.py:467
  9.9 3.8 %first_step.1 = (bf16[512,2048]{1,0:T(8,128)(2,1)}, bf16[512,1024]{1,0:T(8,128)(2,1)}, bf16[64,2048]{1,0:T(8,128)(2,1)}) custom-call(s32[1]{0:T(128)} %bitcast.start, s32[1]{0:T(128)} %bitcast.4.shift, bf16[64,3712]{1,0:T(8,128)(2,1)} %get-tuple-element.84.tokens.refs_0_, bf16[448,512]{1,0:T(8,128)(2,1)} %refs_0_.1, bf16[448,512]{1,0:T(8,128)(2,1)} %copy-done.19, ...), custom_call_target="tpu_custom_call" | custom-call | flops 99999997952 | bytes 1000 | tf_op jit(solution)/shard_map/first_step/pallas_call | solution.py:196
  14.8 3.1 %collective-permute-done.5.refs_1_ = bf16[32,3712]{1,0:T(8,128)(2,1)S(1)} collective-permute-done((bf16[32,3712]{1,0:T(8,128)(2,1)}, bf16[32,3712]{1,0:T(8,128)(2,1)S(1)}, u32[]{:S(2)}, u32[]{:S(2)}) %collective-permute-start.5) | collective-permute-done | bytes 237600 | tf_op jit(solution)/shard_map/ppermute | solution.py:467
  18.8 1.6 %copy-done.14 = bf16[512,2048]{1,0:T(8,128)(2,1)S(1)} copy-done((bf16[512,2048]{1,0:T(8,128)(2,1)S(1)}, bf16[512,2048]{1,0:T(8,128)(2,1)}, u32[]{:S(2)}) %copy-start.14) | copy-done | bytes 2097176
  21.6 1.4 collective-permute-start.10
  23.8 1.7 %collective-permute-start.9 = (bf16[32,5760]{1,0:T(8,128)(2,1)}, bf16[32,5760]{1,0:T(8,128)(2,1)S(1)}, u32[]{:S(2)}, u32[]{:S(2)}) collective-permute-start(bf16[32,5760]{1,0:T(8,128)(2,1)} %get-tuple-element.94), channel_id=1, source_target_pairs={{0,4},{4,8},{8,12},{12,14},{14,10},{10,6},{6,2},{2,0},{1,5},{5,9},... | collective-permute-start | bytes 1105928 | tf_op jit(solution)/shard_map/ppermute | solution.py:467
  25.9 1.7 %collective-permute-start.12 = (bf16[32,5760]{1,0:T(8,128)(2,1)S(1)}, bf16[32,5760]{1,0:T(8,128)(2,1)S(1)}, u32[]{:S(2)}, u32[]{:S(2)}) collective-permute-start(bf16[32,5760]{1,0:T(8,128)(2,1)S(1)} %get-tuple-element.101), channel_id=1, source_target_pairs={{0,4},{4,8},{8,12},{12,14},{14,10},{10,6},{6,2},{2,0},{1,5},{5,9},... | collective-permute-start | bytes 1105928 | tf_op jit(solution)/shard_map/ppermute | solution.py:467
  27.6 5.8 %collective-permute-done.10.back.refs_1_ = bf16[32,5760]{1,0:T(8,128)(2,1)S(1)} collective-permute-done((bf16[32,5760]{1,0:T(8,128)(2,1)}, bf16[32,5760]{1,0:T(8,128)(2,1)S(1)}, u32[]{:S(2)}, u32[]{:S(2)}) %collective-permute-start.10) | collective-permute-done | bytes 368672 | tf_op jit(solution)/shard_map/ppermute | solution.py:468
  33.4 2.2 %collective-permute-done.9.on.refs_0_ = bf16[32,5760]{1,0:T(8,128)(2,1)S(1)} collective-permute-done((bf16[32,5760]{1,0:T(8,128)(2,1)}, bf16[32,5760]{1,0:T(8,128)(2,1)S(1)}, u32[]{:S(2)}, u32[]{:S(2)}) %collective-permute-start.9) | collective-permute-done | bytes 368672 | tf_op jit(solution)/shard_map/ppermute | solution.py:467
  35.6 1.6 %copy-done.15 = bf16[512,2048]{1,0:T(8,128)(2,1)S(1)} copy-done((bf16[512,2048]{1,0:T(8,128)(2,1)S(1)}, bf16[512,2048]{1,0:T(8,128)(2,1)}, u32[]{:S(2)}) %copy-start.15) | copy-done | bytes 2097176
  37.7 1.8 %collective-permute-start.14 = (bf16[32,5760]{1,0:T(8,128)(2,1)S(1)}, bf16[32,5760]{1,0:T(8,128)(2,1)S(1)}, u32[]{:S(2)}, u32[]{:S(2)}) collective-permute-start(bf16[32,5760]{1,0:T(8,128)(2,1)S(1)} %get-tuple-element.97), channel_id=1, source_target_pairs={{0,4},{4,8},{8,12},{12,14},{14,10},{10,6},{6,2},{2,0},{1,5},{5,9},... | collective-permute-start | bytes 1105928 | tf_op jit(solution)/shard_map/ppermute | solution.py:467
  39.7 1.3 pick_rows.4
  41.1 2.4 %collective-permute-done.12.on = bf16[32,5760]{1,0:T(8,128)(2,1)S(1)} collective-permute-done((bf16[32,5760]{1,0:T(8,128)(2,1)S(1)}, bf16[32,5760]{1,0:T(8,128)(2,1)S(1)}, u32[]{:S(2)}, u32[]{:S(2)}) %collective-permute-start.12) | collective-permute-done | bytes 368672 | tf_op jit(solution)/shard_map/ppermute | solution.py:467
  44.1 1.8 %collective-permute-start.17 = (bf16[32,5760]{1,0:T(8,128)(2,1)S(1)}, bf16[32,5760]{1,0:T(8,128)(2,1)S(1)}, u32[]{:S(2)}, u32[]{:S(2)}) collective-permute-start(bf16[32,5760]{1,0:T(8,128)(2,1)S(1)} %get-tuple-element.104), channel_id=1, source_target_pairs={{0,4},{4,8},{8,12},{12,14},{14,10},{10,6},{6,2},{2,0},{1,5},{5,9},... | collective-permute-start | bytes 1105928 | tf_op jit(solution)/shard_map/ppermute | solution.py:467
  46.1 5.2 %collective-permute-done.14.on.refs_0_ = bf16[32,5760]{1,0:T(8,128)(2,1)S(1)} collective-permute-done((bf16[32,5760]{1,0:T(8,128)(2,1)S(1)}, bf16[32,5760]{1,0:T(8,128)(2,1)S(1)}, u32[]{:S(2)}, u32[]{:S(2)}) %collective-permute-start.14) | collective-permute-done | bytes 368672 | tf_op jit(solution)/shard_map/ppermute | solution.py:467
  51.9 1.8 %collective-permute-start.19 = (bf16[32,5760]{1,0:T(8,128)(2,1)S(1)}, bf16[32,5760]{1,0:T(8,128)(2,1)S(1)}, u32[]{:S(2)}, u32[]{:S(2)}) collective-permute-start(bf16[32,5760]{1,0:T(8,128)(2,1)S(1)} %get-tuple-element.107), channel_id=1, source_target_pairs={{0,4},{4,8},{8,12},{12,14},{14,10},{10,6},{6,2},{2,0},{1,5},{5,9},... | collective-permute-start | bytes 1105928 | tf_op jit(solution)/shard_map/ppermute | solution.py:467
  53.6 1.3 pick_rows.5
  55.0 4.3 %collective-permute-done.17.on = bf16[32,5760]{1,0:T(8,128)(2,1)S(1)} collective-permute-done((bf16[32,5760]{1,0:T(8,128)(2,1)S(1)}, bf16[32,5760]{1,0:T(8,128)(2,1)S(1)}, u32[]{:S(2)}, u32[]{:S(2)}) %collective-permute-start.17) | collective-permute-done | bytes 368672 | tf_op jit(solution)/shard_map/ppermute | solution.py:467
  59.8 1.7 %collective-permute-start.20 = (bf16[32,2048]{1,0:T(8,128)(2,1)S(1)}, bf16[32,2048]{1,0:T(8,128)(2,1)S(1)}, u32[]{:S(2)}, u32[]{:S(2)}) collective-permute-start(bf16[32,2048]{1,0:T(8,128)(2,1)S(1)} %get-tuple-element.115), channel_id=1, source_target_pairs={{4,0},{8,4},{12,8},{14,12},{10,14},{6,10},{2,6},{0,2},{5,1},{9,5},... | collective-permute-start | bytes 393224 | tf_op jit(solution)/shard_map/ppermute | solution.py:468
  61.9 1.7 %collective-permute-start.22 = (bf16[32,5760]{1,0:T(8,128)(2,1)S(1)}, bf16[32,5760]{1,0:T(8,128)(2,1)S(1)}, u32[]{:S(2)}, u32[]{:S(2)}) collective-permute-start(bf16[32,5760]{1,0:T(8,128)(2,1)S(1)} %get-tuple-element.119), channel_id=1, source_target_pairs={{4,0},{8,4},{12,8},{14,12},{10,14},{6,10},{2,6},{0,2},{5,1},{9,5},... | collective-permute-start | bytes 1105928 | tf_op jit(solution)/shard_map/ppermute | solution.py:468
  63.6 2.6 %collective-permute-done.20.side = bf16[32,2048]{1,0:T(8,128)(2,1)S(1)} collective-permute-done((bf16[32,2048]{1,0:T(8,128)(2,1)S(1)}, bf16[32,2048]{1,0:T(8,128)(2,1)S(1)}, u32[]{:S(2)}, u32[]{:S(2)}) %collective-permute-start.20) | collective-permute-done | bytes 131104 | tf_op jit(solution)/shard_map/ppermute | solution.py:468
  67.2 1.3 pick_rows.6
  68.5 1.4 copy-done
  69.9 3.7 %collective-permute-done.22.main = bf16[32,5760]{1,0:T(8,128)(2,1)S(1)} collective-permute-done((bf16[32,5760]{1,0:T(8,128)(2,1)S(1)}, bf16[32,5760]{1,0:T(8,128)(2,1)S(1)}, u32[]{:S(2)}, u32[]{:S(2)}) %collective-permute-start.22) | collective-permute-done | bytes 368672 | tf_op jit(solution)/shard_map/ppermute | solution.py:468
  74.2 1.7 %collective-permute-start.26 = (bf16[32,1024]{1,0:T(8,128)(2,1)S(1)}, bf16[32,1024]{1,0:T(8,128)(2,1)S(1)}, u32[]{:S(2)}, u32[]{:S(2)}) collective-permute-start(bf16[32,1024]{1,0:T(8,128)(2,1)S(1)} %last_step.2.refs_0_), channel_id=1, source_target_pairs={{4,0},{8,4},{12,8},{14,12},{10,14},{6,10},{2,6},{0,2},{5,1},{9,5},... | collective-permute-start | bytes 196616 | tf_op jit(solution)/shard_map/ppermute | solution.py:468
  76.3 1.3 pick_rows.7
  80.8 20.4 %run_experts.1 = (bf16[4,80,3584]{2,1,0:T(8,128)(2,1)S(1)}, bf16[4,80,3584]{2,1,0:T(8,128)(2,1)S(1)}, bf16[4,80,3584]{2,1,0:T(8,128)(2,1)S(1)}, bf16[4,80,3584]{2,1,0:T(8,128)(2,1)S(1)}) custom-call(s32[1]{0:T(128)} %bitcast.1.first, bf16[4,80,3712]{2,1,0:T(8,128)(2,1)S(1)} %get-tuple-element.124.refs_0_, ...), custom_call_target="tpu_custom_call" | custom-call | flops 99999997952 | bytes 1000 | tf_op jit(solution)/shard_map/run_experts/pallas_call | solution.py:118
  104.9 1.2 add_step.8
  107.0 1.2 add_step.9
  108.2 1.6 %collective-permute-start.32 = (bf16[32,4608]{1,0:T(8,128)(2,1)}, bf16[32,4608]{1,0:T(8,128)(2,1)}, u32[]{:S(2)}, u32[]{:S(2)}) collective-permute-start(bf16[32,4608]{1,0:T(8,128)(2,1)} %get-tuple-element.138), channel_id=1, source_target_pairs={{0,4},{4,8},{8,12},{12,14},{14,10},{10,6},{6,2},{2,0},{1,5},{5,9},... | collective-permute-start | bytes 884744 | tf_op jit(solution)/shard_map/ppermute | solution.py:467
  110.2 2.1 %merge_rows.5 = (f32[128,3584]{1,0:T(8,128)S(1)}, f32[128,3584]{1,0:T(8,128)S(1)}, bf16[256,3584]{1,0:T(8,128)(2,1)S(1)}) custom-call(bf16[256,320]{1,0:T(8,128)(2,1)S(1)} %get-tuple-element.139.refs_0_, bf16[256,320]{1,0:T(8,128)(2,1)S(1)} %get-tuple-element.99.refs_1_, bf16[4,80,3584]{2,1,0:T(8,128)(2,1)S(1)} %get-tuple-element.140.refs_2_, ...), custom_call_target="tpu_custom_call" | custom-call | flops 99999997952 | bytes 1000 | tf_op jit(solution)/shard_map/merge_rows/pallas_call | solution.py:351
  112.4 1.3 collective-permute-start.33
  113.6 2.7 %collective-permute-done.29.refs_0_ = bf16[32,4608]{1,0:T(8,128)(2,1)} collective-permute-done((bf16[32,4608]{1,0:T(8,128)(2,1)}, bf16[32,4608]{1,0:T(8,128)(2,1)}, u32[]{:S(2)}, u32[]{:S(2)}) %collective-permute-start.29) | collective-permute-done | bytes 294944 | tf_op jit(solution)/shard_map/ppermute | solution.py:467
  116.3 3.4 %collective-permute-done.30.refs_1_ = bf16[32,4608]{1,0:T(8,128)(2,1)S(1)} collective-permute-done((bf16[32,4608]{1,0:T(8,128)(2,1)S(1)}, bf16[32,4608]{1,0:T(8,128)(2,1)S(1)}, u32[]{:S(2)}, u32[]{:S(2)}) %collective-permute-start.30) | collective-permute-done | bytes 294944 | tf_op jit(solution)/shard_map/ppermute | solution.py:468
  119.7 1.6 %add_step.10 = (bf16[32,4608]{1,0:T(8,128)(2,1)S(1)}, bf16[32,4608]{1,0:T(8,128)(2,1)S(1)}) custom-call(s32[1]{0:T(128)} %bitcast.start, f32[128,3584]{1,0:T(8,128)S(1)} %get-tuple-element.132.own, bf16[128,3584]{1,0:T(8,128)(2,1)S(1)} %collective-permute-done.28.other, bf16[512,1024]{1,0:T(8,128)(2,1)S(1)} %copy-done.17, ...), custom_call_target="tpu_custom_call" | custom-call | flops 99999997952 | bytes 1000 | tf_op jit(solution)/shard_map/add_step/pallas_call | solution.py:408
  121.3 1.6 %collective-permute-start.34 = (bf16[32,4608]{1,0:T(8,128)(2,1)S(1)}, bf16[32,4608]{1,0:T(8,128)(2,1)S(1)}, u32[]{:S(2)}, u32[]{:S(2)}) collective-permute-start(bf16[32,4608]{1,0:T(8,128)(2,1)S(1)} %get-tuple-element.145), channel_id=1, source_target_pairs={{0,4},{4,8},{8,12},{12,14},{14,10},{10,6},{6,2},{2,0},{1,5},{5,9},... | collective-permute-start | bytes 884744 | tf_op jit(solution)/shard_map/ppermute | solution.py:467
  123.4 2.6 %collective-permute-done.33.refs_1_ = bf16[32,4608]{1,0:T(8,128)(2,1)S(1)} collective-permute-done((bf16[32,4608]{1,0:T(8,128)(2,1)S(1)}, bf16[32,4608]{1,0:T(8,128)(2,1)S(1)}, u32[]{:S(2)}, u32[]{:S(2)}) %collective-permute-start.33) | collective-permute-done | bytes 294944 | tf_op jit(solution)/shard_map/ppermute | solution.py:468
  126.0 1.6 %add_step.11 = (bf16[32,4608]{1,0:T(8,128)(2,1)S(1)}, bf16[32,4608]{1,0:T(8,128)(2,1)S(1)}) custom-call(s32[1]{0:T(128)} %bitcast.start, f32[128,3584]{1,0:T(8,128)S(1)} %get-tuple-element.142.own, bf16[256,3584]{1,0:T(8,128)(2,1)S(1)} %collective-permute-done.31.other, bf16[512,1024]{1,0:T(8,128)(2,1)S(1)} %copy-done.17, ...), custom_call_target="tpu_custom_call" | custom-call | flops 99999997952 | bytes 1000 | tf_op jit(solution)/shard_map/add_step/pallas_call | solution.py:408
  127.7 1.6 %collective-permute-start.36 = (bf16[32,4608]{1,0:T(8,128)(2,1)S(1)}, bf16[32,4608]{1,0:T(8,128)(2,1)S(1)}, u32[]{:S(2)}, u32[]{:S(2)}) collective-permute-start(bf16[32,4608]{1,0:T(8,128)(2,1)S(1)} %get-tuple-element.149), channel_id=1, source_target_pairs={{0,4},{4,8},{8,12},{12,14},{14,10},{10,6},{6,2},{2,0},{1,5},{5,9},... | collective-permute-start | bytes 884744 | tf_op jit(solution)/shard_map/ppermute | solution.py:467
  129.7 3.2 %collective-permute-done.35.refs_1_ = bf16[32,4608]{1,0:T(8,128)(2,1)S(1)} collective-permute-done((bf16[32,4608]{1,0:T(8,128)(2,1)S(1)}, bf16[32,4608]{1,0:T(8,128)(2,1)S(1)}, u32[]{:S(2)}, u32[]{:S(2)}) %collective-permute-start.35) | collective-permute-done | bytes 294944 | tf_op jit(solution)/shard_map/ppermute | solution.py:468
  133.4 1.6 %collective-permute-start.38 = (bf16[32,4608]{1,0:T(8,128)(2,1)S(1)}, bf16[32,4608]{1,0:T(8,128)(2,1)S(1)}, u32[]{:S(2)}, u32[]{:S(2)}) collective-permute-start(bf16[32,4608]{1,0:T(8,128)(2,1)S(1)} %get-tuple-element.152), channel_id=1, source_target_pairs={{0,4},{4,8},{8,12},{12,14},{14,10},{10,6},{6,2},{2,0},{1,5},{5,9},... | collective-permute-start | bytes 884744 | tf_op jit(solution)/shard_map/ppermute | solution.py:467
  136.7 2.5 %collective-permute-done.37.refs_1_ = bf16[32,4608]{1,0:T(8,128)(2,1)S(1)} collective-permute-done((bf16[32,4608]{1,0:T(8,128)(2,1)S(1)}, bf16[32,4608]{1,0:T(8,128)(2,1)S(1)}, u32[]{:S(2)}, u32[]{:S(2)}) %collective-permute-start.37) | collective-permute-done | bytes 294944 | tf_op jit(solution)/shard_map/ppermute | solution.py:468
  139.8 1.6 %collective-permute-start.41 = (bf16[32,4608]{1,0:T(8,128)(2,1)S(1)}, bf16[32,4608]{1,0:T(8,128)(2,1)S(1)}, u32[]{:S(2)}, u32[]{:S(2)}) collective-permute-start(bf16[32,4608]{1,0:T(8,128)(2,1)S(1)} %get-tuple-element.156), channel_id=1, source_target_pairs={{0,4},{4,8},{8,12},{12,14},{14,10},{10,6},{6,2},{2,0},{1,5},{5,9},... | collective-permute-start | bytes 884744 | tf_op jit(solution)/shard_map/ppermute | solution.py:467
  142.9 2.6 %collective-permute-done.39.refs_1_ = bf16[32,4608]{1,0:T(8,128)(2,1)S(1)} collective-permute-done((bf16[32,4608]{1,0:T(8,128)(2,1)S(1)}, bf16[32,4608]{1,0:T(8,128)(2,1)S(1)}, u32[]{:S(2)}, u32[]{:S(2)}) %collective-permute-start.39) | collective-permute-done | bytes 294944 | tf_op jit(solution)/shard_map/ppermute | solution.py:468
  146.1 1.6 %collective-permute-start.42 = (bf16[32,3584]{1,0:T(8,128)(2,1)S(1)}, bf16[32,3584]{1,0:T(8,128)(2,1)S(1)}, u32[]{:S(2)}, u32[]{:S(2)}) collective-permute-start(bf16[32,3584]{1,0:T(8,128)(2,1)S(1)} %get-tuple-element.159), channel_id=1, source_target_pairs={{0,4},{4,8},{8,12},{12,14},{14,10},{10,6},{6,2},{2,0},{1,5},{5,9},... | collective-permute-start | bytes 688136 | tf_op jit(solution)/shard_map/ppermute | solution.py:467
  148.2 3.7 %collective-permute-done.40.refs_0_ = bf16[32,4608]{1,0:T(8,128)(2,1)S(1)} collective-permute-done((bf16[32,4608]{1,0:T(8,128)(2,1)S(1)}, bf16[32,4608]{1,0:T(8,128)(2,1)S(1)}, u32[]{:S(2)}, u32[]{:S(2)}) %collective-permute-start.40) | collective-permute-done | bytes 294944 | tf_op jit(solution)/shard_map/ppermute | solution.py:468
  152.4 2.3 %collective-permute-done.43.second = bf16[32,3584]{1,0:T(8,128)(2,1)S(1)} collective-permute-done((bf16[32,3584]{1,0:T(8,128)(2,1)S(1)}, bf16[32,3584]{1,0:T(8,128)(2,1)S(1)}, u32[]{:S(2)}, u32[]{:S(2)}) %collective-permute-start.43) | collective-permute-done | bytes 229408 | tf_op jit(solution)/shard_map/ppermute | solution.py:468
  (109 shorter events, 30.0 us)
Async XLA Ops:
  2.1 4.0 %collective-permute-start = (bf16[64,3712]{1,0:T(8,128)(2,1)}, bf16[64,3712]{1,0:T(8,128)(2,1)S(1)}, u32[]{:S(2)}, u32[]{:S(2)}) collective-permute-start(bf16[64,3712]{1,0:T(8,128)(2,1)} %get-tuple-element.84.tokens.refs_0_), channel_id=1, source_target_pairs={{0,1},{1,0},{2,3},{3,2},{4,5},{5,4},{6,7},{7,6},{8,9},{9,8},{10,11... | collective-permute-start | bytes 1425416 | tf_op jit(solution)/shard_map/ppermute | solution.py:469
  2.5 4.6 %collective-permute-start.3 = (bf16[448,512]{1,0:T(8,128)(2,1)}, bf16[448,512]{1,0:T(8,128)(2,1)S(1)}, u32[]{:S(2)}, u32[]{:S(2)}) collective-permute-start(bf16[448,512]{1,0:T(8,128)(2,1)} %bitcast.8), channel_id=1, source_target_pairs={{0,1},{1,0},{2,3},{3,2},{4,5},{5,4},{6,7},{7,6},{8,9},{9,8},{10,11... | collective-permute-start | bytes 1376264 | tf_op jit(solution)/shard_map/ppermute | solution.py:469
  2.6 5.6 %collective-permute-start.1 = (bf16[448,512]{1,0:T(8,128)(2,1)}, bf16[448,512]{1,0:T(8,128)(2,1)S(1)}, u32[]{:S(2)}, u32[]{:S(2)}) collective-permute-start(bf16[448,512]{1,0:T(8,128)(2,1)} %refs_0_.1), channel_id=1, source_target_pairs={{0,1},{1,0},{2,3},{3,2},{4,5},{5,4},{6,7},{7,6},{8,9},{9,8},{10,11... | collective-permute-start | bytes 1376264 | tf_op jit(solution)/shard_map/ppermute | solution.py:469
  3.0 6.1 %collective-permute-start.2 = (bf16[448,512]{1,0:T(8,128)(2,1)}, bf16[448,512]{1,0:T(8,128)(2,1)S(1)}, u32[]{:S(2)}, u32[]{:S(2)}) collective-permute-start(bf16[448,512]{1,0:T(8,128)(2,1)} %refs_2_.1), channel_id=1, source_target_pairs={{0,1},{1,0},{2,3},{3,2},{4,5},{5,4},{6,7},{7,6},{8,9},{9,8},{10,11... | collective-permute-start | bytes 1376264 | tf_op jit(solution)/shard_map/ppermute | solution.py:469
  3.1 11.7 %collective-permute-start.4 = (bf16[32,3712]{1,0:T(8,128)(2,1)}, bf16[32,3712]{1,0:T(8,128)(2,1)S(1)}, u32[]{:S(2)}, u32[]{:S(2)}) collective-permute-start(bf16[32,3712]{1,0:T(8,128)(2,1)} %get-tuple-element.89), channel_id=1, source_target_pairs={{0,4},{4,8},{8,12},{12,14},{14,10},{10,6},{6,2},{2,0},{1,5},{5,9},... | collective-permute-start | bytes 712712 | tf_op jit(solution)/shard_map/ppermute | solution.py:467
  6.1 7.6 %copy-start.4 = (bf16[64,3712]{1,0:T(8,128)(2,1)}, bf16[64,3712]{1,0:T(8,128)(2,1)S(1)}, u32[]{:S(2)}) copy-start(bf16[64,3712]{1,0:T(8,128)(2,1)S(1)} %collective-permute-done.refs_2_) | copy-start | bytes 1425412
  6.1 11.8 %collective-permute-start.6 = (bf16[32,3712]{1,0:T(8,128)(2,1)}, bf16[32,3712]{1,0:T(8,128)(2,1)S(1)}, u32[]{:S(2)}, u32[]{:S(2)}) collective-permute-start(bf16[32,3712]{1,0:T(8,128)(2,1)} %get-tuple-element.89), channel_id=1, source_target_pairs={{4,0},{8,4},{12,8},{14,12},{10,14},{6,10},{2,6},{0,2},{5,1},{9,5},... | collective-permute-start | bytes 712712 | tf_op jit(solution)/shard_map/ppermute | solution.py:468
  7.1 10.9 %collective-permute-start.5 = (bf16[32,3712]{1,0:T(8,128)(2,1)}, bf16[32,3712]{1,0:T(8,128)(2,1)S(1)}, u32[]{:S(2)}, u32[]{:S(2)}) collective-permute-start(bf16[32,3712]{1,0:T(8,128)(2,1)} %get-tuple-element.90), channel_id=1, source_target_pairs={{0,4},{4,8},{8,12},{12,14},{14,10},{10,6},{6,2},{2,0},{1,5},{5,9},... | collective-permute-start | bytes 712712 | tf_op jit(solution)/shard_map/ppermute | solution.py:467
  8.1 10.7 %collective-permute-start.7 = (bf16[32,3712]{1,0:T(8,128)(2,1)}, bf16[32,3712]{1,0:T(8,128)(2,1)S(1)}, u32[]{:S(2)}, u32[]{:S(2)}) collective-permute-start(bf16[32,3712]{1,0:T(8,128)(2,1)} %get-tuple-element.90), channel_id=1, source_target_pairs={{4,0},{8,4},{12,8},{14,12},{10,14},{6,10},{2,6},{0,2},{5,1},{9,5},... | collective-permute-start | bytes 712712 | tf_op jit(solution)/shard_map/ppermute | solution.py:468
  13.7 9.3 %collective-permute-start.8 = (bf16[64,2048]{1,0:T(8,128)(2,1)}, bf16[64,2048]{1,0:T(8,128)(2,1)S(1)}, u32[]{:S(2)}, u32[]{:S(2)}) collective-permute-start(bf16[64,2048]{1,0:T(8,128)(2,1)} %get-tuple-element.93), channel_id=1, source_target_pairs={{0,4},{4,8},{8,12},{12,14},{14,10},{10,6},{6,2},{2,0},{1,5},{5,9},... | collective-permute-start | bytes 786440 | tf_op jit(solution)/shard_map/ppermute | solution.py:467
  21.6 11.7 %collective-permute-start.10 = (bf16[32,5760]{1,0:T(8,128)(2,1)}, bf16[32,5760]{1,0:T(8,128)(2,1)S(1)}, u32[]{:S(2)}, u32[]{:S(2)}) collective-permute-start(bf16[32,5760]{1,0:T(8,128)(2,1)} %get-tuple-element.96), channel_id=1, source_target_pairs={{4,0},{8,4},{12,8},{14,12},{10,14},{6,10},{2,6},{0,2},{5,1},{9,5},... | collective-permute-start | bytes 1105928 | tf_op jit(solution)/shard_map/ppermute | solution.py:468
  23.8 11.7 %collective-permute-start.9 = (bf16[32,5760]{1,0:T(8,128)(2,1)}, bf16[32,5760]{1,0:T(8,128)(2,1)S(1)}, u32[]{:S(2)}, u32[]{:S(2)}) collective-permute-start(bf16[32,5760]{1,0:T(8,128)(2,1)} %get-tuple-element.94), channel_id=1, source_target_pairs={{0,4},{4,8},{8,12},{12,14},{14,10},{10,6},{6,2},{2,0},{1,5},{5,9},... | collective-permute-start | bytes 1105928 | tf_op jit(solution)/shard_map/ppermute | solution.py:467
  25.5 14.2 %collective-permute-start.11 = (bf16[128,3712]{1,0:T(8,128)(2,1)S(1)}, bf16[128,3712]{1,0:T(8,128)(2,1)S(1)}, u32[]{:S(2)}, u32[]{:S(2)}) collective-permute-start(bf16[128,3712]{1,0:T(8,128)(2,1)S(1)} %get-tuple-element.98.refs_0_), channel_id=1, source_target_pairs={{0,1},{1,0},{2,3},{3,2},{4,5},{5,4},{6,7},{7,6},{8,9},{9,8},{10,11... | collective-permute-start | bytes 2850824 | tf_op jit(solution)/shard_map/ppermute | solution.py:469
  25.5 15.5 %collective-permute-start.13 = (bf16[32,5760]{1,0:T(8,128)(2,1)S(1)}, bf16[32,5760]{1,0:T(8,128)(2,1)S(1)}, u32[]{:S(2)}, u32[]{:S(2)}) collective-permute-start(bf16[32,5760]{1,0:T(8,128)(2,1)S(1)} %get-tuple-element.102), channel_id=1, source_target_pairs={{4,0},{8,4},{12,8},{14,12},{10,14},{6,10},{2,6},{0,2},{5,1},{9,5},... | collective-permute-start | bytes 1105928 | tf_op jit(solution)/shard_map/ppermute | solution.py:468
  25.9 17.6 %collective-permute-start.12 = (bf16[32,5760]{1,0:T(8,128)(2,1)S(1)}, bf16[32,5760]{1,0:T(8,128)(2,1)S(1)}, u32[]{:S(2)}, u32[]{:S(2)}) collective-permute-start(bf16[32,5760]{1,0:T(8,128)(2,1)S(1)} %get-tuple-element.101), channel_id=1, source_target_pairs={{0,4},{4,8},{8,12},{12,14},{14,10},{10,6},{6,2},{2,0},{1,5},{5,9},... | collective-permute-start | bytes 1105928 | tf_op jit(solution)/shard_map/ppermute | solution.py:467
  37.7 13.7 %collective-permute-start.14 = (bf16[32,5760]{1,0:T(8,128)(2,1)S(1)}, bf16[32,5760]{1,0:T(8,128)(2,1)S(1)}, u32[]{:S(2)}, u32[]{:S(2)}) collective-permute-start(bf16[32,5760]{1,0:T(8,128)(2,1)S(1)} %get-tuple-element.97), channel_id=1, source_target_pairs={{0,4},{4,8},{8,12},{12,14},{14,10},{10,6},{6,2},{2,0},{1,5},{5,9},... | collective-permute-start | bytes 1105928 | tf_op jit(solution)/shard_map/ppermute | solution.py:467
  39.4 12.0 %collective-permute-start.15 = (bf16[32,5760]{1,0:T(8,128)(2,1)S(1)}, bf16[32,5760]{1,0:T(8,128)(2,1)S(1)}, u32[]{:S(2)}, u32[]{:S(2)}) collective-permute-start(bf16[32,5760]{1,0:T(8,128)(2,1)S(1)} %get-tuple-element.106), channel_id=1, source_target_pairs={{4,0},{8,4},{12,8},{14,12},{10,14},{6,10},{2,6},{0,2},{5,1},{9,5},... | collective-permute-start | bytes 1105928 | tf_op jit(solution)/shard_map/ppermute | solution.py:468
  44.0 9.7 %collective-permute-start.16 = (bf16[128,3712]{1,0:T(8,128)(2,1)S(1)}, bf16[128,3712]{1,0:T(8,128)(2,1)S(1)}, u32[]{:S(2)}, u32[]{:S(2)}) collective-permute-start(bf16[128,3712]{1,0:T(8,128)(2,1)S(1)} %get-tuple-element.108.refs_0_), channel_id=1, source_target_pairs={{0,1},{1,0},{2,3},{3,2},{4,5},{5,4},{6,7},{7,6},{8,9},{9,8},{10,11... | collective-permute-start | bytes 2850824 | tf_op jit(solution)/shard_map/ppermute | solution.py:469
  44.1 15.2 %collective-permute-start.17 = (bf16[32,5760]{1,0:T(8,128)(2,1)S(1)}, bf16[32,5760]{1,0:T(8,128)(2,1)S(1)}, u32[]{:S(2)}, u32[]{:S(2)}) collective-permute-start(bf16[32,5760]{1,0:T(8,128)(2,1)S(1)} %get-tuple-element.104), channel_id=1, source_target_pairs={{0,4},{4,8},{8,12},{12,14},{14,10},{10,6},{6,2},{2,0},{1,5},{5,9},... | collective-permute-start | bytes 1105928 | tf_op jit(solution)/shard_map/ppermute | solution.py:467
  45.8 13.5 %collective-permute-start.18 = (bf16[32,5760]{1,0:T(8,128)(2,1)S(1)}, bf16[32,5760]{1,0:T(8,128)(2,1)S(1)}, u32[]{:S(2)}, u32[]{:S(2)}) collective-permute-start(bf16[32,5760]{1,0:T(8,128)(2,1)S(1)} %get-tuple-element.111), channel_id=1, source_target_pairs={{4,0},{8,4},{12,8},{14,12},{10,14},{6,10},{2,6},{0,2},{5,1},{9,5},... | collective-permute-start | bytes 1105928 | tf_op jit(solution)/shard_map/ppermute | solution.py:468
  51.9 14.8 %collective-permute-start.19 = (bf16[32,5760]{1,0:T(8,128)(2,1)S(1)}, bf16[32,5760]{1,0:T(8,128)(2,1)S(1)}, u32[]{:S(2)}, u32[]{:S(2)}) collective-permute-start(bf16[32,5760]{1,0:T(8,128)(2,1)S(1)} %get-tuple-element.107), channel_id=1, source_target_pairs={{0,4},{4,8},{8,12},{12,14},{14,10},{10,6},{6,2},{2,0},{1,5},{5,9},... | collective-permute-start | bytes 1105928 | tf_op jit(solution)/shard_map/ppermute | solution.py:467
  59.8 7.4 %collective-permute-start.21 = (bf16[128,3712]{1,0:T(8,128)(2,1)S(1)}, bf16[128,3712]{1,0:T(8,128)(2,1)S(1)}, u32[]{:S(2)}, u32[]{:S(2)}) collective-permute-start(bf16[128,3712]{1,0:T(8,128)(2,1)S(1)} %get-tuple-element.116.refs_0_), channel_id=1, source_target_pairs={{0,1},{1,0},{2,3},{3,2},{4,5},{5,4},{6,7},{7,6},{8,9},{9,8},{10,11... | collective-permute-start | bytes 2850824 | tf_op jit(solution)/shard_map/ppermute | solution.py:469
  59.8 6.3 %collective-permute-start.20 = (bf16[32,2048]{1,0:T(8,128)(2,1)S(1)}, bf16[32,2048]{1,0:T(8,128)(2,1)S(1)}, u32[]{:S(2)}, u32[]{:S(2)}) collective-permute-start(bf16[32,2048]{1,0:T(8,128)(2,1)S(1)} %get-tuple-element.115), channel_id=1, source_target_pairs={{4,0},{8,4},{12,8},{14,12},{10,14},{6,10},{2,6},{0,2},{5,1},{9,5},... | collective-permute-start | bytes 393224 | tf_op jit(solution)/shard_map/ppermute | solution.py:468
  61.6 8.4 %collective-permute-start.23 = (bf16[32,2048]{1,0:T(8,128)(2,1)S(1)}, bf16[32,2048]{1,0:T(8,128)(2,1)S(1)}, u32[]{:S(2)}, u32[]{:S(2)}) collective-permute-start(bf16[32,2048]{1,0:T(8,128)(2,1)S(1)} %get-tuple-element.113), channel_id=1, source_target_pairs={{0,4},{4,8},{8,12},{12,14},{14,10},{10,6},{6,2},{2,0},{1,5},{5,9},... | collective-permute-start | bytes 393224 | tf_op jit(solution)/shard_map/ppermute | solution.py:467
  61.9 11.7 %collective-permute-start.22 = (bf16[32,5760]{1,0:T(8,128)(2,1)S(1)}, bf16[32,5760]{1,0:T(8,128)(2,1)S(1)}, u32[]{:S(2)}, u32[]{:S(2)}) collective-permute-start(bf16[32,5760]{1,0:T(8,128)(2,1)S(1)} %get-tuple-element.119), channel_id=1, source_target_pairs={{4,0},{8,4},{12,8},{14,12},{10,14},{6,10},{2,6},{0,2},{5,1},{9,5},... | collective-permute-start | bytes 1105928 | tf_op jit(solution)/shard_map/ppermute | solution.py:468
  67.1 7.1 %copy-start.6 = (bf16[32,1024]{1,0:T(8,128)(2,1)}, bf16[32,1024]{1,0:T(8,128)(2,1)S(1)}, u32[]{:S(2)}) copy-start(bf16[32,1024]{1,0:T(8,128)(2,1)S(1)} %last_step.2.refs_0_) | copy-start | bytes 196612
  69.9 6.4 %copy-start.5 = (bf16[64,3712]{1,0:T(8,128)(2,1)S(1)}, bf16[64,3712]{1,0:T(8,128)(2,1)}, u32[]{:S(2)}) copy-start(bf16[64,3712]{1,0:T(8,128)(2,1)} %copy-done.4) | copy-start | bytes 1425412
  74.1 2.2 %collective-permute-start.24 = (bf16[64,3712]{1,0:T(8,128)(2,1)S(1)}, bf16[64,3712]{1,0:T(8,128)(2,1)S(1)}, u32[]{:S(2)}, u32[]{:S(2)}) collective-permute-start(bf16[64,3712]{1,0:T(8,128)(2,1)S(1)} %get-tuple-element.120.refs_1_), channel_id=1, source_target_pairs={{0,1},{1,0},{2,3},{3,2},{4,5},{5,4},{6,7},{7,6},{8,9},{9,8},{10,11... | collective-permute-start | bytes 1425416 | tf_op jit(solution)/shard_map/ppermute | solution.py:469
  74.2 4.5 %collective-permute-start.26 = (bf16[32,1024]{1,0:T(8,128)(2,1)S(1)}, bf16[32,1024]{1,0:T(8,128)(2,1)S(1)}, u32[]{:S(2)}, u32[]{:S(2)}) collective-permute-start(bf16[32,1024]{1,0:T(8,128)(2,1)S(1)} %last_step.2.refs_0_), channel_id=1, source_target_pairs={{4,0},{8,4},{12,8},{14,12},{10,14},{6,10},{2,6},{0,2},{5,1},{9,5},... | collective-permute-start | bytes 196616 | tf_op jit(solution)/shard_map/ppermute | solution.py:468
  75.9 4.3 %collective-permute-start.25 = (bf16[32,1024]{1,0:T(8,128)(2,1)S(1)}, bf16[32,1024]{1,0:T(8,128)(2,1)S(1)}, u32[]{:S(2)}, u32[]{:S(2)}) collective-permute-start(bf16[32,1024]{1,0:T(8,128)(2,1)S(1)} %get-tuple-element.122.refs_1_), channel_id=1, source_target_pairs={{0,4},{4,8},{8,12},{12,14},{14,10},{10,6},{6,2},{2,0},{1,5},{5,9},... | collective-permute-start | bytes 196616 | tf_op jit(solution)/shard_map/ppermute | solution.py:467
  102.3 2.5 %collective-permute-start.27 = (bf16[128,3584]{1,0:T(8,128)(2,1)S(1)}, bf16[128,3584]{1,0:T(8,128)(2,1)S(1)}, u32[]{:S(2)}, u32[]{:S(2)}) collective-permute-start(bf16[128,3584]{1,0:T(8,128)(2,1)S(1)} %get-tuple-element.134), channel_id=1, source_target_pairs={{0,1},{1,0},{2,3},{3,2},{4,5},{5,4},{6,7},{7,6},{8,9},{9,8},{10,11... | collective-permute-start | bytes 2752520 | tf_op jit(solution)/shard_map/ppermute | solution.py:469
  103.6 3.4 %collective-permute-start.28 = (bf16[128,3584]{1,0:T(8,128)(2,1)S(1)}, bf16[128,3584]{1,0:T(8,128)(2,1)S(1)}, u32[]{:S(2)}, u32[]{:S(2)}) collective-permute-start(bf16[128,3584]{1,0:T(8,128)(2,1)S(1)} %get-tuple-element.137), channel_id=1, source_target_pairs={{0,1},{1,0},{2,3},{3,2},{4,5},{5,4},{6,7},{7,6},{8,9},{9,8},{10,11... | collective-permute-start | bytes 2752520 | tf_op jit(solution)/shard_map/ppermute | solution.py:469
  106.1 10.2 %collective-permute-start.29 = (bf16[32,4608]{1,0:T(8,128)(2,1)}, bf16[32,4608]{1,0:T(8,128)(2,1)}, u32[]{:S(2)}, u32[]{:S(2)}) collective-permute-start(bf16[32,4608]{1,0:T(8,128)(2,1)} %get-tuple-element.135), channel_id=1, source_target_pairs={{0,4},{4,8},{8,12},{12,14},{14,10},{10,6},{6,2},{2,0},{1,5},{5,9},... | collective-permute-start | bytes 884744 | tf_op jit(solution)/shard_map/ppermute | solution.py:467
  108.2 15.2 %collective-permute-start.32 = (bf16[32,4608]{1,0:T(8,128)(2,1)}, bf16[32,4608]{1,0:T(8,128)(2,1)}, u32[]{:S(2)}, u32[]{:S(2)}) collective-permute-start(bf16[32,4608]{1,0:T(8,128)(2,1)} %get-tuple-element.138), channel_id=1, source_target_pairs={{0,4},{4,8},{8,12},{12,14},{14,10},{10,6},{6,2},{2,0},{1,5},{5,9},... | collective-permute-start | bytes 884744 | tf_op jit(solution)/shard_map/ppermute | solution.py:467
  109.8 9.9 %collective-permute-start.30 = (bf16[32,4608]{1,0:T(8,128)(2,1)S(1)}, bf16[32,4608]{1,0:T(8,128)(2,1)S(1)}, u32[]{:S(2)}, u32[]{:S(2)}) collective-permute-start(bf16[32,4608]{1,0:T(8,128)(2,1)S(1)} %get-tuple-element.144), channel_id=1, source_target_pairs={{4,0},{8,4},{12,8},{14,12},{10,14},{6,10},{2,6},{0,2},{5,1},{9,5},... | collective-permute-start | bytes 884744 | tf_op jit(solution)/shard_map/ppermute | solution.py:468
  112.3 13.7 %collective-permute-start.31 = (bf16[256,3584]{1,0:T(8,128)(2,1)S(1)}, bf16[256,3584]{1,0:T(8,128)(2,1)S(1)}, u32[]{:S(2)}, u32[]{:S(2)}) collective-permute-start(bf16[256,3584]{1,0:T(8,128)(2,1)S(1)} %get-tuple-element.147), channel_id=1, source_target_pairs={{0,1},{1,0},{2,3},{3,2},{4,5},{5,4},{6,7},{7,6},{8,9},{9,8},{10,11... | collective-permute-start | bytes 5505032 | tf_op jit(solution)/shard_map/ppermute | solution.py:469
  112.4 13.7 %collective-permute-start.33 = (bf16[32,4608]{1,0:T(8,128)(2,1)S(1)}, bf16[32,4608]{1,0:T(8,128)(2,1)S(1)}, u32[]{:S(2)}, u32[]{:S(2)}) collective-permute-start(bf16[32,4608]{1,0:T(8,128)(2,1)S(1)} %get-tuple-element.148), channel_id=1, source_target_pairs={{4,0},{8,4},{12,8},{14,12},{10,14},{6,10},{2,6},{0,2},{5,1},{9,5},... | collective-permute-start | bytes 884744 | tf_op jit(solution)/shard_map/ppermute | solution.py:468
  121.3 8.4 %collective-permute-start.34 = (bf16[32,4608]{1,0:T(8,128)(2,1)S(1)}, bf16[32,4608]{1,0:T(8,128)(2,1)S(1)}, u32[]{:S(2)}, u32[]{:S(2)}) collective-permute-start(bf16[32,4608]{1,0:T(8,128)(2,1)S(1)} %get-tuple-element.145), channel_id=1, source_target_pairs={{0,4},{4,8},{8,12},{12,14},{14,10},{10,6},{6,2},{2,0},{1,5},{5,9},... | collective-permute-start | bytes 884744 | tf_op jit(solution)/shard_map/ppermute | solution.py:467
  122.9 9.9 %collective-permute-start.35 = (bf16[32,4608]{1,0:T(8,128)(2,1)S(1)}, bf16[32,4608]{1,0:T(8,128)(2,1)S(1)}, u32[]{:S(2)}, u32[]{:S(2)}) collective-permute-start(bf16[32,4608]{1,0:T(8,128)(2,1)S(1)} %get-tuple-element.151), channel_id=1, source_target_pairs={{4,0},{8,4},{12,8},{14,12},{10,14},{6,10},{2,6},{0,2},{5,1},{9,5},... | collective-permute-start | bytes 884744 | tf_op jit(solution)/shard_map/ppermute | solution.py:468
  127.7 9.1 %collective-permute-start.36 = (bf16[32,4608]{1,0:T(8,128)(2,1)S(1)}, bf16[32,4608]{1,0:T(8,128)(2,1)S(1)}, u32[]{:S(2)}, u32[]{:S(2)}) collective-permute-start(bf16[32,4608]{1,0:T(8,128)(2,1)S(1)} %get-tuple-element.149), channel_id=1, source_target_pairs={{0,4},{4,8},{8,12},{12,14},{14,10},{10,6},{6,2},{2,0},{1,5},{5,9},... | collective-permute-start | bytes 884744 | tf_op jit(solution)/shard_map/ppermute | solution.py:467
  129.3 9.9 %collective-permute-start.37 = (bf16[32,4608]{1,0:T(8,128)(2,1)S(1)}, bf16[32,4608]{1,0:T(8,128)(2,1)S(1)}, u32[]{:S(2)}, u32[]{:S(2)}) collective-permute-start(bf16[32,4608]{1,0:T(8,128)(2,1)S(1)} %get-tuple-element.155), channel_id=1, source_target_pairs={{4,0},{8,4},{12,8},{14,12},{10,14},{6,10},{2,6},{0,2},{5,1},{9,5},... | collective-permute-start | bytes 884744 | tf_op jit(solution)/shard_map/ppermute | solution.py:468
  133.4 9.5 %collective-permute-start.38 = (bf16[32,4608]{1,0:T(8,128)(2,1)S(1)}, bf16[32,4608]{1,0:T(8,128)(2,1)S(1)}, u32[]{:S(2)}, u32[]{:S(2)}) collective-permute-start(bf16[32,4608]{1,0:T(8,128)(2,1)S(1)} %get-tuple-element.152), channel_id=1, source_target_pairs={{0,4},{4,8},{8,12},{12,14},{14,10},{10,6},{6,2},{2,0},{1,5},{5,9},... | collective-permute-start | bytes 884744 | tf_op jit(solution)/shard_map/ppermute | solution.py:467
  135.0 10.5 %collective-permute-start.39 = (bf16[32,4608]{1,0:T(8,128)(2,1)S(1)}, bf16[32,4608]{1,0:T(8,128)(2,1)S(1)}, u32[]{:S(2)}, u32[]{:S(2)}) collective-permute-start(bf16[32,4608]{1,0:T(8,128)(2,1)S(1)} %get-tuple-element.158), channel_id=1, source_target_pairs={{4,0},{8,4},{12,8},{14,12},{10,14},{6,10},{2,6},{0,2},{5,1},{9,5},... | collective-permute-start | bytes 884744 | tf_op jit(solution)/shard_map/ppermute | solution.py:468
  139.8 12.1 %collective-permute-start.41 = (bf16[32,4608]{1,0:T(8,128)(2,1)S(1)}, bf16[32,4608]{1,0:T(8,128)(2,1)S(1)}, u32[]{:S(2)}, u32[]{:S(2)}) collective-permute-start(bf16[32,4608]{1,0:T(8,128)(2,1)S(1)} %get-tuple-element.156), channel_id=1, source_target_pairs={{0,4},{4,8},{8,12},{12,14},{14,10},{10,6},{6,2},{2,0},{1,5},{5,9},... | collective-permute-start | bytes 884744 | tf_op jit(solution)/shard_map/ppermute | solution.py:467
  141.3 10.5 %copy-start.2 = (bf16[128,3584]{1,0:T(8,128)(2,1)S(1)}, bf16[128,3584]{1,0:T(8,128)(2,1)}, u32[]{:S(2)}) copy-start(bf16[128,3584]{1,0:T(8,128)(2,1)} %copy-done.1) | copy-start | bytes 2752516
  141.3 10.5 %collective-permute-start.40 = (bf16[32,4608]{1,0:T(8,128)(2,1)S(1)}, bf16[32,4608]{1,0:T(8,128)(2,1)S(1)}, u32[]{:S(2)}, u32[]{:S(2)}) collective-permute-start(bf16[32,4608]{1,0:T(8,128)(2,1)S(1)} %get-tuple-element.161), channel_id=1, source_target_pairs={{4,0},{8,4},{12,8},{14,12},{10,14},{6,10},{2,6},{0,2},{5,1},{9,5},... | collective-permute-start | bytes 884744 | tf_op jit(solution)/shard_map/ppermute | solution.py:468
  146.1 6.3 %collective-permute-start.42 = (bf16[32,3584]{1,0:T(8,128)(2,1)S(1)}, bf16[32,3584]{1,0:T(8,128)(2,1)S(1)}, u32[]{:S(2)}, u32[]{:S(2)}) collective-permute-start(bf16[32,3584]{1,0:T(8,128)(2,1)S(1)} %get-tuple-element.159), channel_id=1, source_target_pairs={{0,4},{4,8},{8,12},{12,14},{14,10},{10,6},{6,2},{2,0},{1,5},{5,9},... | collective-permute-start | bytes 688136 | tf_op jit(solution)/shard_map/ppermute | solution.py:467
  147.6 7.1 %collective-permute-start.43 = (bf16[32,3584]{1,0:T(8,128)(2,1)S(1)}, bf16[32,3584]{1,0:T(8,128)(2,1)S(1)}, u32[]{:S(2)}, u32[]{:S(2)}) collective-permute-start(bf16[32,3584]{1,0:T(8,128)(2,1)S(1)} %get-tuple-element.162), channel_id=1, source_target_pairs={{4,0},{8,4},{12,8},{14,12},{10,14},{6,10},{2,6},{0,2},{5,1},{9,5},... | collective-permute-start | bytes 688136 | tf_op jit(solution)/shard_map/ppermute | solution.py:468
  (17 other events, 38.7 us)

commit v4 on v3

--- a/solution.py
+++ b/solution.py
@@ -84,30 +84,89 @@
     )(first, *tokens)
 
 
-def expert_kernel(count, top, first, *refs):
-    rows_in, (gate, up, down) = refs[:count], refs[count : count + 3]
-    rows_out, rows = refs[count + 3 : 2 * count + 3], refs[2 * count + 3]
+def expert_kernel(count, pieces, top, first, *refs):
+    rows_in, weights = refs[:count], refs[count : count + 3]
+    rows_out, refs = refs[count + 3 : 2 * count + 3], refs[2 * count + 3 :]
+    rows, held, sems, piece_sems = refs[0], refs[1:4], refs[4], refs[5]
     slots, wide = rows_in[0].shape[1:]
-    features = down.shape[2]
+    features = held[0].shape[1]
+    here = pl.program_id(0)
+    last = pl.num_programs(0) - 1
+    depth = features // pieces
+
+    def fetch(expert, which):
+        slot = lax.rem(expert, 2)
+        copy = pltpu.make_async_copy
+        return copy(weights[which].at[expert], held[which].at[slot], sems.at[slot, which])
+
+    def fetch_piece(at, which):
+        part = pl.ds(at * depth, depth)
+        copy = pltpu.make_async_copy
+        return copy(weights[which].at[0, part], held[which].at[0, part], piece_sems.at[at, which])
+
+    @pl.when(here == 0)
+    def _():
+        for at in range(pieces):
+            for which in range(2):
+                fetch_piece(at, which).start()
+        fetch(0, 2).start()
+
     for i, r in enumerate(rows_in):
-        rows[i * slots : (i + 1) * slots, :] = r[0]
+        rows[i * slots : (i + 1) * slots, :] = r[here]
     notes = rows[:, features:].astype(F32)
     lane = lax.broadcasted_iota(jnp.int32, notes.shape, 1)
-    expert = (first[0] + pl.program_id(0)).astype(F32)
+    expert = (first[0] + here).astype(F32)
     chosen = jnp.where((notes == expert) & (lane < top), 1.0, 0.0)
     scale = jnp.zeros((notes.shape[0], 1), F32)
     for part in (1, 2, 3):
         moved = jnp.concatenate([notes[:, part * top :], notes[:, : part * top]], axis=1)
         scale = scale + jnp.sum(chosen * moved, axis=1, keepdims=True)
-    value = rows[:, :features]
-    gated = jnp.dot(value, gate[0], preferred_element_type=F32)
-    upward = jnp.dot(value, up[0], preferred_element_type=F32)
-    hidden = (silu(gated) * upward * scale).astype(BF16)
-    for at, width in column_tiles(features):
-        done = jnp.dot(hidden, down[0, :, at : at + width], preferred_element_type=F32)
-        done = done.astype(BF16)
-        for i, r in enumerate(rows_out):
-            r[0, :, at : at + width] = done[i * slots : (i + 1) * slots]
+
+    def finish(gated, upward, down):
+        hidden = (silu(gated) * upward * scale).astype(BF16)
+        for at, width in column_tiles(features):
+            done = jnp.dot(hidden, down[:, at : at + width], preferred_element_type=F32)
+            done = done.astype(BF16)
+            for i, r in enumerate(rows_out):
+                r[here, :, at : at + width] = done[i * slots : (i + 1) * slots]
+
+    @pl.when(here == 0)
+    def _():
+        gated = upward = None
+        for at in range(pieces):
+            for which in range(2):
+                fetch_piece(at, which).wait()
+            if at == 1:
+
+                @pl.when(here < last)
+                def _():
+                    for which in range(3):
+                        fetch(1, which).start()
+
+            part = slice(at * depth, (at + 1) * depth)
+            value = rows[:, part]
+            g = jnp.dot(value, held[0][0, part], preferred_element_type=F32)
+            u = jnp.dot(value, held[1][0, part], preferred_element_type=F32)
+            gated, upward = (g, u) if at == 0 else (gated + g, upward + u)
+
+        fetch(0, 2).wait()
+        finish(gated, upward, held[2].at[0])
+
+    @pl.when(here > 0)
+    def _():
+        @pl.when(here < last)
+        def _():
+            for which in range(3):
+                fetch(here + 1, which).start()
+
+        slot = lax.rem(here, 2)
+        for which in range(2):
+            fetch(here, which).wait()
+        value = rows[:, :features]
+        gated = jnp.dot(value, held[0][slot], preferred_element_type=F32)
+        upward = jnp.dot(value, held[1][slot], preferred_element_type=F32)
+        fetch(here, 2).wait()
+        finish(gated, upward, held[2].at[slot])
 
 
 def run_experts(first, rows, gate, up, down, top):
@@ -115,23 +174,25 @@
     features, hidden = gate.shape[1:]
     count = len(rows)
     height = count * slots
-    return pl.pallas_call(
-        functools.partial(expert_kernel, count, top),
-        out_shape=[jax.ShapeDtypeStruct((experts, slots, features), BF16)] * count,
+    pieces = 7
+    vmem = pl.BlockSpec(memory_space=pltpu.VMEM)
+    rows = [pltpu.with_memory_space_constraint(r, pltpu.VMEM) for r in rows]
+    weights = [pltpu.with_memory_space_constraint(w, pltpu.HBM) for w in (gate, up, down)]
+    return pl.pallas_call(
+        functools.partial(expert_kernel, count, pieces, top),
+        out_shape=[pltpu.VMEM((experts, slots, features), BF16)] * count,
         grid=(experts,),
         in_specs=[pl.BlockSpec(memory_space=pltpu.SMEM)]
-        + [pl.BlockSpec((1, slots, wide), lambda e: (e, 0, 0))] * count
-        + [
-            pl.BlockSpec((1, features, hidden), lambda e: (e, 0, 0)),
-            pl.BlockSpec((1, features, hidden), lambda e: (e, 0, 0)),
-            pl.BlockSpec((1, hidden, features), lambda e: (e, 0, 0)),
-        ],
-        out_specs=[pl.BlockSpec((1, slots, features), lambda e: (e, 0, 0))] * count,
-        scratch_shapes=[pltpu.VMEM((height, wide), BF16)],
-        compiler_params=params(38),
+        + [vmem] * count
+        + [pl.BlockSpec(memory_space=pl.ANY)] * 3,
+        out_specs=[vmem] * count,
+        scratch_shapes=[pltpu.VMEM((height, wide), BF16)]
+        + [pltpu.VMEM((2, *w.shape[1:]), BF16) for w in (gate, up, down)]
+        + [pltpu.SemaphoreType.DMA((2, 3)), pltpu.SemaphoreType.DMA((pieces, 2))],
+        compiler_params=params(28),
         cost_estimate=cost(100000000000),
         name="run_experts",
-    )(first, *rows, gate, up, down)
+    )(first, *rows, *weights)
 
 
 def note_kernel(tokens, ids, gates, *sends):
@@ -355,7 +416,7 @@
         in_specs=[whole(a) for a in arrays],
         out_specs=[whole(o) for o in outs],
         compiler_params=params(36),
-        cost_estimate=cost(100000000000),
+        cost_estimate=cost(1000),
         name="merge_rows",
     )(*arrays)
 
@@ -532,7 +593,7 @@
         return {c: (own, other, i * block) for i, (c, own) in enumerate(zip(chunks, owns))}
 
     block = 2 * row_count
-    terms = terms_of([0], lag)
+    terms = terms_of([0], routed[0])
     terms.update(terms_of([half - 1], terms[0][0]))
     places, done = (row_count, row_count + split), terms[half - 1][0]
     lead = add_step(after(start, done), terms[0], down, places, [[units[0]], [units[1]]])

time: 156 us -> 151 us (0.968)
  Pallas kernels: 49.5 us -> 45.2 us
  local copies, waits for them, and re-layouts: 6.65 us -> 3.98 us
  waiting for transfers between devices: 58.7 us -> 60.6 us
    ppermute x17, waiting for transfers between devices: 23.6 us -> 30.6 us  [on_device(): send_on = lambda a: lax.ppermute(a, 'expert', onward)]
    ppermute x16, waiting for transfers between devices: 34.4 us -> 28.2 us  [on_device(): send_back = lambda a: lax.ppermute(a, 'expert', backward)]
    pallas_call x8, Pallas kernels: 7.84 us -> 4.28 us  [add_step(): pl.pallas_call(functools.partial(add_kernel, places, base, counts, joined...]
    unnamed x42 -> x20, local copies, waits for them, and re-layouts: 6.65 us -> 3.98 us
  transfers between devices with their start and end apart: 44 -> 44, of which waited for: 23 -> 24; matrix products, arithmetic and copies ran while one was open for 0% -> 0% of each run, Pallas kernels for 16% -> 13%
where the time goes in v4:
time: 151 us; the launch traced here: 150 us
  waiting for transfers between devices  60.6 us (40%)
  Pallas kernels  45.2 us (30%)
  starting transfers between devices  40.3 us (27%)
  local copies, waits for them, and re-layouts  3.98 us (3%)
    ppermute x17, waiting for transfers between devices, on_device(): send_on = lambda a: lax.ppermute(a, 'expert', onward)  30.6 us
    ppermute x16, waiting for transfers between devices, on_device(): send_back = lambda a: lax.ppermute(a, 'expert', backward)  28.2 us
    ppermute x17, starting transfers between devices, on_device(): send_on = lambda a: lax.ppermute(a, 'expert', onward)  26.4 us
    pallas_call x1, Pallas kernels, run_experts(): pl.pallas_call(functools.partial(expert_kernel, count, pieces, top), out_...  19.6 us
    ppermute x16, starting transfers between devices, on_device(): send_back = lambda a: lax.ppermute(a, 'expert', backward)  12.2 us
    pallas_call x4, Pallas kernels, pick_rows(): pl.pallas_call(functools.partial(pick_kernel, len(tokens), experts, top),...  5.34 us
    pallas_call x3, Pallas kernels, merge_rows(): pl.pallas_call(functools.partial(merge_kernel, count), out_shape=outs, gr...  4.3 us
    pallas_call x8, Pallas kernels, add_step(): pl.pallas_call(functools.partial(add_kernel, places, base, counts, joined...  4.28 us
  transfers between devices with their start and end apart: 44, of which 24 were waited for; matrix products, arithmetic and copies ran while one was open for 0% of the time, Pallas kernels for 13%

profile of v4, /device:TPU:0, one launch (start us, length us, event | category | flops | bytes accessed | tf_op | source)
XLA Modules:
  0.0 150.4 jit_solution(4871060036183034388)
XLA Ops:
  0.0 2.1 %note_tokens.1 = (bf16[32,3712]{1,0:T(8,128)(2,1)}, bf16[32,3712]{1,0:T(8,128)(2,1)}, bf16[64,3712]{1,0:T(8,128)(2,1)}) custom-call(bf16[64,3584]{1,0:T(8,128)(2,1)} %tokens.1, s32[8,64]{1,0:T(8,128)} %bitcast.6, f32[8,64]{1,0:T(8,128)} %bitcast.7), custom_call_target="tpu_custom_call" | custom-call | flops 1000 | bytes 1000 | tf_op jit(solution)/shard_map/note_tokens/pallas_call | solution.py:217
  3.1 3.0 %collective-permute-start.4 = (bf16[32,3712]{1,0:T(8,128)(2,1)}, bf16[32,3712]{1,0:T(8,128)(2,1)S(1)}, u32[]{:S(2)}, u32[]{:S(2)}) collective-permute-start(bf16[32,3712]{1,0:T(8,128)(2,1)} %get-tuple-element.89), channel_id=1, source_target_pairs={{0,4},{4,8},{8,12},{12,14},{14,10},{10,6},{6,2},{2,0},{1,5},{5,9},... | collective-permute-start | bytes 712712 | tf_op jit(solution)/shard_map/ppermute | solution.py:528
  9.9 3.8 %first_step.1 = (bf16[512,2048]{1,0:T(8,128)(2,1)}, bf16[512,1024]{1,0:T(8,128)(2,1)}, bf16[64,2048]{1,0:T(8,128)(2,1)}) custom-call(s32[1]{0:T(128)} %bitcast.start, s32[1]{0:T(128)} %bitcast.4.shift, bf16[64,3712]{1,0:T(8,128)(2,1)} %get-tuple-element.84.tokens.refs_0_, bf16[448,512]{1,0:T(8,128)(2,1)} %refs_0_.1, bf16[448,512]{1,0:T(8,128)(2,1)} %copy-done.7, ...), custom_call_target="tpu_custom_call" | custom-call | flops 99999997952 | bytes 1000 | tf_op jit(solution)/shard_map/first_step/pallas_call | solution.py:257
  14.8 3.2 %collective-permute-done.5.refs_1_ = bf16[32,3712]{1,0:T(8,128)(2,1)S(1)} collective-permute-done((bf16[32,3712]{1,0:T(8,128)(2,1)}, bf16[32,3712]{1,0:T(8,128)(2,1)S(1)}, u32[]{:S(2)}, u32[]{:S(2)}) %collective-permute-start.5) | collective-permute-done | bytes 237600 | tf_op jit(solution)/shard_map/ppermute | solution.py:528
  18.8 1.6 %copy-done.3 = bf16[512,2048]{1,0:T(8,128)(2,1)S(1)} copy-done((bf16[512,2048]{1,0:T(8,128)(2,1)S(1)}, bf16[512,2048]{1,0:T(8,128)(2,1)}, u32[]{:S(2)}) %copy-start.3) | copy-done | bytes 2097176
  21.6 1.4 collective-permute-start.10
  23.9 1.7 %collective-permute-start.9 = (bf16[32,5760]{1,0:T(8,128)(2,1)}, bf16[32,5760]{1,0:T(8,128)(2,1)S(1)}, u32[]{:S(2)}, u32[]{:S(2)}) collective-permute-start(bf16[32,5760]{1,0:T(8,128)(2,1)} %get-tuple-element.94), channel_id=1, source_target_pairs={{0,4},{4,8},{8,12},{12,14},{14,10},{10,6},{6,2},{2,0},{1,5},{5,9},... | collective-permute-start | bytes 1105928 | tf_op jit(solution)/shard_map/ppermute | solution.py:528
  25.9 1.7 %collective-permute-start.12 = (bf16[32,5760]{1,0:T(8,128)(2,1)S(1)}, bf16[32,5760]{1,0:T(8,128)(2,1)S(1)}, u32[]{:S(2)}, u32[]{:S(2)}) collective-permute-start(bf16[32,5760]{1,0:T(8,128)(2,1)S(1)} %get-tuple-element.101), channel_id=1, source_target_pairs={{0,4},{4,8},{8,12},{12,14},{14,10},{10,6},{6,2},{2,0},{1,5},{5,9},... | collective-permute-start | bytes 1105928 | tf_op jit(solution)/shard_map/ppermute | solution.py:528
  27.6 5.8 %collective-permute-done.10.back.refs_1_ = bf16[32,5760]{1,0:T(8,128)(2,1)S(1)} collective-permute-done((bf16[32,5760]{1,0:T(8,128)(2,1)}, bf16[32,5760]{1,0:T(8,128)(2,1)S(1)}, u32[]{:S(2)}, u32[]{:S(2)}) %collective-permute-start.10) | collective-permute-done | bytes 368672 | tf_op jit(solution)/shard_map/ppermute | solution.py:529
  33.4 2.2 %collective-permute-done.9.on.refs_0_ = bf16[32,5760]{1,0:T(8,128)(2,1)S(1)} collective-permute-done((bf16[32,5760]{1,0:T(8,128)(2,1)}, bf16[32,5760]{1,0:T(8,128)(2,1)S(1)}, u32[]{:S(2)}, u32[]{:S(2)}) %collective-permute-start.9) | collective-permute-done | bytes 368672 | tf_op jit(solution)/shard_map/ppermute | solution.py:528
  35.6 1.6 %copy-done.4 = bf16[512,2048]{1,0:T(8,128)(2,1)S(1)} copy-done((bf16[512,2048]{1,0:T(8,128)(2,1)S(1)}, bf16[512,2048]{1,0:T(8,128)(2,1)}, u32[]{:S(2)}) %copy-start.4) | copy-done | bytes 2097176
  37.7 1.7 %collective-permute-start.14 = (bf16[32,5760]{1,0:T(8,128)(2,1)S(1)}, bf16[32,5760]{1,0:T(8,128)(2,1)S(1)}, u32[]{:S(2)}, u32[]{:S(2)}) collective-permute-start(bf16[32,5760]{1,0:T(8,128)(2,1)S(1)} %get-tuple-element.97), channel_id=1, source_target_pairs={{0,4},{4,8},{8,12},{12,14},{14,10},{10,6},{6,2},{2,0},{1,5},{5,9},... | collective-permute-start | bytes 1105928 | tf_op jit(solution)/shard_map/ppermute | solution.py:528
  41.1 2.4 %collective-permute-done.12.on = bf16[32,5760]{1,0:T(8,128)(2,1)S(1)} collective-permute-done((bf16[32,5760]{1,0:T(8,128)(2,1)S(1)}, bf16[32,5760]{1,0:T(8,128)(2,1)S(1)}, u32[]{:S(2)}, u32[]{:S(2)}) %collective-permute-start.12) | collective-permute-done | bytes 368672 | tf_op jit(solution)/shard_map/ppermute | solution.py:528
  44.1 1.7 %collective-permute-start.17 = (bf16[32,5760]{1,0:T(8,128)(2,1)S(1)}, bf16[32,5760]{1,0:T(8,128)(2,1)S(1)}, u32[]{:S(2)}, u32[]{:S(2)}) collective-permute-start(bf16[32,5760]{1,0:T(8,128)(2,1)S(1)} %get-tuple-element.104), channel_id=1, source_target_pairs={{0,4},{4,8},{8,12},{12,14},{14,10},{10,6},{6,2},{2,0},{1,5},{5,9},... | collective-permute-start | bytes 1105928 | tf_op jit(solution)/shard_map/ppermute | solution.py:528
  46.2 5.2 %collective-permute-done.14.on.refs_0_ = bf16[32,5760]{1,0:T(8,128)(2,1)S(1)} collective-permute-done((bf16[32,5760]{1,0:T(8,128)(2,1)S(1)}, bf16[32,5760]{1,0:T(8,128)(2,1)S(1)}, u32[]{:S(2)}, u32[]{:S(2)}) %collective-permute-start.14) | collective-permute-done | bytes 368672 | tf_op jit(solution)/shard_map/ppermute | solution.py:528
  51.9 1.7 %collective-permute-start.19 = (bf16[32,5760]{1,0:T(8,128)(2,1)S(1)}, bf16[32,5760]{1,0:T(8,128)(2,1)S(1)}, u32[]{:S(2)}, u32[]{:S(2)}) collective-permute-start(bf16[32,5760]{1,0:T(8,128)(2,1)S(1)} %get-tuple-element.107), channel_id=1, source_target_pairs={{0,4},{4,8},{8,12},{12,14},{14,10},{10,6},{6,2},{2,0},{1,5},{5,9},... | collective-permute-start | bytes 1105928 | tf_op jit(solution)/shard_map/ppermute | solution.py:528
  53.6 1.3 pick_rows.5
  55.0 4.3 %collective-permute-done.17.on = bf16[32,5760]{1,0:T(8,128)(2,1)S(1)} collective-permute-done((bf16[32,5760]{1,0:T(8,128)(2,1)S(1)}, bf16[32,5760]{1,0:T(8,128)(2,1)S(1)}, u32[]{:S(2)}, u32[]{:S(2)}) %collective-permute-start.17) | collective-permute-done | bytes 368672 | tf_op jit(solution)/shard_map/ppermute | solution.py:528
  59.9 1.7 %collective-permute-start.20 = (bf16[32,2048]{1,0:T(8,128)(2,1)S(1)}, bf16[32,2048]{1,0:T(8,128)(2,1)S(1)}, u32[]{:S(2)}, u32[]{:S(2)}) collective-permute-start(bf16[32,2048]{1,0:T(8,128)(2,1)S(1)} %get-tuple-element.115), channel_id=1, source_target_pairs={{4,0},{8,4},{12,8},{14,12},{10,14},{6,10},{2,6},{0,2},{5,1},{9,5},... | collective-permute-start | bytes 393224 | tf_op jit(solution)/shard_map/ppermute | solution.py:529
  61.9 1.6 %collective-permute-start.22 = (bf16[32,5760]{1,0:T(8,128)(2,1)S(1)}, bf16[32,5760]{1,0:T(8,128)(2,1)S(1)}, u32[]{:S(2)}, u32[]{:S(2)}) collective-permute-start(bf16[32,5760]{1,0:T(8,128)(2,1)S(1)} %get-tuple-element.119), channel_id=1, source_target_pairs={{4,0},{8,4},{12,8},{14,12},{10,14},{6,10},{2,6},{0,2},{5,1},{9,5},... | collective-permute-start | bytes 1105928 | tf_op jit(solution)/shard_map/ppermute | solution.py:529
  63.6 2.6 %collective-permute-done.20.side = bf16[32,2048]{1,0:T(8,128)(2,1)S(1)} collective-permute-done((bf16[32,2048]{1,0:T(8,128)(2,1)S(1)}, bf16[32,2048]{1,0:T(8,128)(2,1)S(1)}, u32[]{:S(2)}, u32[]{:S(2)}) %collective-permute-start.20) | collective-permute-done | bytes 131104 | tf_op jit(solution)/shard_map/ppermute | solution.py:529
  67.1 1.3 pick_rows.6
  68.5 5.1 %collective-permute-done.22.main = bf16[32,5760]{1,0:T(8,128)(2,1)S(1)} collective-permute-done((bf16[32,5760]{1,0:T(8,128)(2,1)S(1)}, bf16[32,5760]{1,0:T(8,128)(2,1)S(1)}, u32[]{:S(2)}, u32[]{:S(2)}) %collective-permute-start.22) | collective-permute-done | bytes 368672 | tf_op jit(solution)/shard_map/ppermute | solution.py:529
  74.2 1.8 %collective-permute-done.24.refs_3_ = bf16[64,3712]{1,0:T(8,128)(2,1)S(1)} collective-permute-done((bf16[64,3712]{1,0:T(8,128)(2,1)S(1)}, bf16[64,3712]{1,0:T(8,128)(2,1)S(1)}, u32[]{:S(2)}, u32[]{:S(2)}) %collective-permute-start.24) | collective-permute-done | bytes 475168 | tf_op jit(solution)/shard_map/ppermute | solution.py:530
  76.1 1.3 pick_rows.7
  77.4 19.6 %run_experts.1 = (bf16[4,80,3584]{2,1,0:T(8,128)(2,1)S(1)}, bf16[4,80,3584]{2,1,0:T(8,128)(2,1)S(1)}, bf16[4,80,3584]{2,1,0:T(8,128)(2,1)S(1)}, bf16[4,80,3584]{2,1,0:T(8,128)(2,1)S(1)}) custom-call(s32[1]{0:T(128)} %bitcast.1.first, bf16[4,80,3712]{2,1,0:T(8,128)(2,1)S(1)} %get-tuple-element.122.refs_0_, ...), custom_call_target="tpu_custom_call" | custom-call | flops 99999997952 | bytes 1000 | tf_op jit(solution)/shard_map/run_experts/pallas_call | solution.py:181
  98.4 1.7 %collective-permute-start.28 = (bf16[32,1024]{1,0:T(8,128)(2,1)S(1)}, bf16[32,1024]{1,0:T(8,128)(2,1)S(1)}, u32[]{:S(2)}, u32[]{:S(2)}) collective-permute-start(bf16[32,1024]{1,0:T(8,128)(2,1)S(1)} %last_step.2.refs_0_), channel_id=1, source_target_pairs={{4,0},{8,4},{12,8},{14,12},{10,14},{6,10},{2,6},{0,2},{5,1},{9,5},... | collective-permute-start | bytes 196616 | tf_op jit(solution)/shard_map/ppermute | solution.py:529
  102.1 1.7 %collective-permute-start.29 = (bf16[32,4608]{1,0:T(8,128)(2,1)S(1)}, bf16[32,4608]{1,0:T(8,128)(2,1)S(1)}, u32[]{:S(2)}, u32[]{:S(2)}) collective-permute-start(bf16[32,4608]{1,0:T(8,128)(2,1)S(1)} %get-tuple-element.135), channel_id=1, source_target_pairs={{0,4},{4,8},{8,12},{12,14},{14,10},{10,6},{6,2},{2,0},{1,5},{5,9},... | collective-permute-start | bytes 884744 | tf_op jit(solution)/shard_map/ppermute | solution.py:528
  104.8 1.9 %collective-permute-start.32 = (bf16[32,4608]{1,0:T(8,128)(2,1)S(1)}, bf16[32,4608]{1,0:T(8,128)(2,1)S(1)}, u32[]{:S(2)}, u32[]{:S(2)}) collective-permute-start(bf16[32,4608]{1,0:T(8,128)(2,1)S(1)} %get-tuple-element.138), channel_id=1, source_target_pairs={{0,4},{4,8},{8,12},{12,14},{14,10},{10,6},{6,2},{2,0},{1,5},{5,9},... | collective-permute-start | bytes 884744 | tf_op jit(solution)/shard_map/ppermute | solution.py:528
  106.7 2.1 %merge_rows.5 = (f32[128,3584]{1,0:T(8,128)S(1)}, f32[128,3584]{1,0:T(8,128)S(1)}, bf16[256,3584]{1,0:T(8,128)(2,1)S(1)}) custom-call(bf16[256,320]{1,0:T(8,128)(2,1)S(1)} %get-tuple-element.139.refs_0_, bf16[256,320]{1,0:T(8,128)(2,1)S(1)} %get-tuple-element.99.refs_1_, bf16[4,80,3584]{2,1,0:T(8,128)(2,1)S(1)} %get-tuple-element.140.refs_2_, ...), custom_call_target="tpu_custom_call" | custom-call | flops 1000 | bytes 1000 | tf_op jit(solution)/shard_map/merge_rows/pallas_call | solution.py:412
  109.4 2.7 %collective-permute-done.29.refs_0_ = bf16[32,4608]{1,0:T(8,128)(2,1)S(1)} collective-permute-done((bf16[32,4608]{1,0:T(8,128)(2,1)S(1)}, bf16[32,4608]{1,0:T(8,128)(2,1)S(1)}, u32[]{:S(2)}, u32[]{:S(2)}) %collective-permute-start.29) | collective-permute-done | bytes 294944 | tf_op jit(solution)/shard_map/ppermute | solution.py:528
  112.0 1.7 %collective-permute-done.30.refs_1_ = bf16[32,4608]{1,0:T(8,128)(2,1)S(1)} collective-permute-done((bf16[32,4608]{1,0:T(8,128)(2,1)S(1)}, bf16[32,4608]{1,0:T(8,128)(2,1)S(1)}, u32[]{:S(2)}, u32[]{:S(2)}) %collective-permute-start.30) | collective-permute-done | bytes 294944 | tf_op jit(solution)/shard_map/ppermute | solution.py:529
  114.3 1.6 %collective-permute-start.34 = (bf16[32,4608]{1,0:T(8,128)(2,1)S(1)}, bf16[32,4608]{1,0:T(8,128)(2,1)S(1)}, u32[]{:S(2)}, u32[]{:S(2)}) collective-permute-start(bf16[32,4608]{1,0:T(8,128)(2,1)S(1)} %get-tuple-element.145), channel_id=1, source_target_pairs={{0,4},{4,8},{8,12},{12,14},{14,10},{10,6},{6,2},{2,0},{1,5},{5,9},... | collective-permute-start | bytes 884744 | tf_op jit(solution)/shard_map/ppermute | solution.py:528
  116.4 2.0 %collective-permute-done.32.refs_0_ = bf16[32,4608]{1,0:T(8,128)(2,1)S(1)} collective-permute-done((bf16[32,4608]{1,0:T(8,128)(2,1)S(1)}, bf16[32,4608]{1,0:T(8,128)(2,1)S(1)}, u32[]{:S(2)}, u32[]{:S(2)}) %collective-permute-start.32) | collective-permute-done | bytes 294944 | tf_op jit(solution)/shard_map/ppermute | solution.py:528
  118.3 1.7 %collective-permute-done.33.refs_1_ = bf16[32,4608]{1,0:T(8,128)(2,1)S(1)} collective-permute-done((bf16[32,4608]{1,0:T(8,128)(2,1)S(1)}, bf16[32,4608]{1,0:T(8,128)(2,1)S(1)}, u32[]{:S(2)}, u32[]{:S(2)}) %collective-permute-start.33) | collective-permute-done | bytes 294944 | tf_op jit(solution)/shard_map/ppermute | solution.py:529
  120.6 1.6 %collective-permute-start.36 = (bf16[32,4608]{1,0:T(8,128)(2,1)S(1)}, bf16[32,4608]{1,0:T(8,128)(2,1)S(1)}, u32[]{:S(2)}, u32[]{:S(2)}) collective-permute-start(bf16[32,4608]{1,0:T(8,128)(2,1)S(1)} %get-tuple-element.149), channel_id=1, source_target_pairs={{0,4},{4,8},{8,12},{12,14},{14,10},{10,6},{6,2},{2,0},{1,5},{5,9},... | collective-permute-start | bytes 884744 | tf_op jit(solution)/shard_map/ppermute | solution.py:528
  122.7 2.0 %collective-permute-done.34.refs_0_ = bf16[32,4608]{1,0:T(8,128)(2,1)S(1)} collective-permute-done((bf16[32,4608]{1,0:T(8,128)(2,1)S(1)}, bf16[32,4608]{1,0:T(8,128)(2,1)S(1)}, u32[]{:S(2)}, u32[]{:S(2)}) %collective-permute-start.34) | collective-permute-done | bytes 294944 | tf_op jit(solution)/shard_map/ppermute | solution.py:528
  124.7 1.7 %collective-permute-done.35.refs_1_ = bf16[32,4608]{1,0:T(8,128)(2,1)S(1)} collective-permute-done((bf16[32,4608]{1,0:T(8,128)(2,1)S(1)}, bf16[32,4608]{1,0:T(8,128)(2,1)S(1)}, u32[]{:S(2)}, u32[]{:S(2)}) %collective-permute-start.35) | collective-permute-done | bytes 294944 | tf_op jit(solution)/shard_map/ppermute | solution.py:529
  126.9 1.6 %collective-permute-start.38 = (bf16[32,4608]{1,0:T(8,128)(2,1)S(1)}, bf16[32,4608]{1,0:T(8,128)(2,1)S(1)}, u32[]{:S(2)}, u32[]{:S(2)}) collective-permute-start(bf16[32,4608]{1,0:T(8,128)(2,1)S(1)} %get-tuple-element.152), channel_id=1, source_target_pairs={{0,4},{4,8},{8,12},{12,14},{14,10},{10,6},{6,2},{2,0},{1,5},{5,9},... | collective-permute-start | bytes 884744 | tf_op jit(solution)/shard_map/ppermute | solution.py:528
  129.0 2.0 %collective-permute-done.36.refs_0_ = bf16[32,4608]{1,0:T(8,128)(2,1)S(1)} collective-permute-done((bf16[32,4608]{1,0:T(8,128)(2,1)S(1)}, bf16[32,4608]{1,0:T(8,128)(2,1)S(1)}, u32[]{:S(2)}, u32[]{:S(2)}) %collective-permute-start.36) | collective-permute-done | bytes 294944 | tf_op jit(solution)/shard_map/ppermute | solution.py:528
  131.0 1.7 %collective-permute-done.37.refs_1_ = bf16[32,4608]{1,0:T(8,128)(2,1)S(1)} collective-permute-done((bf16[32,4608]{1,0:T(8,128)(2,1)S(1)}, bf16[32,4608]{1,0:T(8,128)(2,1)S(1)}, u32[]{:S(2)}, u32[]{:S(2)}) %collective-permute-start.37) | collective-permute-done | bytes 294944 | tf_op jit(solution)/shard_map/ppermute | solution.py:529
  133.2 1.6 %collective-permute-start.41 = (bf16[32,4608]{1,0:T(8,128)(2,1)S(1)}, bf16[32,4608]{1,0:T(8,128)(2,1)S(1)}, u32[]{:S(2)}, u32[]{:S(2)}) collective-permute-start(bf16[32,4608]{1,0:T(8,128)(2,1)S(1)} %get-tuple-element.156), channel_id=1, source_target_pairs={{0,4},{4,8},{8,12},{12,14},{14,10},{10,6},{6,2},{2,0},{1,5},{5,9},... | collective-permute-start | bytes 884744 | tf_op jit(solution)/shard_map/ppermute | solution.py:528
  135.3 2.0 %collective-permute-done.38.refs_0_ = bf16[32,4608]{1,0:T(8,128)(2,1)S(1)} collective-permute-done((bf16[32,4608]{1,0:T(8,128)(2,1)S(1)}, bf16[32,4608]{1,0:T(8,128)(2,1)S(1)}, u32[]{:S(2)}, u32[]{:S(2)}) %collective-permute-start.38) | collective-permute-done | bytes 294944 | tf_op jit(solution)/shard_map/ppermute | solution.py:528
  137.3 1.7 %collective-permute-done.39.refs_1_ = bf16[32,4608]{1,0:T(8,128)(2,1)S(1)} collective-permute-done((bf16[32,4608]{1,0:T(8,128)(2,1)S(1)}, bf16[32,4608]{1,0:T(8,128)(2,1)S(1)}, u32[]{:S(2)}, u32[]{:S(2)}) %collective-permute-start.39) | collective-permute-done | bytes 294944 | tf_op jit(solution)/shard_map/ppermute | solution.py:529
  139.6 1.6 %collective-permute-start.42 = (bf16[32,3584]{1,0:T(8,128)(2,1)S(1)}, bf16[32,3584]{1,0:T(8,128)(2,1)S(1)}, u32[]{:S(2)}, u32[]{:S(2)}) collective-permute-start(bf16[32,3584]{1,0:T(8,128)(2,1)S(1)} %get-tuple-element.159), channel_id=1, source_target_pairs={{0,4},{4,8},{8,12},{12,14},{14,10},{10,6},{6,2},{2,0},{1,5},{5,9},... | collective-permute-start | bytes 688136 | tf_op jit(solution)/shard_map/ppermute | solution.py:528
  141.6 3.7 %collective-permute-done.40.refs_0_ = bf16[32,4608]{1,0:T(8,128)(2,1)S(1)} collective-permute-done((bf16[32,4608]{1,0:T(8,128)(2,1)S(1)}, bf16[32,4608]{1,0:T(8,128)(2,1)S(1)}, u32[]{:S(2)}, u32[]{:S(2)}) %collective-permute-start.40) | collective-permute-done | bytes 294944 | tf_op jit(solution)/shard_map/ppermute | solution.py:529
  145.9 2.2 %collective-permute-done.42.first = bf16[32,3584]{1,0:T(8,128)(2,1)S(1)} collective-permute-done((bf16[32,3584]{1,0:T(8,128)(2,1)S(1)}, bf16[32,3584]{1,0:T(8,128)(2,1)S(1)}, u32[]{:S(2)}, u32[]{:S(2)}) %collective-permute-start.42) | collective-permute-done | bytes 229408 | tf_op jit(solution)/shard_map/ppermute | solution.py:528
  148.1 1.4 collective-permute-done.43.second
  (87 shorter events, 26.2 us)
Async XLA Ops:
  2.1 4.0 %collective-permute-start = (bf16[64,3712]{1,0:T(8,128)(2,1)}, bf16[64,3712]{1,0:T(8,128)(2,1)S(1)}, u32[]{:S(2)}, u32[]{:S(2)}) collective-permute-start(bf16[64,3712]{1,0:T(8,128)(2,1)} %get-tuple-element.84.tokens.refs_0_), channel_id=1, source_target_pairs={{0,1},{1,0},{2,3},{3,2},{4,5},{5,4},{6,7},{7,6},{8,9},{9,8},{10,11... | collective-permute-start | bytes 1425416 | tf_op jit(solution)/shard_map/ppermute | solution.py:530
  2.5 4.6 %collective-permute-start.1 = (bf16[448,512]{1,0:T(8,128)(2,1)}, bf16[448,512]{1,0:T(8,128)(2,1)S(1)}, u32[]{:S(2)}, u32[]{:S(2)}) collective-permute-start(bf16[448,512]{1,0:T(8,128)(2,1)} %refs_0_.1), channel_id=1, source_target_pairs={{0,1},{1,0},{2,3},{3,2},{4,5},{5,4},{6,7},{7,6},{8,9},{9,8},{10,11... | collective-permute-start | bytes 1376264 | tf_op jit(solution)/shard_map/ppermute | solution.py:530
  2.6 5.6 %collective-permute-start.2 = (bf16[448,512]{1,0:T(8,128)(2,1)}, bf16[448,512]{1,0:T(8,128)(2,1)S(1)}, u32[]{:S(2)}, u32[]{:S(2)}) collective-permute-start(bf16[448,512]{1,0:T(8,128)(2,1)} %refs_2_.1), channel_id=1, source_target_pairs={{0,1},{1,0},{2,3},{3,2},{4,5},{5,4},{6,7},{7,6},{8,9},{9,8},{10,11... | collective-permute-start | bytes 1376264 | tf_op jit(solution)/shard_map/ppermute | solution.py:530
  3.0 6.1 %collective-permute-start.3 = (bf16[448,512]{1,0:T(8,128)(2,1)}, bf16[448,512]{1,0:T(8,128)(2,1)S(1)}, u32[]{:S(2)}, u32[]{:S(2)}) collective-permute-start(bf16[448,512]{1,0:T(8,128)(2,1)} %bitcast.8), channel_id=1, source_target_pairs={{0,1},{1,0},{2,3},{3,2},{4,5},{5,4},{6,7},{7,6},{8,9},{9,8},{10,11... | collective-permute-start | bytes 1376264 | tf_op jit(solution)/shard_map/ppermute | solution.py:530
  3.1 11.7 %collective-permute-start.4 = (bf16[32,3712]{1,0:T(8,128)(2,1)}, bf16[32,3712]{1,0:T(8,128)(2,1)S(1)}, u32[]{:S(2)}, u32[]{:S(2)}) collective-permute-start(bf16[32,3712]{1,0:T(8,128)(2,1)} %get-tuple-element.89), channel_id=1, source_target_pairs={{0,4},{4,8},{8,12},{12,14},{14,10},{10,6},{6,2},{2,0},{1,5},{5,9},... | collective-permute-start | bytes 712712 | tf_op jit(solution)/shard_map/ppermute | solution.py:528
  6.1 7.6 %copy-start.1 = (bf16[64,3712]{1,0:T(8,128)(2,1)}, bf16[64,3712]{1,0:T(8,128)(2,1)S(1)}, u32[]{:S(2)}) copy-start(bf16[64,3712]{1,0:T(8,128)(2,1)S(1)} %collective-permute-done.refs_2_) | copy-start | bytes 1425412
  6.1 11.8 %collective-permute-start.6 = (bf16[32,3712]{1,0:T(8,128)(2,1)}, bf16[32,3712]{1,0:T(8,128)(2,1)S(1)}, u32[]{:S(2)}, u32[]{:S(2)}) collective-permute-start(bf16[32,3712]{1,0:T(8,128)(2,1)} %get-tuple-element.89), channel_id=1, source_target_pairs={{4,0},{8,4},{12,8},{14,12},{10,14},{6,10},{2,6},{0,2},{5,1},{9,5},... | collective-permute-start | bytes 712712 | tf_op jit(solution)/shard_map/ppermute | solution.py:529
  7.1 10.9 %collective-permute-start.5 = (bf16[32,3712]{1,0:T(8,128)(2,1)}, bf16[32,3712]{1,0:T(8,128)(2,1)S(1)}, u32[]{:S(2)}, u32[]{:S(2)}) collective-permute-start(bf16[32,3712]{1,0:T(8,128)(2,1)} %get-tuple-element.90), channel_id=1, source_target_pairs={{0,4},{4,8},{8,12},{12,14},{14,10},{10,6},{6,2},{2,0},{1,5},{5,9},... | collective-permute-start | bytes 712712 | tf_op jit(solution)/shard_map/ppermute | solution.py:528
  8.2 10.7 %collective-permute-start.7 = (bf16[32,3712]{1,0:T(8,128)(2,1)}, bf16[32,3712]{1,0:T(8,128)(2,1)S(1)}, u32[]{:S(2)}, u32[]{:S(2)}) collective-permute-start(bf16[32,3712]{1,0:T(8,128)(2,1)} %get-tuple-element.90), channel_id=1, source_target_pairs={{4,0},{8,4},{12,8},{14,12},{10,14},{6,10},{2,6},{0,2},{5,1},{9,5},... | collective-permute-start | bytes 712712 | tf_op jit(solution)/shard_map/ppermute | solution.py:529
  13.7 9.3 %collective-permute-start.8 = (bf16[64,2048]{1,0:T(8,128)(2,1)}, bf16[64,2048]{1,0:T(8,128)(2,1)S(1)}, u32[]{:S(2)}, u32[]{:S(2)}) collective-permute-start(bf16[64,2048]{1,0:T(8,128)(2,1)} %get-tuple-element.93), channel_id=1, source_target_pairs={{0,4},{4,8},{8,12},{12,14},{14,10},{10,6},{6,2},{2,0},{1,5},{5,9},... | collective-permute-start | bytes 786440 | tf_op jit(solution)/shard_map/ppermute | solution.py:528
  21.6 11.7 %collective-permute-start.10 = (bf16[32,5760]{1,0:T(8,128)(2,1)}, bf16[32,5760]{1,0:T(8,128)(2,1)S(1)}, u32[]{:S(2)}, u32[]{:S(2)}) collective-permute-start(bf16[32,5760]{1,0:T(8,128)(2,1)} %get-tuple-element.96), channel_id=1, source_target_pairs={{4,0},{8,4},{12,8},{14,12},{10,14},{6,10},{2,6},{0,2},{5,1},{9,5},... | collective-permute-start | bytes 1105928 | tf_op jit(solution)/shard_map/ppermute | solution.py:529
  23.9 11.7 %collective-permute-start.9 = (bf16[32,5760]{1,0:T(8,128)(2,1)}, bf16[32,5760]{1,0:T(8,128)(2,1)S(1)}, u32[]{:S(2)}, u32[]{:S(2)}) collective-permute-start(bf16[32,5760]{1,0:T(8,128)(2,1)} %get-tuple-element.94), channel_id=1, source_target_pairs={{0,4},{4,8},{8,12},{12,14},{14,10},{10,6},{6,2},{2,0},{1,5},{5,9},... | collective-permute-start | bytes 1105928 | tf_op jit(solution)/shard_map/ppermute | solution.py:528
  25.6 14.2 %collective-permute-start.11 = (bf16[128,3712]{1,0:T(8,128)(2,1)S(1)}, bf16[128,3712]{1,0:T(8,128)(2,1)S(1)}, u32[]{:S(2)}, u32[]{:S(2)}) collective-permute-start(bf16[128,3712]{1,0:T(8,128)(2,1)S(1)} %get-tuple-element.98.refs_0_), channel_id=1, source_target_pairs={{0,1},{1,0},{2,3},{3,2},{4,5},{5,4},{6,7},{7,6},{8,9},{9,8},{10,11... | collective-permute-start | bytes 2850824 | tf_op jit(solution)/shard_map/ppermute | solution.py:530
  25.6 15.5 %collective-permute-start.13 = (bf16[32,5760]{1,0:T(8,128)(2,1)S(1)}, bf16[32,5760]{1,0:T(8,128)(2,1)S(1)}, u32[]{:S(2)}, u32[]{:S(2)}) collective-permute-start(bf16[32,5760]{1,0:T(8,128)(2,1)S(1)} %get-tuple-element.102), channel_id=1, source_target_pairs={{4,0},{8,4},{12,8},{14,12},{10,14},{6,10},{2,6},{0,2},{5,1},{9,5},... | collective-permute-start | bytes 1105928 | tf_op jit(solution)/shard_map/ppermute | solution.py:529
  25.9 17.6 %collective-permute-start.12 = (bf16[32,5760]{1,0:T(8,128)(2,1)S(1)}, bf16[32,5760]{1,0:T(8,128)(2,1)S(1)}, u32[]{:S(2)}, u32[]{:S(2)}) collective-permute-start(bf16[32,5760]{1,0:T(8,128)(2,1)S(1)} %get-tuple-element.101), channel_id=1, source_target_pairs={{0,4},{4,8},{8,12},{12,14},{14,10},{10,6},{6,2},{2,0},{1,5},{5,9},... | collective-permute-start | bytes 1105928 | tf_op jit(solution)/shard_map/ppermute | solution.py:528
  37.7 13.7 %collective-permute-start.14 = (bf16[32,5760]{1,0:T(8,128)(2,1)S(1)}, bf16[32,5760]{1,0:T(8,128)(2,1)S(1)}, u32[]{:S(2)}, u32[]{:S(2)}) collective-permute-start(bf16[32,5760]{1,0:T(8,128)(2,1)S(1)} %get-tuple-element.97), channel_id=1, source_target_pairs={{0,4},{4,8},{8,12},{12,14},{14,10},{10,6},{6,2},{2,0},{1,5},{5,9},... | collective-permute-start | bytes 1105928 | tf_op jit(solution)/shard_map/ppermute | solution.py:528
  39.4 12.0 %collective-permute-start.15 = (bf16[32,5760]{1,0:T(8,128)(2,1)S(1)}, bf16[32,5760]{1,0:T(8,128)(2,1)S(1)}, u32[]{:S(2)}, u32[]{:S(2)}) collective-permute-start(bf16[32,5760]{1,0:T(8,128)(2,1)S(1)} %get-tuple-element.106), channel_id=1, source_target_pairs={{4,0},{8,4},{12,8},{14,12},{10,14},{6,10},{2,6},{0,2},{5,1},{9,5},... | collective-permute-start | bytes 1105928 | tf_op jit(solution)/shard_map/ppermute | solution.py:529
  44.0 9.6 %collective-permute-start.16 = (bf16[128,3712]{1,0:T(8,128)(2,1)S(1)}, bf16[128,3712]{1,0:T(8,128)(2,1)S(1)}, u32[]{:S(2)}, u32[]{:S(2)}) collective-permute-start(bf16[128,3712]{1,0:T(8,128)(2,1)S(1)} %get-tuple-element.108.refs_0_), channel_id=1, source_target_pairs={{0,1},{1,0},{2,3},{3,2},{4,5},{5,4},{6,7},{7,6},{8,9},{9,8},{10,11... | collective-permute-start | bytes 2850824 | tf_op jit(solution)/shard_map/ppermute | solution.py:530
  44.1 15.2 %collective-permute-start.17 = (bf16[32,5760]{1,0:T(8,128)(2,1)S(1)}, bf16[32,5760]{1,0:T(8,128)(2,1)S(1)}, u32[]{:S(2)}, u32[]{:S(2)}) collective-permute-start(bf16[32,5760]{1,0:T(8,128)(2,1)S(1)} %get-tuple-element.104), channel_id=1, source_target_pairs={{0,4},{4,8},{8,12},{12,14},{14,10},{10,6},{6,2},{2,0},{1,5},{5,9},... | collective-permute-start | bytes 1105928 | tf_op jit(solution)/shard_map/ppermute | solution.py:528
  45.8 13.5 %collective-permute-start.18 = (bf16[32,5760]{1,0:T(8,128)(2,1)S(1)}, bf16[32,5760]{1,0:T(8,128)(2,1)S(1)}, u32[]{:S(2)}, u32[]{:S(2)}) collective-permute-start(bf16[32,5760]{1,0:T(8,128)(2,1)S(1)} %get-tuple-element.111), channel_id=1, source_target_pairs={{4,0},{8,4},{12,8},{14,12},{10,14},{6,10},{2,6},{0,2},{5,1},{9,5},... | collective-permute-start | bytes 1105928 | tf_op jit(solution)/shard_map/ppermute | solution.py:529
  51.9 14.8 %collective-permute-start.19 = (bf16[32,5760]{1,0:T(8,128)(2,1)S(1)}, bf16[32,5760]{1,0:T(8,128)(2,1)S(1)}, u32[]{:S(2)}, u32[]{:S(2)}) collective-permute-start(bf16[32,5760]{1,0:T(8,128)(2,1)S(1)} %get-tuple-element.107), channel_id=1, source_target_pairs={{0,4},{4,8},{8,12},{12,14},{14,10},{10,6},{6,2},{2,0},{1,5},{5,9},... | collective-permute-start | bytes 1105928 | tf_op jit(solution)/shard_map/ppermute | solution.py:528
  59.8 7.3 %collective-permute-start.21 = (bf16[128,3712]{1,0:T(8,128)(2,1)S(1)}, bf16[128,3712]{1,0:T(8,128)(2,1)S(1)}, u32[]{:S(2)}, u32[]{:S(2)}) collective-permute-start(bf16[128,3712]{1,0:T(8,128)(2,1)S(1)} %get-tuple-element.116.refs_0_), channel_id=1, source_target_pairs={{0,1},{1,0},{2,3},{3,2},{4,5},{5,4},{6,7},{7,6},{8,9},{9,8},{10,11... | collective-permute-start | bytes 2850824 | tf_op jit(solution)/shard_map/ppermute | solution.py:530
  59.9 6.3 %collective-permute-start.20 = (bf16[32,2048]{1,0:T(8,128)(2,1)S(1)}, bf16[32,2048]{1,0:T(8,128)(2,1)S(1)}, u32[]{:S(2)}, u32[]{:S(2)}) collective-permute-start(bf16[32,2048]{1,0:T(8,128)(2,1)S(1)} %get-tuple-element.115), channel_id=1, source_target_pairs={{4,0},{8,4},{12,8},{14,12},{10,14},{6,10},{2,6},{0,2},{5,1},{9,5},... | collective-permute-start | bytes 393224 | tf_op jit(solution)/shard_map/ppermute | solution.py:529
  61.6 7.0 %collective-permute-start.23 = (bf16[32,2048]{1,0:T(8,128)(2,1)S(1)}, bf16[32,2048]{1,0:T(8,128)(2,1)S(1)}, u32[]{:S(2)}, u32[]{:S(2)}) collective-permute-start(bf16[32,2048]{1,0:T(8,128)(2,1)S(1)} %get-tuple-element.113), channel_id=1, source_target_pairs={{0,4},{4,8},{8,12},{12,14},{14,10},{10,6},{6,2},{2,0},{1,5},{5,9},... | collective-permute-start | bytes 393224 | tf_op jit(solution)/shard_map/ppermute | solution.py:528
  61.9 11.7 %collective-permute-start.22 = (bf16[32,5760]{1,0:T(8,128)(2,1)S(1)}, bf16[32,5760]{1,0:T(8,128)(2,1)S(1)}, u32[]{:S(2)}, u32[]{:S(2)}) collective-permute-start(bf16[32,5760]{1,0:T(8,128)(2,1)S(1)} %get-tuple-element.119), channel_id=1, source_target_pairs={{4,0},{8,4},{12,8},{14,12},{10,14},{6,10},{2,6},{0,2},{5,1},{9,5},... | collective-permute-start | bytes 1105928 | tf_op jit(solution)/shard_map/ppermute | solution.py:529
  68.5 7.6 %copy-start = (bf16[64,3712]{1,0:T(8,128)(2,1)S(1)}, bf16[64,3712]{1,0:T(8,128)(2,1)}, u32[]{:S(2)}) copy-start(bf16[64,3712]{1,0:T(8,128)(2,1)} %get-tuple-element.84.tokens.refs_0_) | copy-start | bytes 1425412
  68.5 7.6 %copy-start.2 = (bf16[64,3712]{1,0:T(8,128)(2,1)S(1)}, bf16[64,3712]{1,0:T(8,128)(2,1)}, u32[]{:S(2)}) copy-start(bf16[64,3712]{1,0:T(8,128)(2,1)} %copy-done.1) | copy-start | bytes 1425412
  74.1 1.9 %collective-permute-start.24 = (bf16[64,3712]{1,0:T(8,128)(2,1)S(1)}, bf16[64,3712]{1,0:T(8,128)(2,1)S(1)}, u32[]{:S(2)}, u32[]{:S(2)}) collective-permute-start(bf16[64,3712]{1,0:T(8,128)(2,1)S(1)} %get-tuple-element.120.refs_1_), channel_id=1, source_target_pairs={{0,1},{1,0},{2,3},{3,2},{4,5},{5,4},{6,7},{7,6},{8,9},{9,8},{10,11... | collective-permute-start | bytes 1425416 | tf_op jit(solution)/shard_map/ppermute | solution.py:530
  97.0 4.6 %copy-start.6 = (bf16[512,1024]{1,0:T(8,128)(2,1)S(1)}, bf16[512,1024]{1,0:T(8,128)(2,1)}, u32[]{:S(2)}) copy-start(bf16[512,1024]{1,0:T(8,128)(2,1)} %get-tuple-element.86.down) | copy-start | bytes 3145732
  98.2 3.4 %collective-permute-start.25 = (bf16[128,3584]{1,0:T(8,128)(2,1)S(1)}, bf16[128,3584]{1,0:T(8,128)(2,1)S(1)}, u32[]{:S(2)}, u32[]{:S(2)}) collective-permute-start(bf16[128,3584]{1,0:T(8,128)(2,1)S(1)} %get-tuple-element.133), channel_id=1, source_target_pairs={{0,1},{1,0},{2,3},{3,2},{4,5},{5,4},{6,7},{7,6},{8,9},{9,8},{10,11... | collective-permute-start | bytes 2752520 | tf_op jit(solution)/shard_map/ppermute | solution.py:530
  98.4 5.9 %collective-permute-start.28 = (bf16[32,1024]{1,0:T(8,128)(2,1)S(1)}, bf16[32,1024]{1,0:T(8,128)(2,1)S(1)}, u32[]{:S(2)}, u32[]{:S(2)}) collective-permute-start(bf16[32,1024]{1,0:T(8,128)(2,1)S(1)} %last_step.2.refs_0_), channel_id=1, source_target_pairs={{4,0},{8,4},{12,8},{14,12},{10,14},{6,10},{2,6},{0,2},{5,1},{9,5},... | collective-permute-start | bytes 196616 | tf_op jit(solution)/shard_map/ppermute | solution.py:529
  100.0 4.3 %collective-permute-start.27 = (bf16[32,1024]{1,0:T(8,128)(2,1)S(1)}, bf16[32,1024]{1,0:T(8,128)(2,1)S(1)}, u32[]{:S(2)}, u32[]{:S(2)}) collective-permute-start(bf16[32,1024]{1,0:T(8,128)(2,1)S(1)} %get-tuple-element.134.refs_1_), channel_id=1, source_target_pairs={{0,4},{4,8},{8,12},{12,14},{14,10},{10,6},{6,2},{2,0},{1,5},{5,9},... | collective-permute-start | bytes 196616 | tf_op jit(solution)/shard_map/ppermute | solution.py:528
  101.5 2.8 %collective-permute-start.26 = (bf16[128,3584]{1,0:T(8,128)(2,1)S(1)}, bf16[128,3584]{1,0:T(8,128)(2,1)S(1)}, u32[]{:S(2)}, u32[]{:S(2)}) collective-permute-start(bf16[128,3584]{1,0:T(8,128)(2,1)S(1)} %get-tuple-element.137), channel_id=1, source_target_pairs={{0,1},{1,0},{2,3},{3,2},{4,5},{5,4},{6,7},{7,6},{8,9},{9,8},{10,11... | collective-permute-start | bytes 2752520 | tf_op jit(solution)/shard_map/ppermute | solution.py:530
  102.1 9.9 %collective-permute-start.29 = (bf16[32,4608]{1,0:T(8,128)(2,1)S(1)}, bf16[32,4608]{1,0:T(8,128)(2,1)S(1)}, u32[]{:S(2)}, u32[]{:S(2)}) collective-permute-start(bf16[32,4608]{1,0:T(8,128)(2,1)S(1)} %get-tuple-element.135), channel_id=1, source_target_pairs={{0,4},{4,8},{8,12},{12,14},{14,10},{10,6},{6,2},{2,0},{1,5},{5,9},... | collective-permute-start | bytes 884744 | tf_op jit(solution)/shard_map/ppermute | solution.py:528
  103.9 9.8 %collective-permute-start.30 = (bf16[32,4608]{1,0:T(8,128)(2,1)S(1)}, bf16[32,4608]{1,0:T(8,128)(2,1)S(1)}, u32[]{:S(2)}, u32[]{:S(2)}) collective-permute-start(bf16[32,4608]{1,0:T(8,128)(2,1)S(1)} %get-tuple-element.144), channel_id=1, source_target_pairs={{4,0},{8,4},{12,8},{14,12},{10,14},{6,10},{2,6},{0,2},{5,1},{9,5},... | collective-permute-start | bytes 884744 | tf_op jit(solution)/shard_map/ppermute | solution.py:529
  104.8 13.5 %collective-permute-start.32 = (bf16[32,4608]{1,0:T(8,128)(2,1)S(1)}, bf16[32,4608]{1,0:T(8,128)(2,1)S(1)}, u32[]{:S(2)}, u32[]{:S(2)}) collective-permute-start(bf16[32,4608]{1,0:T(8,128)(2,1)S(1)} %get-tuple-element.138), channel_id=1, source_target_pairs={{0,4},{4,8},{8,12},{12,14},{14,10},{10,6},{6,2},{2,0},{1,5},{5,9},... | collective-permute-start | bytes 884744 | tf_op jit(solution)/shard_map/ppermute | solution.py:528
  108.8 11.2 %collective-permute-start.31 = (bf16[256,3584]{1,0:T(8,128)(2,1)S(1)}, bf16[256,3584]{1,0:T(8,128)(2,1)S(1)}, u32[]{:S(2)}, u32[]{:S(2)}) collective-permute-start(bf16[256,3584]{1,0:T(8,128)(2,1)S(1)} %get-tuple-element.147), channel_id=1, source_target_pairs={{0,1},{1,0},{2,3},{3,2},{4,5},{5,4},{6,7},{7,6},{8,9},{9,8},{10,11... | collective-permute-start | bytes 5505032 | tf_op jit(solution)/shard_map/ppermute | solution.py:530
  108.9 11.1 %collective-permute-start.33 = (bf16[32,4608]{1,0:T(8,128)(2,1)S(1)}, bf16[32,4608]{1,0:T(8,128)(2,1)S(1)}, u32[]{:S(2)}, u32[]{:S(2)}) collective-permute-start(bf16[32,4608]{1,0:T(8,128)(2,1)S(1)} %get-tuple-element.148), channel_id=1, source_target_pairs={{4,0},{8,4},{12,8},{14,12},{10,14},{6,10},{2,6},{0,2},{5,1},{9,5},... | collective-permute-start | bytes 884744 | tf_op jit(solution)/shard_map/ppermute | solution.py:529
  114.3 10.4 %collective-permute-start.34 = (bf16[32,4608]{1,0:T(8,128)(2,1)S(1)}, bf16[32,4608]{1,0:T(8,128)(2,1)S(1)}, u32[]{:S(2)}, u32[]{:S(2)}) collective-permute-start(bf16[32,4608]{1,0:T(8,128)(2,1)S(1)} %get-tuple-element.145), channel_id=1, source_target_pairs={{0,4},{4,8},{8,12},{12,14},{14,10},{10,6},{6,2},{2,0},{1,5},{5,9},... | collective-permute-start | bytes 884744 | tf_op jit(solution)/shard_map/ppermute | solution.py:528
  115.9 10.4 %collective-permute-start.35 = (bf16[32,4608]{1,0:T(8,128)(2,1)S(1)}, bf16[32,4608]{1,0:T(8,128)(2,1)S(1)}, u32[]{:S(2)}, u32[]{:S(2)}) collective-permute-start(bf16[32,4608]{1,0:T(8,128)(2,1)S(1)} %get-tuple-element.151), channel_id=1, source_target_pairs={{4,0},{8,4},{12,8},{14,12},{10,14},{6,10},{2,6},{0,2},{5,1},{9,5},... | collective-permute-start | bytes 884744 | tf_op jit(solution)/shard_map/ppermute | solution.py:529
  120.6 10.4 %collective-permute-start.36 = (bf16[32,4608]{1,0:T(8,128)(2,1)S(1)}, bf16[32,4608]{1,0:T(8,128)(2,1)S(1)}, u32[]{:S(2)}, u32[]{:S(2)}) collective-permute-start(bf16[32,4608]{1,0:T(8,128)(2,1)S(1)} %get-tuple-element.149), channel_id=1, source_target_pairs={{0,4},{4,8},{8,12},{12,14},{14,10},{10,6},{6,2},{2,0},{1,5},{5,9},... | collective-permute-start | bytes 884744 | tf_op jit(solution)/shard_map/ppermute | solution.py:528
  122.3 10.4 %collective-permute-start.37 = (bf16[32,4608]{1,0:T(8,128)(2,1)S(1)}, bf16[32,4608]{1,0:T(8,128)(2,1)S(1)}, u32[]{:S(2)}, u32[]{:S(2)}) collective-permute-start(bf16[32,4608]{1,0:T(8,128)(2,1)S(1)} %get-tuple-element.155), channel_id=1, source_target_pairs={{4,0},{8,4},{12,8},{14,12},{10,14},{6,10},{2,6},{0,2},{5,1},{9,5},... | collective-permute-start | bytes 884744 | tf_op jit(solution)/shard_map/ppermute | solution.py:529
  126.9 10.4 %collective-permute-start.38 = (bf16[32,4608]{1,0:T(8,128)(2,1)S(1)}, bf16[32,4608]{1,0:T(8,128)(2,1)S(1)}, u32[]{:S(2)}, u32[]{:S(2)}) collective-permute-start(bf16[32,4608]{1,0:T(8,128)(2,1)S(1)} %get-tuple-element.152), channel_id=1, source_target_pairs={{0,4},{4,8},{8,12},{12,14},{14,10},{10,6},{6,2},{2,0},{1,5},{5,9},... | collective-permute-start | bytes 884744 | tf_op jit(solution)/shard_map/ppermute | solution.py:528
  128.6 10.4 %collective-permute-start.39 = (bf16[32,4608]{1,0:T(8,128)(2,1)S(1)}, bf16[32,4608]{1,0:T(8,128)(2,1)S(1)}, u32[]{:S(2)}, u32[]{:S(2)}) collective-permute-start(bf16[32,4608]{1,0:T(8,128)(2,1)S(1)} %get-tuple-element.158), channel_id=1, source_target_pairs={{4,0},{8,4},{12,8},{14,12},{10,14},{6,10},{2,6},{0,2},{5,1},{9,5},... | collective-permute-start | bytes 884744 | tf_op jit(solution)/shard_map/ppermute | solution.py:529
  133.2 12.1 %collective-permute-start.41 = (bf16[32,4608]{1,0:T(8,128)(2,1)S(1)}, bf16[32,4608]{1,0:T(8,128)(2,1)S(1)}, u32[]{:S(2)}, u32[]{:S(2)}) collective-permute-start(bf16[32,4608]{1,0:T(8,128)(2,1)S(1)} %get-tuple-element.156), channel_id=1, source_target_pairs={{0,4},{4,8},{8,12},{12,14},{14,10},{10,6},{6,2},{2,0},{1,5},{5,9},... | collective-permute-start | bytes 884744 | tf_op jit(solution)/shard_map/ppermute | solution.py:528
  134.9 10.5 %collective-permute-start.40 = (bf16[32,4608]{1,0:T(8,128)(2,1)S(1)}, bf16[32,4608]{1,0:T(8,128)(2,1)S(1)}, u32[]{:S(2)}, u32[]{:S(2)}) collective-permute-start(bf16[32,4608]{1,0:T(8,128)(2,1)S(1)} %get-tuple-element.161), channel_id=1, source_target_pairs={{4,0},{8,4},{12,8},{14,12},{10,14},{6,10},{2,6},{0,2},{5,1},{9,5},... | collective-permute-start | bytes 884744 | tf_op jit(solution)/shard_map/ppermute | solution.py:529
  139.6 8.5 %collective-permute-start.42 = (bf16[32,3584]{1,0:T(8,128)(2,1)S(1)}, bf16[32,3584]{1,0:T(8,128)(2,1)S(1)}, u32[]{:S(2)}, u32[]{:S(2)}) collective-permute-start(bf16[32,3584]{1,0:T(8,128)(2,1)S(1)} %get-tuple-element.159), channel_id=1, source_target_pairs={{0,4},{4,8},{8,12},{12,14},{14,10},{10,6},{6,2},{2,0},{1,5},{5,9},... | collective-permute-start | bytes 688136 | tf_op jit(solution)/shard_map/ppermute | solution.py:528
  141.2 8.3 %collective-permute-start.43 = (bf16[32,3584]{1,0:T(8,128)(2,1)S(1)}, bf16[32,3584]{1,0:T(8,128)(2,1)S(1)}, u32[]{:S(2)}, u32[]{:S(2)}) collective-permute-start(bf16[32,3584]{1,0:T(8,128)(2,1)S(1)} %get-tuple-element.162), channel_id=1, source_target_pairs={{4,0},{8,4},{12,8},{14,12},{10,14},{6,10},{2,6},{0,2},{5,1},{9,5},... | collective-permute-start | bytes 688136 | tf_op jit(solution)/shard_map/ppermute | solution.py:529
  (6 other events, 10.7 us)

commit v5 on v4

--- a/solution.py
+++ b/solution.py
@@ -226,8 +226,8 @@
     )(tokens, ids, gates)
 
 
-def first_kernel(shifts, start, shift, tokens, *refs):
-    parts, (weight, down, sums) = refs[:6], refs[6:]
+def first_kernel(shifts, shift, *refs):
+    parts, (weight, down) = refs[:6], refs[6:]
     height, width = parts[0].shape
     gap = weight.shape[0] - height
     for s in shifts:
@@ -243,27 +243,42 @@
                 if s < gap:
                     out[s + height :, here] = jnp.zeros((gap - s, size), BF16)
 
+
+def sums_kernel(start, tokens, weight, sums):
     window = pl.ds(pl.multiple_of(start[0], LANES), weight.shape[0])
     value = jnp.dot(tokens[:, window], weight[...], preferred_element_type=F32)
     sums[...] = value.astype(BF16)
 
 
-def first_step(start, shift, shifts, tokens, weights, width):
+def first_sums(start, tokens, weight):
+    vmem = pl.BlockSpec(memory_space=pltpu.VMEM)
+    return pl.pallas_call(
+        sums_kernel,
+        out_shape=jax.ShapeDtypeStruct((tokens.shape[0], weight.shape[1]), BF16),
+        in_specs=[pl.BlockSpec(memory_space=pltpu.SMEM), vmem, vmem],
+        out_specs=vmem,
+        compiler_params=params(16),
+        cost_estimate=cost(10000000000),
+        name="first_sums",
+    )(start, tokens, weight)
+
+
+def first_step(shift, shifts, weights, width):
     inner = weights[0].shape[1]
-    outs = [(width, 4 * inner), (width, 2 * inner), (tokens.shape[0], 4 * inner)]
+    outs = [(width, 4 * inner), (width, 2 * inner)]
     outs = [jax.ShapeDtypeStruct(shape, BF16) for shape in outs]
     smem = pl.BlockSpec(memory_space=pltpu.SMEM)
-    arrays = [tokens, *weights]
+    arrays = list(weights)
     return pl.pallas_call(
         functools.partial(first_kernel, shifts),
         out_shape=outs,
         grid=(1,),
-        in_specs=[smem, smem] + [whole(a) for a in arrays],
+        in_specs=[smem] + [whole(a) for a in arrays],
         out_specs=[whole(o) for o in outs],
         compiler_params=params(60),
         cost_estimate=cost(100000000000),
         name="first_step",
-    )(start, shift, *arrays)
+    )(shift, *arrays)
 
 
 def step_kernel(wide, sends, start, weight, on, back, *refs):
@@ -383,7 +398,7 @@
         in_specs=[pl.BlockSpec(memory_space=pltpu.SMEM)] + [vmem] * (3 + len(others)),
         out_specs=[vmem] * (1 + len(others)),
         compiler_params=params(16),
-        cost_estimate=cost(7000000000),
+        cost_estimate=cost(10000000000),
         name="last_step",
     )(start, weight, main, side, *others)
 
@@ -544,12 +559,12 @@
     wide = tokens.shape[1]
     ahead, behind = [send_on(p) for p in parts], [send_back(p) for p in parts]
     own = swap(tokens)
-    first_start = after(start, own)
-    both, down, sums = first_step(first_start, shift, sorted(shifts), tokens, weights, width)
-    sums = send_on(sums)
+    both, down = first_step(after(shift, own), sorted(shifts), weights, width)
+    sums = first_sums(start, tokens, both)
+    done, sums = sums, send_on(sums)
     pick = lambda arrays, work=10000000000: pick_rows(first, arrays, experts, slots, top, work)
     pairs, picked = {}, {}
-    terms, *sends, pair = open_step(after(start, down), both, ahead, behind)
+    terms, *sends, pair = open_step(after(start, done), both, ahead, behind)
     pairs[1] = [pair, swap(pair)]
     behind = [send_back(m) for m in sends]
     sends = onward_step(terms, sums, ahead)

time: 151 us -> 149 us (0.987)
    ppermute x16, waiting for transfers between devices: 28.2 us -> 21.5 us  [on_device(): send_back = lambda a: lax.ppermute(a, 'expert', backward)]
    ppermute x16, starting transfers between devices: 12.2 us -> 6.16 us  [on_device(): send_back = lambda a: lax.ppermute(a, 'expert', backward)]
    ppermute x17, waiting for transfers between devices: 30.6 us -> 36 us  [on_device(): send_on = lambda a: lax.ppermute(a, 'expert', onward)]
    ppermute x17, starting transfers between devices: 26.4 us -> 31.5 us  [on_device(): send_on = lambda a: lax.ppermute(a, 'expert', onward)]
    unnamed x20 -> x22, local copies, waits for them, and re-layouts: 3.98 us -> 3.98 us
where the time goes in v5:
time: 149 us; the launch traced here: 148 us
  waiting for transfers between devices  59.4 us (40%)
  Pallas kernels  45.5 us (31%)
  starting transfers between devices  39.2 us (26%)
  local copies, waits for them, and re-layouts  3.98 us (3%)
    ppermute x17, waiting for transfers between devices, on_device(): send_on = lambda a: lax.ppermute(a, 'expert', onward)  36 us
    ppermute x17, starting transfers between devices, on_device(): send_on = lambda a: lax.ppermute(a, 'expert', onward)  31.5 us
    ppermute x16, waiting for transfers between devices, on_device(): send_back = lambda a: lax.ppermute(a, 'expert', backward)  21.5 us
    pallas_call x1, Pallas kernels, run_experts(): pl.pallas_call(functools.partial(expert_kernel, count, pieces, top), out_...  19.6 us
    ppermute x16, starting transfers between devices, on_device(): send_back = lambda a: lax.ppermute(a, 'expert', backward)  6.16 us
    pallas_call x4, Pallas kernels, pick_rows(): pl.pallas_call(functools.partial(pick_kernel, len(tokens), experts, top),...  5.35 us
    pallas_call x3, Pallas kernels, merge_rows(): pl.pallas_call(functools.partial(merge_kernel, count), out_shape=outs, gr...  4.3 us
    pallas_call x8, Pallas kernels, add_step(): pl.pallas_call(functools.partial(add_kernel, places, base, counts, joined...  4.28 us
  transfers between devices with their start and end apart: 44, of which 24 were waited for; matrix products, arithmetic and copies ran while one was open for 0% of the time, Pallas kernels for 13%

profile of v5, /device:TPU:0, one launch (start us, length us, event | category | flops | bytes accessed | tf_op | source)
XLA Modules:
  0.0 148.4 jit_solution(3384529819399675058)
XLA Ops:
  0.0 2.1 %note_tokens.1 = (bf16[32,3712]{1,0:T(8,128)(2,1)}, bf16[32,3712]{1,0:T(8,128)(2,1)}, bf16[64,3712]{1,0:T(8,128)(2,1)}) custom-call(bf16[64,3584]{1,0:T(8,128)(2,1)} %tokens.1, s32[8,64]{1,0:T(8,128)} %bitcast.6, f32[8,64]{1,0:T(8,128)} %bitcast.7), custom_call_target="tpu_custom_call" | custom-call | flops 1000 | bytes 1000 | tf_op jit(solution)/shard_map/note_tokens/pallas_call | solution.py:217
  3.1 3.0 %collective-permute-start.4 = (bf16[32,3712]{1,0:T(8,128)(2,1)}, bf16[32,3712]{1,0:T(8,128)(2,1)S(1)}, u32[]{:S(2)}, u32[]{:S(2)}) collective-permute-start(bf16[32,3712]{1,0:T(8,128)(2,1)} %get-tuple-element.87), channel_id=1, source_target_pairs={{0,4},{4,8},{8,12},{12,14},{14,10},{10,6},{6,2},{2,0},{1,5},{5,9},... | collective-permute-start | bytes 712712 | tf_op jit(solution)/shard_map/ppermute | solution.py:543
  9.9 3.6 %first_step.1 = (bf16[512,2048]{1,0:T(8,128)(2,1)}, bf16[512,1024]{1,0:T(8,128)(2,1)}) custom-call(s32[1]{0:T(128)} %bitcast.4.shift, bf16[448,512]{1,0:T(8,128)(2,1)} %refs_0_.1, bf16[448,512]{1,0:T(8,128)(2,1)} %copy-done.8, bf16[448,512]{1,0:T(8,128)(2,1)} %refs_2_.1, bf16[448,512]{1,0:T(8,128)(2,1)} %copy-done.9, bf16[448,512]{1,0:T(8,128)(2,1)} %bitcast.9, ...), custom_call_target="tpu_custom_call" | custom-call | flops 99999997952 | bytes 1000 | tf_op jit(solution)/shard_map/first_step/pallas_call | solution.py:272
  13.5 1.6 %copy-done.4 = bf16[512,2048]{1,0:T(8,128)(2,1)S(1)} copy-done((bf16[512,2048]{1,0:T(8,128)(2,1)S(1)}, bf16[512,2048]{1,0:T(8,128)(2,1)}, u32[]{:S(2)}) %copy-start.4) | copy-done | bytes 2097176
  15.6 1.4 collective-permute-start.8
  17.3 1.5 %collective-permute-done.7.refs_3_ = bf16[32,3712]{1,0:T(8,128)(2,1)S(1)} collective-permute-done((bf16[32,3712]{1,0:T(8,128)(2,1)}, bf16[32,3712]{1,0:T(8,128)(2,1)S(1)}, u32[]{:S(2)}, u32[]{:S(2)}) %collective-permute-start.7) | collective-permute-done | bytes 237600 | tf_op jit(solution)/shard_map/ppermute | solution.py:544
  20.0 1.4 collective-permute-start.10
  21.4 1.7 %collective-permute-done.8.sums = bf16[64,2048]{1,0:T(8,128)(2,1)S(1)} collective-permute-done((bf16[64,2048]{1,0:T(8,128)(2,1)S(1)}, bf16[64,2048]{1,0:T(8,128)(2,1)S(1)}, u32[]{:S(2)}, u32[]{:S(2)}) %collective-permute-start.8) | collective-permute-done | bytes 262176 | tf_op jit(solution)/shard_map/ppermute | solution.py:543
  24.0 1.6 %collective-permute-start.9 = (bf16[32,5760]{1,0:T(8,128)(2,1)}, bf16[32,5760]{1,0:T(8,128)(2,1)S(1)}, u32[]{:S(2)}, u32[]{:S(2)}) collective-permute-start(bf16[32,5760]{1,0:T(8,128)(2,1)} %get-tuple-element.91), channel_id=1, source_target_pairs={{0,4},{4,8},{8,12},{12,14},{14,10},{10,6},{6,2},{2,0},{1,5},{5,9},... | collective-permute-start | bytes 1105928 | tf_op jit(solution)/shard_map/ppermute | solution.py:543
  26.0 1.6 %collective-permute-start.12 = (bf16[32,5760]{1,0:T(8,128)(2,1)S(1)}, bf16[32,5760]{1,0:T(8,128)(2,1)S(1)}, u32[]{:S(2)}, u32[]{:S(2)}) collective-permute-start(bf16[32,5760]{1,0:T(8,128)(2,1)S(1)} %get-tuple-element.98), channel_id=1, source_target_pairs={{0,4},{4,8},{8,12},{12,14},{14,10},{10,6},{6,2},{2,0},{1,5},{5,9},... | collective-permute-start | bytes 1105928 | tf_op jit(solution)/shard_map/ppermute | solution.py:543
  27.6 3.2 %collective-permute-done.10.back.refs_1_ = bf16[32,5760]{1,0:T(8,128)(2,1)S(1)} collective-permute-done((bf16[32,5760]{1,0:T(8,128)(2,1)}, bf16[32,5760]{1,0:T(8,128)(2,1)S(1)}, u32[]{:S(2)}, u32[]{:S(2)}) %collective-permute-start.10) | collective-permute-done | bytes 368672 | tf_op jit(solution)/shard_map/ppermute | solution.py:544
  30.8 5.0 %collective-permute-done.9.on.refs_0_ = bf16[32,5760]{1,0:T(8,128)(2,1)S(1)} collective-permute-done((bf16[32,5760]{1,0:T(8,128)(2,1)}, bf16[32,5760]{1,0:T(8,128)(2,1)S(1)}, u32[]{:S(2)}, u32[]{:S(2)}) %collective-permute-start.9) | collective-permute-done | bytes 368672 | tf_op jit(solution)/shard_map/ppermute | solution.py:543
  35.7 1.6 %copy-done.5 = bf16[512,2048]{1,0:T(8,128)(2,1)S(1)} copy-done((bf16[512,2048]{1,0:T(8,128)(2,1)S(1)}, bf16[512,2048]{1,0:T(8,128)(2,1)}, u32[]{:S(2)}) %copy-start.5) | copy-done | bytes 2097176
  37.8 1.6 %collective-permute-start.14 = (bf16[32,5760]{1,0:T(8,128)(2,1)S(1)}, bf16[32,5760]{1,0:T(8,128)(2,1)S(1)}, u32[]{:S(2)}, u32[]{:S(2)}) collective-permute-start(bf16[32,5760]{1,0:T(8,128)(2,1)S(1)} %get-tuple-element.94), channel_id=1, source_target_pairs={{0,4},{4,8},{8,12},{12,14},{14,10},{10,6},{6,2},{2,0},{1,5},{5,9},... | collective-permute-start | bytes 1105928 | tf_op jit(solution)/shard_map/ppermute | solution.py:543
  41.2 2.4 %collective-permute-done.12.on = bf16[32,5760]{1,0:T(8,128)(2,1)S(1)} collective-permute-done((bf16[32,5760]{1,0:T(8,128)(2,1)S(1)}, bf16[32,5760]{1,0:T(8,128)(2,1)S(1)}, u32[]{:S(2)}, u32[]{:S(2)}) %collective-permute-start.12) | collective-permute-done | bytes 368672 | tf_op jit(solution)/shard_map/ppermute | solution.py:543
  44.2 1.6 %collective-permute-start.17 = (bf16[32,5760]{1,0:T(8,128)(2,1)S(1)}, bf16[32,5760]{1,0:T(8,128)(2,1)S(1)}, u32[]{:S(2)}, u32[]{:S(2)}) collective-permute-start(bf16[32,5760]{1,0:T(8,128)(2,1)S(1)} %get-tuple-element.101), channel_id=1, source_target_pairs={{0,4},{4,8},{8,12},{12,14},{14,10},{10,6},{6,2},{2,0},{1,5},{5,9},... | collective-permute-start | bytes 1105928 | tf_op jit(solution)/shard_map/ppermute | solution.py:543
  46.3 4.1 %collective-permute-done.14.on.refs_0_ = bf16[32,5760]{1,0:T(8,128)(2,1)S(1)} collective-permute-done((bf16[32,5760]{1,0:T(8,128)(2,1)S(1)}, bf16[32,5760]{1,0:T(8,128)(2,1)S(1)}, u32[]{:S(2)}, u32[]{:S(2)}) %collective-permute-start.14) | collective-permute-done | bytes 368672 | tf_op jit(solution)/shard_map/ppermute | solution.py:543
  50.9 2.0 %collective-permute-start.19 = (bf16[32,5760]{1,0:T(8,128)(2,1)S(1)}, bf16[32,5760]{1,0:T(8,128)(2,1)S(1)}, u32[]{:S(2)}, u32[]{:S(2)}) collective-permute-start(bf16[32,5760]{1,0:T(8,128)(2,1)S(1)} %get-tuple-element.104), channel_id=1, source_target_pairs={{0,4},{4,8},{8,12},{12,14},{14,10},{10,6},{6,2},{2,0},{1,5},{5,9},... | collective-permute-start | bytes 1105928 | tf_op jit(solution)/shard_map/ppermute | solution.py:543
  53.0 1.3 pick_rows.5
  54.3 4.0 %collective-permute-done.17.on = bf16[32,5760]{1,0:T(8,128)(2,1)S(1)} collective-permute-done((bf16[32,5760]{1,0:T(8,128)(2,1)S(1)}, bf16[32,5760]{1,0:T(8,128)(2,1)S(1)}, u32[]{:S(2)}, u32[]{:S(2)}) %collective-permute-start.17) | collective-permute-done | bytes 368672 | tf_op jit(solution)/shard_map/ppermute | solution.py:543
  58.9 2.0 %collective-permute-start.23 = (bf16[32,2048]{1,0:T(8,128)(2,1)S(1)}, bf16[32,2048]{1,0:T(8,128)(2,1)S(1)}, u32[]{:S(2)}, u32[]{:S(2)}) collective-permute-start(bf16[32,2048]{1,0:T(8,128)(2,1)S(1)} %get-tuple-element.110), channel_id=1, source_target_pairs={{0,4},{4,8},{8,12},{12,14},{14,10},{10,6},{6,2},{2,0},{1,5},{5,9},... | collective-permute-start | bytes 393224 | tf_op jit(solution)/shard_map/ppermute | solution.py:543
  61.0 5.1 %collective-permute-done.19.main.refs_0_ = bf16[32,5760]{1,0:T(8,128)(2,1)S(1)} collective-permute-done((bf16[32,5760]{1,0:T(8,128)(2,1)S(1)}, bf16[32,5760]{1,0:T(8,128)(2,1)S(1)}, u32[]{:S(2)}, u32[]{:S(2)}) %collective-permute-start.19) | collective-permute-done | bytes 368672 | tf_op jit(solution)/shard_map/ppermute | solution.py:543
  68.0 3.6 %collective-permute-done.22.main = bf16[32,5760]{1,0:T(8,128)(2,1)S(1)} collective-permute-done((bf16[32,5760]{1,0:T(8,128)(2,1)S(1)}, bf16[32,5760]{1,0:T(8,128)(2,1)S(1)}, u32[]{:S(2)}, u32[]{:S(2)}) %collective-permute-start.22) | collective-permute-done | bytes 368672 | tf_op jit(solution)/shard_map/ppermute | solution.py:544
  72.1 1.8 %collective-permute-done.24.refs_3_ = bf16[64,3712]{1,0:T(8,128)(2,1)S(1)} collective-permute-done((bf16[64,3712]{1,0:T(8,128)(2,1)S(1)}, bf16[64,3712]{1,0:T(8,128)(2,1)S(1)}, u32[]{:S(2)}, u32[]{:S(2)}) %collective-permute-start.24) | collective-permute-done | bytes 475168 | tf_op jit(solution)/shard_map/ppermute | solution.py:545
  74.0 1.3 pick_rows.7
  75.3 19.6 %run_experts.1 = (bf16[4,80,3584]{2,1,0:T(8,128)(2,1)S(1)}, bf16[4,80,3584]{2,1,0:T(8,128)(2,1)S(1)}, bf16[4,80,3584]{2,1,0:T(8,128)(2,1)S(1)}, bf16[4,80,3584]{2,1,0:T(8,128)(2,1)S(1)}) custom-call(s32[1]{0:T(128)} %bitcast.1.first, bf16[4,80,3712]{2,1,0:T(8,128)(2,1)S(1)} %get-tuple-element.119.refs_0_, ...), custom_call_target="tpu_custom_call" | custom-call | flops 99999997952 | bytes 1000 | tf_op jit(solution)/shard_map/run_experts/pallas_call | solution.py:181
  96.6 1.7 %collective-permute-start.27 = (bf16[32,1024]{1,0:T(8,128)(2,1)S(1)}, bf16[32,1024]{1,0:T(8,128)(2,1)S(1)}, u32[]{:S(2)}, u32[]{:S(2)}) collective-permute-start(bf16[32,1024]{1,0:T(8,128)(2,1)S(1)} %get-tuple-element.132.refs_1_), channel_id=1, source_target_pairs={{0,4},{4,8},{8,12},{12,14},{14,10},{10,6},{6,2},{2,0},{1,5},{5,9},... | collective-permute-start | bytes 196616 | tf_op jit(solution)/shard_map/ppermute | solution.py:543
  100.1 1.6 %collective-permute-start.29 = (bf16[32,4608]{1,0:T(8,128)(2,1)S(1)}, bf16[32,4608]{1,0:T(8,128)(2,1)S(1)}, u32[]{:S(2)}, u32[]{:S(2)}) collective-permute-start(bf16[32,4608]{1,0:T(8,128)(2,1)S(1)} %get-tuple-element.133), channel_id=1, source_target_pairs={{0,4},{4,8},{8,12},{12,14},{14,10},{10,6},{6,2},{2,0},{1,5},{5,9},... | collective-permute-start | bytes 884744 | tf_op jit(solution)/shard_map/ppermute | solution.py:543
  102.7 1.9 %collective-permute-start.32 = (bf16[32,4608]{1,0:T(8,128)(2,1)S(1)}, bf16[32,4608]{1,0:T(8,128)(2,1)S(1)}, u32[]{:S(2)}, u32[]{:S(2)}) collective-permute-start(bf16[32,4608]{1,0:T(8,128)(2,1)S(1)} %get-tuple-element.136), channel_id=1, source_target_pairs={{0,4},{4,8},{8,12},{12,14},{14,10},{10,6},{6,2},{2,0},{1,5},{5,9},... | collective-permute-start | bytes 884744 | tf_op jit(solution)/shard_map/ppermute | solution.py:543
  104.5 2.1 %merge_rows.5 = (f32[128,3584]{1,0:T(8,128)S(1)}, f32[128,3584]{1,0:T(8,128)S(1)}, bf16[256,3584]{1,0:T(8,128)(2,1)S(1)}) custom-call(bf16[256,320]{1,0:T(8,128)(2,1)S(1)} %get-tuple-element.137.refs_0_, bf16[256,320]{1,0:T(8,128)(2,1)S(1)} %get-tuple-element.96.refs_1_, bf16[4,80,3584]{2,1,0:T(8,128)(2,1)S(1)} %get-tuple-element.138.refs_2_, ...), custom_call_target="tpu_custom_call" | custom-call | flops 1000 | bytes 1000 | tf_op jit(solution)/shard_map/merge_rows/pallas_call | solution.py:427
  107.2 2.7 %collective-permute-done.29.refs_0_ = bf16[32,4608]{1,0:T(8,128)(2,1)S(1)} collective-permute-done((bf16[32,4608]{1,0:T(8,128)(2,1)S(1)}, bf16[32,4608]{1,0:T(8,128)(2,1)S(1)}, u32[]{:S(2)}, u32[]{:S(2)}) %collective-permute-start.29) | collective-permute-done | bytes 294944 | tf_op jit(solution)/shard_map/ppermute | solution.py:543
  109.9 1.6 %collective-permute-done.30.refs_1_ = bf16[32,4608]{1,0:T(8,128)(2,1)S(1)} collective-permute-done((bf16[32,4608]{1,0:T(8,128)(2,1)S(1)}, bf16[32,4608]{1,0:T(8,128)(2,1)S(1)}, u32[]{:S(2)}, u32[]{:S(2)}) %collective-permute-start.30) | collective-permute-done | bytes 294944 | tf_op jit(solution)/shard_map/ppermute | solution.py:544
  112.1 2.0 %collective-permute-start.34 = (bf16[32,4608]{1,0:T(8,128)(2,1)S(1)}, bf16[32,4608]{1,0:T(8,128)(2,1)S(1)}, u32[]{:S(2)}, u32[]{:S(2)}) collective-permute-start(bf16[32,4608]{1,0:T(8,128)(2,1)S(1)} %get-tuple-element.143), channel_id=1, source_target_pairs={{0,4},{4,8},{8,12},{12,14},{14,10},{10,6},{6,2},{2,0},{1,5},{5,9},... | collective-permute-start | bytes 884744 | tf_op jit(solution)/shard_map/ppermute | solution.py:543
  114.1 2.1 %collective-permute-done.32.refs_0_ = bf16[32,4608]{1,0:T(8,128)(2,1)S(1)} collective-permute-done((bf16[32,4608]{1,0:T(8,128)(2,1)S(1)}, bf16[32,4608]{1,0:T(8,128)(2,1)S(1)}, u32[]{:S(2)}, u32[]{:S(2)}) %collective-permute-start.32) | collective-permute-done | bytes 294944 | tf_op jit(solution)/shard_map/ppermute | solution.py:543
  116.2 1.6 %collective-permute-done.33.refs_1_ = bf16[32,4608]{1,0:T(8,128)(2,1)S(1)} collective-permute-done((bf16[32,4608]{1,0:T(8,128)(2,1)S(1)}, bf16[32,4608]{1,0:T(8,128)(2,1)S(1)}, u32[]{:S(2)}, u32[]{:S(2)}) %collective-permute-start.33) | collective-permute-done | bytes 294944 | tf_op jit(solution)/shard_map/ppermute | solution.py:544
  118.4 2.0 %collective-permute-start.36 = (bf16[32,4608]{1,0:T(8,128)(2,1)S(1)}, bf16[32,4608]{1,0:T(8,128)(2,1)S(1)}, u32[]{:S(2)}, u32[]{:S(2)}) collective-permute-start(bf16[32,4608]{1,0:T(8,128)(2,1)S(1)} %get-tuple-element.147), channel_id=1, source_target_pairs={{0,4},{4,8},{8,12},{12,14},{14,10},{10,6},{6,2},{2,0},{1,5},{5,9},... | collective-permute-start | bytes 884744 | tf_op jit(solution)/shard_map/ppermute | solution.py:543
  120.5 2.1 %collective-permute-done.34.refs_0_ = bf16[32,4608]{1,0:T(8,128)(2,1)S(1)} collective-permute-done((bf16[32,4608]{1,0:T(8,128)(2,1)S(1)}, bf16[32,4608]{1,0:T(8,128)(2,1)S(1)}, u32[]{:S(2)}, u32[]{:S(2)}) %collective-permute-start.34) | collective-permute-done | bytes 294944 | tf_op jit(solution)/shard_map/ppermute | solution.py:543
  122.6 1.6 %collective-permute-done.35.refs_1_ = bf16[32,4608]{1,0:T(8,128)(2,1)S(1)} collective-permute-done((bf16[32,4608]{1,0:T(8,128)(2,1)S(1)}, bf16[32,4608]{1,0:T(8,128)(2,1)S(1)}, u32[]{:S(2)}, u32[]{:S(2)}) %collective-permute-start.35) | collective-permute-done | bytes 294944 | tf_op jit(solution)/shard_map/ppermute | solution.py:544
  124.7 2.0 %collective-permute-start.38 = (bf16[32,4608]{1,0:T(8,128)(2,1)S(1)}, bf16[32,4608]{1,0:T(8,128)(2,1)S(1)}, u32[]{:S(2)}, u32[]{:S(2)}) collective-permute-start(bf16[32,4608]{1,0:T(8,128)(2,1)S(1)} %get-tuple-element.150), channel_id=1, source_target_pairs={{0,4},{4,8},{8,12},{12,14},{14,10},{10,6},{6,2},{2,0},{1,5},{5,9},... | collective-permute-start | bytes 884744 | tf_op jit(solution)/shard_map/ppermute | solution.py:543
  126.8 2.1 %collective-permute-done.36.refs_0_ = bf16[32,4608]{1,0:T(8,128)(2,1)S(1)} collective-permute-done((bf16[32,4608]{1,0:T(8,128)(2,1)S(1)}, bf16[32,4608]{1,0:T(8,128)(2,1)S(1)}, u32[]{:S(2)}, u32[]{:S(2)}) %collective-permute-start.36) | collective-permute-done | bytes 294944 | tf_op jit(solution)/shard_map/ppermute | solution.py:543
  128.9 1.6 %collective-permute-done.37.refs_1_ = bf16[32,4608]{1,0:T(8,128)(2,1)S(1)} collective-permute-done((bf16[32,4608]{1,0:T(8,128)(2,1)S(1)}, bf16[32,4608]{1,0:T(8,128)(2,1)S(1)}, u32[]{:S(2)}, u32[]{:S(2)}) %collective-permute-start.37) | collective-permute-done | bytes 294944 | tf_op jit(solution)/shard_map/ppermute | solution.py:544
  131.0 2.0 %collective-permute-start.41 = (bf16[32,4608]{1,0:T(8,128)(2,1)S(1)}, bf16[32,4608]{1,0:T(8,128)(2,1)S(1)}, u32[]{:S(2)}, u32[]{:S(2)}) collective-permute-start(bf16[32,4608]{1,0:T(8,128)(2,1)S(1)} %get-tuple-element.154), channel_id=1, source_target_pairs={{0,4},{4,8},{8,12},{12,14},{14,10},{10,6},{6,2},{2,0},{1,5},{5,9},... | collective-permute-start | bytes 884744 | tf_op jit(solution)/shard_map/ppermute | solution.py:543
  133.1 2.1 %collective-permute-done.38.refs_0_ = bf16[32,4608]{1,0:T(8,128)(2,1)S(1)} collective-permute-done((bf16[32,4608]{1,0:T(8,128)(2,1)S(1)}, bf16[32,4608]{1,0:T(8,128)(2,1)S(1)}, u32[]{:S(2)}, u32[]{:S(2)}) %collective-permute-start.38) | collective-permute-done | bytes 294944 | tf_op jit(solution)/shard_map/ppermute | solution.py:543
  135.2 1.6 %collective-permute-done.39.refs_1_ = bf16[32,4608]{1,0:T(8,128)(2,1)S(1)} collective-permute-done((bf16[32,4608]{1,0:T(8,128)(2,1)S(1)}, bf16[32,4608]{1,0:T(8,128)(2,1)S(1)}, u32[]{:S(2)}, u32[]{:S(2)}) %collective-permute-start.39) | collective-permute-done | bytes 294944 | tf_op jit(solution)/shard_map/ppermute | solution.py:544
  137.3 2.0 %collective-permute-start.42 = (bf16[32,3584]{1,0:T(8,128)(2,1)S(1)}, bf16[32,3584]{1,0:T(8,128)(2,1)S(1)}, u32[]{:S(2)}, u32[]{:S(2)}) collective-permute-start(bf16[32,3584]{1,0:T(8,128)(2,1)S(1)} %get-tuple-element.157), channel_id=1, source_target_pairs={{0,4},{4,8},{8,12},{12,14},{14,10},{10,6},{6,2},{2,0},{1,5},{5,9},... | collective-permute-start | bytes 688136 | tf_op jit(solution)/shard_map/ppermute | solution.py:543
  139.4 3.7 %collective-permute-done.40.refs_0_ = bf16[32,4608]{1,0:T(8,128)(2,1)S(1)} collective-permute-done((bf16[32,4608]{1,0:T(8,128)(2,1)S(1)}, bf16[32,4608]{1,0:T(8,128)(2,1)S(1)}, u32[]{:S(2)}, u32[]{:S(2)}) %collective-permute-start.40) | collective-permute-done | bytes 294944 | tf_op jit(solution)/shard_map/ppermute | solution.py:544
  143.7 2.3 %collective-permute-done.42.first = bf16[32,3584]{1,0:T(8,128)(2,1)S(1)} collective-permute-done((bf16[32,3584]{1,0:T(8,128)(2,1)S(1)}, bf16[32,3584]{1,0:T(8,128)(2,1)S(1)}, u32[]{:S(2)}, u32[]{:S(2)}) %collective-permute-start.42) | collective-permute-done | bytes 229408 | tf_op jit(solution)/shard_map/ppermute | solution.py:543
  146.0 1.5 %collective-permute-done.43.second = bf16[32,3584]{1,0:T(8,128)(2,1)S(1)} collective-permute-done((bf16[32,3584]{1,0:T(8,128)(2,1)S(1)}, bf16[32,3584]{1,0:T(8,128)(2,1)S(1)}, u32[]{:S(2)}, u32[]{:S(2)}) %collective-permute-start.43) | collective-permute-done | bytes 229408 | tf_op jit(solution)/shard_map/ppermute | solution.py:544
  (90 shorter events, 24.0 us)
Async XLA Ops:
  2.1 4.0 %collective-permute-start = (bf16[64,3712]{1,0:T(8,128)(2,1)}, bf16[64,3712]{1,0:T(8,128)(2,1)S(1)}, u32[]{:S(2)}, u32[]{:S(2)}) collective-permute-start(bf16[64,3712]{1,0:T(8,128)(2,1)} %get-tuple-element.83.tokens.refs_0_), channel_id=1, source_target_pairs={{0,1},{1,0},{2,3},{3,2},{4,5},{5,4},{6,7},{7,6},{8,9},{9,8},{10,11... | collective-permute-start | bytes 1425416 | tf_op jit(solution)/shard_map/ppermute | solution.py:545
  2.5 4.6 %collective-permute-start.1 = (bf16[448,512]{1,0:T(8,128)(2,1)}, bf16[448,512]{1,0:T(8,128)(2,1)S(1)}, u32[]{:S(2)}, u32[]{:S(2)}) collective-permute-start(bf16[448,512]{1,0:T(8,128)(2,1)} %refs_0_.1), channel_id=1, source_target_pairs={{0,1},{1,0},{2,3},{3,2},{4,5},{5,4},{6,7},{7,6},{8,9},{9,8},{10,11... | collective-permute-start | bytes 1376264 | tf_op jit(solution)/shard_map/ppermute | solution.py:545
  2.6 5.6 %collective-permute-start.2 = (bf16[448,512]{1,0:T(8,128)(2,1)}, bf16[448,512]{1,0:T(8,128)(2,1)S(1)}, u32[]{:S(2)}, u32[]{:S(2)}) collective-permute-start(bf16[448,512]{1,0:T(8,128)(2,1)} %refs_2_.1), channel_id=1, source_target_pairs={{0,1},{1,0},{2,3},{3,2},{4,5},{5,4},{6,7},{7,6},{8,9},{9,8},{10,11... | collective-permute-start | bytes 1376264 | tf_op jit(solution)/shard_map/ppermute | solution.py:545
  3.0 6.1 %collective-permute-start.3 = (bf16[448,512]{1,0:T(8,128)(2,1)}, bf16[448,512]{1,0:T(8,128)(2,1)S(1)}, u32[]{:S(2)}, u32[]{:S(2)}) collective-permute-start(bf16[448,512]{1,0:T(8,128)(2,1)} %bitcast.8), channel_id=1, source_target_pairs={{0,1},{1,0},{2,3},{3,2},{4,5},{5,4},{6,7},{7,6},{8,9},{9,8},{10,11... | collective-permute-start | bytes 1376264 | tf_op jit(solution)/shard_map/ppermute | solution.py:545
  3.1 13.9 %collective-permute-start.4 = (bf16[32,3712]{1,0:T(8,128)(2,1)}, bf16[32,3712]{1,0:T(8,128)(2,1)S(1)}, u32[]{:S(2)}, u32[]{:S(2)}) collective-permute-start(bf16[32,3712]{1,0:T(8,128)(2,1)} %get-tuple-element.87), channel_id=1, source_target_pairs={{0,4},{4,8},{8,12},{12,14},{14,10},{10,6},{6,2},{2,0},{1,5},{5,9},... | collective-permute-start | bytes 712712 | tf_op jit(solution)/shard_map/ppermute | solution.py:543
  6.1 7.4 %copy-start.2 = (bf16[64,3712]{1,0:T(8,128)(2,1)}, bf16[64,3712]{1,0:T(8,128)(2,1)S(1)}, u32[]{:S(2)}) copy-start(bf16[64,3712]{1,0:T(8,128)(2,1)S(1)} %collective-permute-done.refs_2_) | copy-start | bytes 1425412
  6.1 11.2 %collective-permute-start.6 = (bf16[32,3712]{1,0:T(8,128)(2,1)}, bf16[32,3712]{1,0:T(8,128)(2,1)S(1)}, u32[]{:S(2)}, u32[]{:S(2)}) collective-permute-start(bf16[32,3712]{1,0:T(8,128)(2,1)} %get-tuple-element.87), channel_id=1, source_target_pairs={{4,0},{8,4},{12,8},{14,12},{10,14},{6,10},{2,6},{0,2},{5,1},{9,5},... | collective-permute-start | bytes 712712 | tf_op jit(solution)/shard_map/ppermute | solution.py:544
  7.1 6.4 %copy-start = (bf16[64,3712]{1,0:T(8,128)(2,1)S(1)}, bf16[64,3712]{1,0:T(8,128)(2,1)}, u32[]{:S(2)}) copy-start(bf16[64,3712]{1,0:T(8,128)(2,1)} %get-tuple-element.83.tokens.refs_0_) | copy-start | bytes 1425412
  7.1 10.2 %collective-permute-start.5 = (bf16[32,3712]{1,0:T(8,128)(2,1)}, bf16[32,3712]{1,0:T(8,128)(2,1)S(1)}, u32[]{:S(2)}, u32[]{:S(2)}) collective-permute-start(bf16[32,3712]{1,0:T(8,128)(2,1)} %get-tuple-element.88), channel_id=1, source_target_pairs={{0,4},{4,8},{8,12},{12,14},{14,10},{10,6},{6,2},{2,0},{1,5},{5,9},... | collective-permute-start | bytes 712712 | tf_op jit(solution)/shard_map/ppermute | solution.py:543
  8.2 10.7 %collective-permute-start.7 = (bf16[32,3712]{1,0:T(8,128)(2,1)}, bf16[32,3712]{1,0:T(8,128)(2,1)S(1)}, u32[]{:S(2)}, u32[]{:S(2)}) collective-permute-start(bf16[32,3712]{1,0:T(8,128)(2,1)} %get-tuple-element.88), channel_id=1, source_target_pairs={{4,0},{8,4},{12,8},{14,12},{10,14},{6,10},{2,6},{0,2},{5,1},{9,5},... | collective-permute-start | bytes 712712 | tf_op jit(solution)/shard_map/ppermute | solution.py:544
  15.6 7.6 %collective-permute-start.8 = (bf16[64,2048]{1,0:T(8,128)(2,1)S(1)}, bf16[64,2048]{1,0:T(8,128)(2,1)S(1)}, u32[]{:S(2)}, u32[]{:S(2)}) collective-permute-start(bf16[64,2048]{1,0:T(8,128)(2,1)S(1)} %first_sums.1), channel_id=1, source_target_pairs={{0,4},{4,8},{8,12},{12,14},{14,10},{10,6},{6,2},{2,0},{1,5},{5,9},... | collective-permute-start | bytes 786440 | tf_op jit(solution)/shard_map/ppermute | solution.py:543
  20.0 10.7 %collective-permute-start.10 = (bf16[32,5760]{1,0:T(8,128)(2,1)}, bf16[32,5760]{1,0:T(8,128)(2,1)S(1)}, u32[]{:S(2)}, u32[]{:S(2)}) collective-permute-start(bf16[32,5760]{1,0:T(8,128)(2,1)} %get-tuple-element.93), channel_id=1, source_target_pairs={{4,0},{8,4},{12,8},{14,12},{10,14},{6,10},{2,6},{0,2},{5,1},{9,5},... | collective-permute-start | bytes 1105928 | tf_op jit(solution)/shard_map/ppermute | solution.py:544
  24.0 11.7 %collective-permute-start.9 = (bf16[32,5760]{1,0:T(8,128)(2,1)}, bf16[32,5760]{1,0:T(8,128)(2,1)S(1)}, u32[]{:S(2)}, u32[]{:S(2)}) collective-permute-start(bf16[32,5760]{1,0:T(8,128)(2,1)} %get-tuple-element.91), channel_id=1, source_target_pairs={{0,4},{4,8},{8,12},{12,14},{14,10},{10,6},{6,2},{2,0},{1,5},{5,9},... | collective-permute-start | bytes 1105928 | tf_op jit(solution)/shard_map/ppermute | solution.py:543
  25.6 14.3 %collective-permute-start.11 = (bf16[128,3712]{1,0:T(8,128)(2,1)S(1)}, bf16[128,3712]{1,0:T(8,128)(2,1)S(1)}, u32[]{:S(2)}, u32[]{:S(2)}) collective-permute-start(bf16[128,3712]{1,0:T(8,128)(2,1)S(1)} %get-tuple-element.95.refs_0_), channel_id=1, source_target_pairs={{0,1},{1,0},{2,3},{3,2},{4,5},{5,4},{6,7},{7,6},{8,9},{9,8},{10,11... | collective-permute-start | bytes 2850824 | tf_op jit(solution)/shard_map/ppermute | solution.py:545
  25.6 15.6 %collective-permute-start.13 = (bf16[32,5760]{1,0:T(8,128)(2,1)S(1)}, bf16[32,5760]{1,0:T(8,128)(2,1)S(1)}, u32[]{:S(2)}, u32[]{:S(2)}) collective-permute-start(bf16[32,5760]{1,0:T(8,128)(2,1)S(1)} %get-tuple-element.99), channel_id=1, source_target_pairs={{4,0},{8,4},{12,8},{14,12},{10,14},{6,10},{2,6},{0,2},{5,1},{9,5},... | collective-permute-start | bytes 1105928 | tf_op jit(solution)/shard_map/ppermute | solution.py:544
  26.0 17.6 %collective-permute-start.12 = (bf16[32,5760]{1,0:T(8,128)(2,1)S(1)}, bf16[32,5760]{1,0:T(8,128)(2,1)S(1)}, u32[]{:S(2)}, u32[]{:S(2)}) collective-permute-start(bf16[32,5760]{1,0:T(8,128)(2,1)S(1)} %get-tuple-element.98), channel_id=1, source_target_pairs={{0,4},{4,8},{8,12},{12,14},{14,10},{10,6},{6,2},{2,0},{1,5},{5,9},... | collective-permute-start | bytes 1105928 | tf_op jit(solution)/shard_map/ppermute | solution.py:543
  37.8 12.6 %collective-permute-start.14 = (bf16[32,5760]{1,0:T(8,128)(2,1)S(1)}, bf16[32,5760]{1,0:T(8,128)(2,1)S(1)}, u32[]{:S(2)}, u32[]{:S(2)}) collective-permute-start(bf16[32,5760]{1,0:T(8,128)(2,1)S(1)} %get-tuple-element.94), channel_id=1, source_target_pairs={{0,4},{4,8},{8,12},{12,14},{14,10},{10,6},{6,2},{2,0},{1,5},{5,9},... | collective-permute-start | bytes 1105928 | tf_op jit(solution)/shard_map/ppermute | solution.py:543
  39.4 11.0 %collective-permute-start.15 = (bf16[32,5760]{1,0:T(8,128)(2,1)S(1)}, bf16[32,5760]{1,0:T(8,128)(2,1)S(1)}, u32[]{:S(2)}, u32[]{:S(2)}) collective-permute-start(bf16[32,5760]{1,0:T(8,128)(2,1)S(1)} %get-tuple-element.103), channel_id=1, source_target_pairs={{4,0},{8,4},{12,8},{14,12},{10,14},{6,10},{2,6},{0,2},{5,1},{9,5},... | collective-permute-start | bytes 1105928 | tf_op jit(solution)/shard_map/ppermute | solution.py:544
  44.1 8.9 %collective-permute-start.16 = (bf16[128,3712]{1,0:T(8,128)(2,1)S(1)}, bf16[128,3712]{1,0:T(8,128)(2,1)S(1)}, u32[]{:S(2)}, u32[]{:S(2)}) collective-permute-start(bf16[128,3712]{1,0:T(8,128)(2,1)S(1)} %get-tuple-element.105.refs_0_), channel_id=1, source_target_pairs={{0,1},{1,0},{2,3},{3,2},{4,5},{5,4},{6,7},{7,6},{8,9},{9,8},{10,11... | collective-permute-start | bytes 2850824 | tf_op jit(solution)/shard_map/ppermute | solution.py:545
  44.2 14.1 %collective-permute-start.17 = (bf16[32,5760]{1,0:T(8,128)(2,1)S(1)}, bf16[32,5760]{1,0:T(8,128)(2,1)S(1)}, u32[]{:S(2)}, u32[]{:S(2)}) collective-permute-start(bf16[32,5760]{1,0:T(8,128)(2,1)S(1)} %get-tuple-element.101), channel_id=1, source_target_pairs={{0,4},{4,8},{8,12},{12,14},{14,10},{10,6},{6,2},{2,0},{1,5},{5,9},... | collective-permute-start | bytes 1105928 | tf_op jit(solution)/shard_map/ppermute | solution.py:543
  45.9 12.5 %collective-permute-start.18 = (bf16[32,5760]{1,0:T(8,128)(2,1)S(1)}, bf16[32,5760]{1,0:T(8,128)(2,1)S(1)}, u32[]{:S(2)}, u32[]{:S(2)}) collective-permute-start(bf16[32,5760]{1,0:T(8,128)(2,1)S(1)} %get-tuple-element.108), channel_id=1, source_target_pairs={{4,0},{8,4},{12,8},{14,12},{10,14},{6,10},{2,6},{0,2},{5,1},{9,5},... | collective-permute-start | bytes 1105928 | tf_op jit(solution)/shard_map/ppermute | solution.py:544
  50.9 15.2 %collective-permute-start.19 = (bf16[32,5760]{1,0:T(8,128)(2,1)S(1)}, bf16[32,5760]{1,0:T(8,128)(2,1)S(1)}, u32[]{:S(2)}, u32[]{:S(2)}) collective-permute-start(bf16[32,5760]{1,0:T(8,128)(2,1)S(1)} %get-tuple-element.104), channel_id=1, source_target_pairs={{0,4},{4,8},{8,12},{12,14},{14,10},{10,6},{6,2},{2,0},{1,5},{5,9},... | collective-permute-start | bytes 1105928 | tf_op jit(solution)/shard_map/ppermute | solution.py:543
  52.9 8.0 %collective-permute-start.20 = (bf16[32,2048]{1,0:T(8,128)(2,1)S(1)}, bf16[32,2048]{1,0:T(8,128)(2,1)S(1)}, u32[]{:S(2)}, u32[]{:S(2)}) collective-permute-start(bf16[32,2048]{1,0:T(8,128)(2,1)S(1)} %get-tuple-element.112), channel_id=1, source_target_pairs={{4,0},{8,4},{12,8},{14,12},{10,14},{6,10},{2,6},{0,2},{5,1},{9,5},... | collective-permute-start | bytes 393224 | tf_op jit(solution)/shard_map/ppermute | solution.py:544
  58.8 7.8 %collective-permute-start.21 = (bf16[128,3712]{1,0:T(8,128)(2,1)S(1)}, bf16[128,3712]{1,0:T(8,128)(2,1)S(1)}, u32[]{:S(2)}, u32[]{:S(2)}) collective-permute-start(bf16[128,3712]{1,0:T(8,128)(2,1)S(1)} %get-tuple-element.113.refs_0_), channel_id=1, source_target_pairs={{0,1},{1,0},{2,3},{3,2},{4,5},{5,4},{6,7},{7,6},{8,9},{9,8},{10,11... | collective-permute-start | bytes 2850824 | tf_op jit(solution)/shard_map/ppermute | solution.py:545
  58.9 9.1 %collective-permute-start.23 = (bf16[32,2048]{1,0:T(8,128)(2,1)S(1)}, bf16[32,2048]{1,0:T(8,128)(2,1)S(1)}, u32[]{:S(2)}, u32[]{:S(2)}) collective-permute-start(bf16[32,2048]{1,0:T(8,128)(2,1)S(1)} %get-tuple-element.110), channel_id=1, source_target_pairs={{0,4},{4,8},{8,12},{12,14},{14,10},{10,6},{6,2},{2,0},{1,5},{5,9},... | collective-permute-start | bytes 393224 | tf_op jit(solution)/shard_map/ppermute | solution.py:543
  60.9 10.7 %collective-permute-start.22 = (bf16[32,5760]{1,0:T(8,128)(2,1)S(1)}, bf16[32,5760]{1,0:T(8,128)(2,1)S(1)}, u32[]{:S(2)}, u32[]{:S(2)}) collective-permute-start(bf16[32,5760]{1,0:T(8,128)(2,1)S(1)} %get-tuple-element.116), channel_id=1, source_target_pairs={{4,0},{8,4},{12,8},{14,12},{10,14},{6,10},{2,6},{0,2},{5,1},{9,5},... | collective-permute-start | bytes 1105928 | tf_op jit(solution)/shard_map/ppermute | solution.py:544
  67.9 6.0 %copy-start.1 = (bf16[64,3712]{1,0:T(8,128)(2,1)S(1)}, bf16[64,3712]{1,0:T(8,128)(2,1)}, u32[]{:S(2)}) copy-start(bf16[64,3712]{1,0:T(8,128)(2,1)} %get-tuple-element.83.tokens.refs_0_) | copy-start | bytes 1425412
  67.9 6.0 %copy-start.3 = (bf16[64,3712]{1,0:T(8,128)(2,1)S(1)}, bf16[64,3712]{1,0:T(8,128)(2,1)}, u32[]{:S(2)}) copy-start(bf16[64,3712]{1,0:T(8,128)(2,1)} %copy-done.2) | copy-start | bytes 1425412
  72.1 1.9 %collective-permute-start.24 = (bf16[64,3712]{1,0:T(8,128)(2,1)S(1)}, bf16[64,3712]{1,0:T(8,128)(2,1)S(1)}, u32[]{:S(2)}, u32[]{:S(2)}) collective-permute-start(bf16[64,3712]{1,0:T(8,128)(2,1)S(1)} %get-tuple-element.117.refs_1_), channel_id=1, source_target_pairs={{0,1},{1,0},{2,3},{3,2},{4,5},{5,4},{6,7},{7,6},{8,9},{9,8},{10,11... | collective-permute-start | bytes 1425416 | tf_op jit(solution)/shard_map/ppermute | solution.py:545
  96.1 3.4 %collective-permute-start.25 = (bf16[128,3584]{1,0:T(8,128)(2,1)S(1)}, bf16[128,3584]{1,0:T(8,128)(2,1)S(1)}, u32[]{:S(2)}, u32[]{:S(2)}) collective-permute-start(bf16[128,3584]{1,0:T(8,128)(2,1)S(1)} %get-tuple-element.130), channel_id=1, source_target_pairs={{0,1},{1,0},{2,3},{3,2},{4,5},{5,4},{6,7},{7,6},{8,9},{9,8},{10,11... | collective-permute-start | bytes 2752520 | tf_op jit(solution)/shard_map/ppermute | solution.py:545
  96.3 5.9 %collective-permute-start.28 = (bf16[32,1024]{1,0:T(8,128)(2,1)S(1)}, bf16[32,1024]{1,0:T(8,128)(2,1)S(1)}, u32[]{:S(2)}, u32[]{:S(2)}) collective-permute-start(bf16[32,1024]{1,0:T(8,128)(2,1)S(1)} %last_step.2.refs_0_), channel_id=1, source_target_pairs={{4,0},{8,4},{12,8},{14,12},{10,14},{6,10},{2,6},{0,2},{5,1},{9,5},... | collective-permute-start | bytes 196616 | tf_op jit(solution)/shard_map/ppermute | solution.py:544
  96.6 5.6 %collective-permute-start.27 = (bf16[32,1024]{1,0:T(8,128)(2,1)S(1)}, bf16[32,1024]{1,0:T(8,128)(2,1)S(1)}, u32[]{:S(2)}, u32[]{:S(2)}) collective-permute-start(bf16[32,1024]{1,0:T(8,128)(2,1)S(1)} %get-tuple-element.132.refs_1_), channel_id=1, source_target_pairs={{0,4},{4,8},{8,12},{12,14},{14,10},{10,6},{6,2},{2,0},{1,5},{5,9},... | collective-permute-start | bytes 196616 | tf_op jit(solution)/shard_map/ppermute | solution.py:543
  99.4 2.7 %collective-permute-start.26 = (bf16[128,3584]{1,0:T(8,128)(2,1)S(1)}, bf16[128,3584]{1,0:T(8,128)(2,1)S(1)}, u32[]{:S(2)}, u32[]{:S(2)}) collective-permute-start(bf16[128,3584]{1,0:T(8,128)(2,1)S(1)} %get-tuple-element.135), channel_id=1, source_target_pairs={{0,1},{1,0},{2,3},{3,2},{4,5},{5,4},{6,7},{7,6},{8,9},{9,8},{10,11... | collective-permute-start | bytes 2752520 | tf_op jit(solution)/shard_map/ppermute | solution.py:545
  100.1 9.9 %collective-permute-start.29 = (bf16[32,4608]{1,0:T(8,128)(2,1)S(1)}, bf16[32,4608]{1,0:T(8,128)(2,1)S(1)}, u32[]{:S(2)}, u32[]{:S(2)}) collective-permute-start(bf16[32,4608]{1,0:T(8,128)(2,1)S(1)} %get-tuple-element.133), channel_id=1, source_target_pairs={{0,4},{4,8},{8,12},{12,14},{14,10},{10,6},{6,2},{2,0},{1,5},{5,9},... | collective-permute-start | bytes 884744 | tf_op jit(solution)/shard_map/ppermute | solution.py:543
  101.7 9.8 %collective-permute-start.30 = (bf16[32,4608]{1,0:T(8,128)(2,1)S(1)}, bf16[32,4608]{1,0:T(8,128)(2,1)S(1)}, u32[]{:S(2)}, u32[]{:S(2)}) collective-permute-start(bf16[32,4608]{1,0:T(8,128)(2,1)S(1)} %get-tuple-element.142), channel_id=1, source_target_pairs={{4,0},{8,4},{12,8},{14,12},{10,14},{6,10},{2,6},{0,2},{5,1},{9,5},... | collective-permute-start | bytes 884744 | tf_op jit(solution)/shard_map/ppermute | solution.py:544
  102.7 13.6 %collective-permute-start.32 = (bf16[32,4608]{1,0:T(8,128)(2,1)S(1)}, bf16[32,4608]{1,0:T(8,128)(2,1)S(1)}, u32[]{:S(2)}, u32[]{:S(2)}) collective-permute-start(bf16[32,4608]{1,0:T(8,128)(2,1)S(1)} %get-tuple-element.136), channel_id=1, source_target_pairs={{0,4},{4,8},{8,12},{12,14},{14,10},{10,6},{6,2},{2,0},{1,5},{5,9},... | collective-permute-start | bytes 884744 | tf_op jit(solution)/shard_map/ppermute | solution.py:543
  106.6 11.2 %collective-permute-start.31 = (bf16[256,3584]{1,0:T(8,128)(2,1)S(1)}, bf16[256,3584]{1,0:T(8,128)(2,1)S(1)}, u32[]{:S(2)}, u32[]{:S(2)}) collective-permute-start(bf16[256,3584]{1,0:T(8,128)(2,1)S(1)} %get-tuple-element.145), channel_id=1, source_target_pairs={{0,1},{1,0},{2,3},{3,2},{4,5},{5,4},{6,7},{7,6},{8,9},{9,8},{10,11... | collective-permute-start | bytes 5505032 | tf_op jit(solution)/shard_map/ppermute | solution.py:545
  106.7 11.1 %collective-permute-start.33 = (bf16[32,4608]{1,0:T(8,128)(2,1)S(1)}, bf16[32,4608]{1,0:T(8,128)(2,1)S(1)}, u32[]{:S(2)}, u32[]{:S(2)}) collective-permute-start(bf16[32,4608]{1,0:T(8,128)(2,1)S(1)} %get-tuple-element.146), channel_id=1, source_target_pairs={{4,0},{8,4},{12,8},{14,12},{10,14},{6,10},{2,6},{0,2},{5,1},{9,5},... | collective-permute-start | bytes 884744 | tf_op jit(solution)/shard_map/ppermute | solution.py:544
  112.1 10.5 %collective-permute-start.34 = (bf16[32,4608]{1,0:T(8,128)(2,1)S(1)}, bf16[32,4608]{1,0:T(8,128)(2,1)S(1)}, u32[]{:S(2)}, u32[]{:S(2)}) collective-permute-start(bf16[32,4608]{1,0:T(8,128)(2,1)S(1)} %get-tuple-element.143), channel_id=1, source_target_pairs={{0,4},{4,8},{8,12},{12,14},{14,10},{10,6},{6,2},{2,0},{1,5},{5,9},... | collective-permute-start | bytes 884744 | tf_op jit(solution)/shard_map/ppermute | solution.py:543
  114.1 10.1 %collective-permute-start.35 = (bf16[32,4608]{1,0:T(8,128)(2,1)S(1)}, bf16[32,4608]{1,0:T(8,128)(2,1)S(1)}, u32[]{:S(2)}, u32[]{:S(2)}) collective-permute-start(bf16[32,4608]{1,0:T(8,128)(2,1)S(1)} %get-tuple-element.149), channel_id=1, source_target_pairs={{4,0},{8,4},{12,8},{14,12},{10,14},{6,10},{2,6},{0,2},{5,1},{9,5},... | collective-permute-start | bytes 884744 | tf_op jit(solution)/shard_map/ppermute | solution.py:544
  118.4 10.5 %collective-permute-start.36 = (bf16[32,4608]{1,0:T(8,128)(2,1)S(1)}, bf16[32,4608]{1,0:T(8,128)(2,1)S(1)}, u32[]{:S(2)}, u32[]{:S(2)}) collective-permute-start(bf16[32,4608]{1,0:T(8,128)(2,1)S(1)} %get-tuple-element.147), channel_id=1, source_target_pairs={{0,4},{4,8},{8,12},{12,14},{14,10},{10,6},{6,2},{2,0},{1,5},{5,9},... | collective-permute-start | bytes 884744 | tf_op jit(solution)/shard_map/ppermute | solution.py:543
  120.4 10.0 %collective-permute-start.37 = (bf16[32,4608]{1,0:T(8,128)(2,1)S(1)}, bf16[32,4608]{1,0:T(8,128)(2,1)S(1)}, u32[]{:S(2)}, u32[]{:S(2)}) collective-permute-start(bf16[32,4608]{1,0:T(8,128)(2,1)S(1)} %get-tuple-element.153), channel_id=1, source_target_pairs={{4,0},{8,4},{12,8},{14,12},{10,14},{6,10},{2,6},{0,2},{5,1},{9,5},... | collective-permute-start | bytes 884744 | tf_op jit(solution)/shard_map/ppermute | solution.py:544
  124.7 10.5 %collective-permute-start.38 = (bf16[32,4608]{1,0:T(8,128)(2,1)S(1)}, bf16[32,4608]{1,0:T(8,128)(2,1)S(1)}, u32[]{:S(2)}, u32[]{:S(2)}) collective-permute-start(bf16[32,4608]{1,0:T(8,128)(2,1)S(1)} %get-tuple-element.150), channel_id=1, source_target_pairs={{0,4},{4,8},{8,12},{12,14},{14,10},{10,6},{6,2},{2,0},{1,5},{5,9},... | collective-permute-start | bytes 884744 | tf_op jit(solution)/shard_map/ppermute | solution.py:543
  126.7 10.1 %collective-permute-start.39 = (bf16[32,4608]{1,0:T(8,128)(2,1)S(1)}, bf16[32,4608]{1,0:T(8,128)(2,1)S(1)}, u32[]{:S(2)}, u32[]{:S(2)}) collective-permute-start(bf16[32,4608]{1,0:T(8,128)(2,1)S(1)} %get-tuple-element.156), channel_id=1, source_target_pairs={{4,0},{8,4},{12,8},{14,12},{10,14},{6,10},{2,6},{0,2},{5,1},{9,5},... | collective-permute-start | bytes 884744 | tf_op jit(solution)/shard_map/ppermute | solution.py:544
  131.0 12.1 %collective-permute-start.41 = (bf16[32,4608]{1,0:T(8,128)(2,1)S(1)}, bf16[32,4608]{1,0:T(8,128)(2,1)S(1)}, u32[]{:S(2)}, u32[]{:S(2)}) collective-permute-start(bf16[32,4608]{1,0:T(8,128)(2,1)S(1)} %get-tuple-element.154), channel_id=1, source_target_pairs={{0,4},{4,8},{8,12},{12,14},{14,10},{10,6},{6,2},{2,0},{1,5},{5,9},... | collective-permute-start | bytes 884744 | tf_op jit(solution)/shard_map/ppermute | solution.py:543
  133.1 10.1 %collective-permute-start.40 = (bf16[32,4608]{1,0:T(8,128)(2,1)S(1)}, bf16[32,4608]{1,0:T(8,128)(2,1)S(1)}, u32[]{:S(2)}, u32[]{:S(2)}) collective-permute-start(bf16[32,4608]{1,0:T(8,128)(2,1)S(1)} %get-tuple-element.159), channel_id=1, source_target_pairs={{4,0},{8,4},{12,8},{14,12},{10,14},{6,10},{2,6},{0,2},{5,1},{9,5},... | collective-permute-start | bytes 884744 | tf_op jit(solution)/shard_map/ppermute | solution.py:544
  137.3 8.7 %collective-permute-start.42 = (bf16[32,3584]{1,0:T(8,128)(2,1)S(1)}, bf16[32,3584]{1,0:T(8,128)(2,1)S(1)}, u32[]{:S(2)}, u32[]{:S(2)}) collective-permute-start(bf16[32,3584]{1,0:T(8,128)(2,1)S(1)} %get-tuple-element.157), channel_id=1, source_target_pairs={{0,4},{4,8},{8,12},{12,14},{14,10},{10,6},{6,2},{2,0},{1,5},{5,9},... | collective-permute-start | bytes 688136 | tf_op jit(solution)/shard_map/ppermute | solution.py:543
  139.4 8.2 %collective-permute-start.43 = (bf16[32,3584]{1,0:T(8,128)(2,1)S(1)}, bf16[32,3584]{1,0:T(8,128)(2,1)S(1)}, u32[]{:S(2)}, u32[]{:S(2)}) collective-permute-start(bf16[32,3584]{1,0:T(8,128)(2,1)S(1)} %get-tuple-element.160), channel_id=1, source_target_pairs={{4,0},{8,4},{12,8},{14,12},{10,14},{6,10},{2,6},{0,2},{5,1},{9,5},... | collective-permute-start | bytes 688136 | tf_op jit(solution)/shard_map/ppermute | solution.py:544
  (7 other events, 15.3 us)
